TPU v7x, 32 devices: a whole 2x2x4 slice. The times are simulated.
32 devices in a mesh: stream: 8 (over y, x, core), span: 4 (over z).
Axes of the slice: x: 2, y: 2, z: 4, core: 2. Of those that a mesh axis runs over, the one named last changes fastest.
Arguments:
- grains: float32 [13, 786432], P(None, ('stream', 'span'))
- send_slots: int32 [32, 2, 2048], P(('stream', 'span')), may hold values from 0 to 24575, as said below
- send_counts: int32 [32, 2], P(('stream', 'span')), may hold values from 0 to 2048, as said below
- cell_index: int32 [917504], P(('stream', 'span')), may hold values from 0 to 65535
- fluid: float32 [3, 256, 32, 256], P(None, 'stream', 'span'), may hold values from -6 to 6
- block_slots: int32 [32, 32, 8], P(('stream', 'span')), may hold values from 0 to 255
- block_counts: int32 [32, 32], P(('stream', 'span')), may hold values from 0 to 8, as said below
Outputs:
- grains_after: float32 [13, 917504], P(None, ('stream', 'span'))
- solid_fields: float32 [4, 256, 32, 256], P(None, 'stream', 'span')
- received: float32 [32, 32, 8, 4, 256], P(('stream', 'span'))
Inputs may be any that keep to these rules, and one draw needn't show every extreme that they name: `send_slots`: the entries of one device's two lists are distinct slots of that device. `send_counts`: live entries are the first ones of a list; a list of 2048 live entries exists in both directions. `block_counts`: every device sends 8 columns to some device and receives 8 from some device.
All inputs are finite; a program needn't handle non-finite values.
Results may differ from a plain program's by a relative error of at most 0.00086.
Values sent between devices are 32-bit elements; how exact they have to be, the bound alone decides.
No kernel may reach another device: no remote copies, remote signals or barrier semaphores. Data moves between devices by JAX's collectives and lax.ppermute only.
A program may use at most 64 MiB of HBM per device.

v0:
```python
import math

import jax
import jax.numpy as jnp
from jax import lax
from jax.sharding import PartitionSpec as P

REACH = 3


spread_cells = 1.5
drag_rate = 0.25


def from_behind(value, axis, steps):
    count = lax.axis_size(axis)
    pairs = [(source, (source + steps) % count) for source in range(count)]
    return lax.ppermute(value, axis, pairs)


def padded(block, sides, width, periodic):
    for axis, dim in sides:
        count = lax.axis_size(axis)
        forward = [(i, i + 1) for i in range(count - 1)]
        if periodic:
            forward.append((count - 1, 0))
        backward = [(target, source) for source, target in forward]
        low = lax.ppermute(
            lax.slice_in_dim(block, block.shape[dim] - width, None, axis=dim), axis, forward
        )
        high = lax.ppermute(lax.slice_in_dim(block, 0, width, axis=dim), axis, backward)
        block = jnp.concatenate([low, block, high], axis=dim)
    return block


def kernel_taps():
    raw = [
        math.exp(-(k * k) / (2.0 * spread_cells * spread_cells)) for k in range(-REACH, REACH + 1)
    ]
    total = sum(raw)
    return [value / total for value in raw]


def taps_along(values, axis, length):
    weights = kernel_taps()
    result = weights[0] * lax.slice_in_dim(values, 0, length, axis=axis)
    for offset in range(1, 2 * REACH + 1):
        result = result + weights[offset] * lax.slice_in_dim(
            values, offset, offset + length, axis=axis
        )
    return result


def depth_pass(values):
    depth = values.shape[3]
    weights = kernel_taps()
    upper = lax.broadcasted_iota(jnp.int32, (depth, depth), 0)
    lower = lax.broadcasted_iota(jnp.int32, (depth, depth), 1)
    distance = upper - lower
    band_matrix = jnp.zeros((depth, depth), jnp.float32)
    for offset in range(2 * REACH + 1):
        band_matrix = band_matrix + weights[offset] * (distance == offset - REACH).astype(
            jnp.float32
        )
    return jnp.einsum("abcz,zw->abcw", values, band_matrix, precision=lax.Precision.HIGHEST)


def per_device(grains, send_slots, send_counts, cell_index, fluid, block_slots, block_counts):
    width_m = send_slots.shape[2]
    slot_count = grains.shape[1]
    slots = send_slots.reshape(2, width_m)
    live = (lax.broadcasted_iota(jnp.int32, (2, width_m), 1) < send_counts[0][:, None]).astype(
        jnp.float32
    )
    leaving = grains[:, slots] * live[None]
    from_below = from_behind(leaving[:, 0], "stream", 1)
    from_above = from_behind(leaving[:, 1], "stream", -1)
    removed = jnp.zeros((slot_count,), jnp.float32).at[slots.reshape(-1)].max(live.reshape(-1))
    kept = grains * (1.0 - removed)[None]
    grains_after = jnp.concatenate([kept, from_below, from_above], axis=1)
    depth_cells = fluid.shape[3]
    rows_x = fluid.shape[1]
    rows_y = fluid.shape[2]
    plane = rows_y * depth_cells
    volume = 4.18879 * grains_after[9] ** 3
    quant = jnp.stack(
        [volume, volume * grains_after[3], volume * grains_after[4], volume * grains_after[5]]
    ).astype(jnp.bfloat16)
    total_grains = grains_after.shape[1]
    step_size = math.gcd(total_grains, 2048)
    steps_count = total_grains // step_size
    quant_steps = jnp.moveaxis(quant.reshape(4, steps_count, step_size), 1, 0)
    row_steps = (cell_index // plane).reshape(steps_count, step_size)
    rest_steps = (cell_index % plane).reshape(steps_count, step_size)

    def add_step(total, pieces):
        values, row_of, rest_of = pieces
        pick_row = (
            row_of[None, :] == lax.broadcasted_iota(jnp.int32, (rows_x, step_size), 0)
        ).astype(jnp.bfloat16)
        left_side = (values[:, None, :] * pick_row[None]).reshape(4 * rows_x, step_size)
        pick_rest = (
            rest_of[:, None] == lax.broadcasted_iota(jnp.int32, (step_size, plane), 1)
        ).astype(jnp.bfloat16)
        return (total + jnp.dot(left_side, pick_rest, preferred_element_type=jnp.float32), None)

    field, _ = lax.scan(
        add_step, jnp.zeros((4 * rows_x, plane), jnp.float32), (quant_steps, row_steps, rest_steps)
    )
    field = field.reshape(4, rows_x, rows_y, depth_cells)
    extended = padded(field, (("stream", 1),), REACH, True)
    extended = padded(extended, (("span", 2),), REACH, False)
    read = taps_along(extended, 1, rows_x)
    solid_fields = taps_along(read, 2, rows_y)
    solid_fields = depth_pass(solid_fields)
    solid = solid_fields[0]
    moved = fluid + drag_rate * (solid_fields[1:4] - solid[None] * fluid)
    void = 1.0 / (1.0 + solid)
    coupled = jnp.concatenate([moved, void[None]], axis=0)
    columns = coupled.reshape(4, rows_x * rows_y, depth_cells).transpose(1, 0, 2)
    peers = block_slots.shape[1]
    width_q = block_slots.shape[2]
    block_live = (
        lax.broadcasted_iota(jnp.int32, (peers, width_q), 1) < block_counts[0][:, None]
    ).astype(jnp.float32)
    outgoing = columns[block_slots[0]] * block_live[:, :, None, None]
    arrived = lax.all_to_all(outgoing, ("stream", "span"), split_axis=0, concat_axis=0, tiled=True)
    return (grains_after, solid_fields, arrived[None])


def solution(mesh):
    return jax.shard_map(
        per_device,
        mesh=mesh,
        in_specs=(
            P(None, ("stream", "span")),
            P(("stream", "span"), None, None),
            P(("stream", "span"), None),
            P(("stream", "span")),
            P(None, "stream", "span", None),
            P(("stream", "span"), None, None),
            P(("stream", "span"), None),
        ),
        out_specs=(
            P(None, ("stream", "span")),
            P(None, "stream", "span", None),
            P(("stream", "span"), None, None, None, None),
        ),
        check_vma=False,
    )
```

profile of v0, /device:TPU:1, one launch (start us, length us, event | category | flops | bytes accessed | tf_op | source)
XLA Modules:
  0.0 174.8 jit_solution(5250602848902096462)
XLA Ops:
  0.6 7.6 %copy.36 = f32[13,24576]{0,1:T(8,128)} copy(f32[13,24576]{1,0:T(8,128)} %param.9) | data formatting | bytes 2555904 | tf_op args[0]
  8.3 18.8 %gather_fusion = f32[4096,13]{1,0:T(8,128)} fusion(f32[13,24576]{0,1:T(8,128)} %copy.36, s32[4096]{0:T(1024)S(1)} %broadcast_clamp_fusion), kind=kCustom, calls=%fused_computation | custom fusion | bytes 442368 | tf_op jit(solution)/shard_map/gather | solution.py:75
  27.1 2.3 %copy.37 = f32[2,2048,13]{1,2,0:T(8,128)S(1)} copy(f32[2,2048,13]{2,1,0:T(8,128)} %bitcast.73) | data formatting | bytes 425984 | tf_op jit(solution)/shard_map/gather | solution.py:75
  30.3 2.5 %collective-permute-start = (f32[13,2048]{1,0:T(8,128)}, f32[13,2048]{1,0:T(8,128)}, u32[]{:S(2)}, u32[]{:S(2)}) collective-permute-start(f32[13,2048]{1,0:T(8,128)} %get-tuple-element.72), channel_id=1, source_target_pairs={{0,4},{4,8},{8,12},{12,16},{16,20},{20,24},{24,28},{28,0},{1,5},{5... | collective-permute-start | bytes 319496 | tf_op jit(solution)/shard_map/ppermute | solution.py:18
  33.0 21.9 %scatter_custom_fusion = f32[24576]{0:T(1024)S(1)} fusion(s32[4096]{0:T(1024)S(1)} %bitcast.84, f32[4096]{0:T(1024)S(1)} %bitcast.85, f32[]{:T(128)} %constant.30.clone.1), kind=kCustom, calls=%fused_computation.111 | custom fusion | flops 4096 | bytes 98308 | tf_op jit(solution)/shard_map/scatter-max | solution.py:78
  58.5 54.8 %while.11 = (s32[]{:T(128)}, f32[128,2048]{1,0:T(8,128)S(1)}, bf16[14,4,2048]{2,1,0:T(4,128)(2,1)S(1)}, s32[14,2048]{1,0:T(8,128)S(1)}, s32[14,2048]{1,0:T(8,128)S(1)}, /*index=5*/s32[]{:T(128)}, s32[]{:T(128)}) while((s32[]{:T(128)}, f32[128,2048]{1,0:T(8,128)S(1)}, bf16[14,4,2048]{2,1,0:T(4,128)(2,1)S(1)}, ...), condition=%wide.region_2.3_spmd.clone, body=%wide.region_1.2_spmd.clone.sunk | while | flops 1078853632 | bytes 3506279 | solution.py:107
  58.6 3.8 %fusion.103 = f32[128,2048]{1,0:T(8,128)S(1)} fusion(bf16[128,2048]{1,0:T(8,128)(2,1)S(1)} %bitcast.68, s32[2048]{0:T(1024)S(1)} %bitcast.80, f32[128,2048]{1,0:T(8,128)S(1)} %get-tuple-element.121, pred[]{:T(512)S(6)} %compare.6), kind=kOutput, calls=%fused_computation.6.clone.1 | convolution fusion | flops 1078460416 | bytes 2629633 | tf_op jit(solution)/shard_map/while/body/eval_jaxpr/dot_general | solution.py:105
  62.5 3.8 %fusion.103 = f32[128,2048]{1,0:T(8,128)S(1)} fusion(bf16[128,2048]{1,0:T(8,128)(2,1)S(1)} %bitcast.68, s32[2048]{0:T(1024)S(1)} %bitcast.80, f32[128,2048]{1,0:T(8,128)S(1)} %get-tuple-element.121, pred[]{:T(512)S(6)} %compare.6), kind=kOutput, calls=%fused_computation.6.clone.1 | convolution fusion | flops 1078460416 | bytes 2629633 | tf_op jit(solution)/shard_map/while/body/eval_jaxpr/dot_general | solution.py:105
  66.4 3.8 %fusion.103 = f32[128,2048]{1,0:T(8,128)S(1)} fusion(bf16[128,2048]{1,0:T(8,128)(2,1)S(1)} %bitcast.68, s32[2048]{0:T(1024)S(1)} %bitcast.80, f32[128,2048]{1,0:T(8,128)S(1)} %get-tuple-element.121, pred[]{:T(512)S(6)} %compare.6), kind=kOutput, calls=%fused_computation.6.clone.1 | convolution fusion | flops 1078460416 | bytes 2629633 | tf_op jit(solution)/shard_map/while/body/eval_jaxpr/dot_general | solution.py:105
  70.4 3.8 %fusion.103 = f32[128,2048]{1,0:T(8,128)S(1)} fusion(bf16[128,2048]{1,0:T(8,128)(2,1)S(1)} %bitcast.68, s32[2048]{0:T(1024)S(1)} %bitcast.80, f32[128,2048]{1,0:T(8,128)S(1)} %get-tuple-element.121, pred[]{:T(512)S(6)} %compare.6), kind=kOutput, calls=%fused_computation.6.clone.1 | convolution fusion | flops 1078460416 | bytes 2629633 | tf_op jit(solution)/shard_map/while/body/eval_jaxpr/dot_general | solution.py:105
  74.3 3.8 %fusion.103 = f32[128,2048]{1,0:T(8,128)S(1)} fusion(bf16[128,2048]{1,0:T(8,128)(2,1)S(1)} %bitcast.68, s32[2048]{0:T(1024)S(1)} %bitcast.80, f32[128,2048]{1,0:T(8,128)S(1)} %get-tuple-element.121, pred[]{:T(512)S(6)} %compare.6), kind=kOutput, calls=%fused_computation.6.clone.1 | convolution fusion | flops 1078460416 | bytes 2629633 | tf_op jit(solution)/shard_map/while/body/eval_jaxpr/dot_general | solution.py:105
  78.2 3.8 %fusion.103 = f32[128,2048]{1,0:T(8,128)S(1)} fusion(bf16[128,2048]{1,0:T(8,128)(2,1)S(1)} %bitcast.68, s32[2048]{0:T(1024)S(1)} %bitcast.80, f32[128,2048]{1,0:T(8,128)S(1)} %get-tuple-element.121, pred[]{:T(512)S(6)} %compare.6), kind=kOutput, calls=%fused_computation.6.clone.1 | convolution fusion | flops 1078460416 | bytes 2629633 | tf_op jit(solution)/shard_map/while/body/eval_jaxpr/dot_general | solution.py:105
  82.1 3.8 %fusion.103 = f32[128,2048]{1,0:T(8,128)S(1)} fusion(bf16[128,2048]{1,0:T(8,128)(2,1)S(1)} %bitcast.68, s32[2048]{0:T(1024)S(1)} %bitcast.80, f32[128,2048]{1,0:T(8,128)S(1)} %get-tuple-element.121, pred[]{:T(512)S(6)} %compare.6), kind=kOutput, calls=%fused_computation.6.clone.1 | convolution fusion | flops 1078460416 | bytes 2629633 | tf_op jit(solution)/shard_map/while/body/eval_jaxpr/dot_general | solution.py:105
  86.0 3.8 %fusion.103 = f32[128,2048]{1,0:T(8,128)S(1)} fusion(bf16[128,2048]{1,0:T(8,128)(2,1)S(1)} %bitcast.68, s32[2048]{0:T(1024)S(1)} %bitcast.80, f32[128,2048]{1,0:T(8,128)S(1)} %get-tuple-element.121, pred[]{:T(512)S(6)} %compare.6), kind=kOutput, calls=%fused_computation.6.clone.1 | convolution fusion | flops 1078460416 | bytes 2629633 | tf_op jit(solution)/shard_map/while/body/eval_jaxpr/dot_general | solution.py:105
  89.9 3.8 %fusion.103 = f32[128,2048]{1,0:T(8,128)S(1)} fusion(bf16[128,2048]{1,0:T(8,128)(2,1)S(1)} %bitcast.68, s32[2048]{0:T(1024)S(1)} %bitcast.80, f32[128,2048]{1,0:T(8,128)S(1)} %get-tuple-element.121, pred[]{:T(512)S(6)} %compare.6), kind=kOutput, calls=%fused_computation.6.clone.1 | convolution fusion | flops 1078460416 | bytes 2629633 | tf_op jit(solution)/shard_map/while/body/eval_jaxpr/dot_general | solution.py:105
  93.8 3.8 %fusion.103 = f32[128,2048]{1,0:T(8,128)S(1)} fusion(bf16[128,2048]{1,0:T(8,128)(2,1)S(1)} %bitcast.68, s32[2048]{0:T(1024)S(1)} %bitcast.80, f32[128,2048]{1,0:T(8,128)S(1)} %get-tuple-element.121, pred[]{:T(512)S(6)} %compare.6), kind=kOutput, calls=%fused_computation.6.clone.1 | convolution fusion | flops 1078460416 | bytes 2629633 | tf_op jit(solution)/shard_map/while/body/eval_jaxpr/dot_general | solution.py:105
  97.8 3.8 %fusion.103 = f32[128,2048]{1,0:T(8,128)S(1)} fusion(bf16[128,2048]{1,0:T(8,128)(2,1)S(1)} %bitcast.68, s32[2048]{0:T(1024)S(1)} %bitcast.80, f32[128,2048]{1,0:T(8,128)S(1)} %get-tuple-element.121, pred[]{:T(512)S(6)} %compare.6), kind=kOutput, calls=%fused_computation.6.clone.1 | convolution fusion | flops 1078460416 | bytes 2629633 | tf_op jit(solution)/shard_map/while/body/eval_jaxpr/dot_general | solution.py:105
  101.7 3.8 %fusion.103 = f32[128,2048]{1,0:T(8,128)S(1)} fusion(bf16[128,2048]{1,0:T(8,128)(2,1)S(1)} %bitcast.68, s32[2048]{0:T(1024)S(1)} %bitcast.80, f32[128,2048]{1,0:T(8,128)S(1)} %get-tuple-element.121, pred[]{:T(512)S(6)} %compare.6), kind=kOutput, calls=%fused_computation.6.clone.1 | convolution fusion | flops 1078460416 | bytes 2629633 | tf_op jit(solution)/shard_map/while/body/eval_jaxpr/dot_general | solution.py:105
  105.6 3.8 %fusion.103 = f32[128,2048]{1,0:T(8,128)S(1)} fusion(bf16[128,2048]{1,0:T(8,128)(2,1)S(1)} %bitcast.68, s32[2048]{0:T(1024)S(1)} %bitcast.80, f32[128,2048]{1,0:T(8,128)S(1)} %get-tuple-element.121, pred[]{:T(512)S(6)} %compare.6), kind=kOutput, calls=%fused_computation.6.clone.1 | convolution fusion | flops 1078460416 | bytes 2629633 | tf_op jit(solution)/shard_map/while/body/eval_jaxpr/dot_general | solution.py:105
  109.5 3.8 %fusion.103 = f32[128,2048]{1,0:T(8,128)S(1)} fusion(bf16[128,2048]{1,0:T(8,128)(2,1)S(1)} %bitcast.68, s32[2048]{0:T(1024)S(1)} %bitcast.80, f32[128,2048]{1,0:T(8,128)S(1)} %get-tuple-element.121, pred[]{:T(512)S(6)} %compare.6), kind=kOutput, calls=%fused_computation.6.clone.1 | convolution fusion | flops 1078460416 | bytes 2629633 | tf_op jit(solution)/shard_map/while/body/eval_jaxpr/dot_general | solution.py:105
  116.0 3.2 %collective-permute-done.3 = f32[4,3,8,256]{3,2,1,0:T(8,128)S(1)} collective-permute-done((f32[4,3,8,256]{3,2,1,0:T(8,128)S(1)}, f32[4,3,8,256]{3,2,1,0:T(8,128)S(1)}, u32[]{:S(2)}, u32[]{:S(2)}) %collective-permute-start.3) | collective-permute-done | bytes 98336 | tf_op jit(solution)/shard_map/ppermute | solution.py:31
  121.1 4.2 %collective-permute-start.4 = (f32[4,38,3,256]{3,0,2,1:T(4,128)S(1)}, f32[4,38,3,256]{3,0,2,1:T(4,128)S(1)}, u32[]{:S(2)}, u32[]{:S(2)}) collective-permute-start(f32[4,38,3,256]{3,0,2,1:T(4,128)S(1)} %copy.42), channel_id=1, source_target_pairs={{0,1},{1,2},{2,3},{4,5},{5,6},{6,7},{8,9},{9,10},{10,11},{12,13},{... | collective-permute-start | bytes 1400840 | tf_op jit(solution)/shard_map/ppermute | solution.py:28
  125.5 7.3 %collective-permute-done.5 = f32[4,38,3,256]{3,0,2,1:T(4,128)S(1)} collective-permute-done((f32[4,38,3,256]{3,0,2,1:T(4,128)S(1)}, f32[4,38,3,256]{3,0,2,1:T(4,128)S(1)}, u32[]{:S(2)}, u32[]{:S(2)}) %collective-permute-start.5) | collective-permute-done | bytes 466976 | tf_op jit(solution)/shard_map/ppermute | solution.py:31
  140.3 33.5 %all_to_all.5 = f32[32,8,4,256]{3,2,1,0:T(4,128)S(1)} all-to-all(f32[32,8,4,256]{3,2,1,0:T(4,128)S(1)} %broadcast_multiply_fusion.2), channel_id=1, replica_groups=mesh['stream'=8,'span'=4] {'stream','span'}, dimensions={0} | all-to-all | bytes 2097152 | tf_op jit(solution)/shard_map/all_to_all | solution.py:127
  (127 shorter events, 19.0 us)
Async XLA Ops:
  0.6 7.6 %copy-start.5 = (s32[1,2,2048]{2,1,0:T(2,128)S(1)}, s32[1,2,2048]{2,1,0:T(2,128)}, u32[]{:S(2)}) copy-start(s32[1,2,2048]{2,1,0:T(2,128)} %param.10) | copy-start | bytes 49156
  8.3 21.1 %copy-start.7 = (s32[1,2]{1,0:T(1,128)S(1)}, s32[1,2]{1,0:T(1,128)}, u32[]{:S(2)}) copy-start(s32[1,2]{1,0:T(1,128)} %param.11) | copy-start | bytes 28
  27.1 27.8 %copy-start = (f32[13,24576]{1,0:T(8,128)S(1)}, f32[13,24576]{1,0:T(8,128)}, u32[]{:S(2)}) copy-start(f32[13,24576]{1,0:T(8,128)} %param.9) | copy-start | bytes 3833860
  29.6 25.5 %copy-start.4 = (s32[28672]{0:T(1024)S(1)}, s32[28672]{0:T(1024)}, u32[]{:S(2)}) copy-start(s32[28672]{0:T(1024)} %param.12) | copy-start | bytes 344068
  30.3 25.0 %collective-permute-start.1 = (f32[13,2048]{1,0:T(8,128)}, f32[13,2048]{1,0:T(8,128)S(1)}, u32[]{:S(2)}, u32[]{:S(2)}) collective-permute-start(f32[13,2048]{1,0:T(8,128)} %get-tuple-element.73), channel_id=1, source_target_pairs={{0,28},{4,0},{8,4},{12,8},{16,12},{20,16},{24,20},{28,24},{1,29},{... | collective-permute-start | bytes 319496 | tf_op jit(solution)/shard_map/ppermute | solution.py:18
  30.3 24.9 %collective-permute-start = (f32[13,2048]{1,0:T(8,128)}, f32[13,2048]{1,0:T(8,128)}, u32[]{:S(2)}, u32[]{:S(2)}) collective-permute-start(f32[13,2048]{1,0:T(8,128)} %get-tuple-element.72), channel_id=1, source_target_pairs={{0,4},{4,8},{8,12},{12,16},{16,20},{20,24},{24,28},{28,0},{1,5},{5... | collective-permute-start | bytes 319496 | tf_op jit(solution)/shard_map/ppermute | solution.py:18
  56.3 1.2 copy-start.1
  113.7 2.2 %collective-permute-start.2 = (f32[4,3,8,256]{3,2,1,0:T(8,128)S(1)}, f32[4,3,8,256]{3,2,1,0:T(8,128)S(1)}, u32[]{:S(2)}, u32[]{:S(2)}) collective-permute-start(f32[4,3,8,256]{3,2,1,0:T(8,128)S(1)} %get-tuple-element.71), channel_id=1, source_target_pairs={{0,4},{4,8},{8,12},{12,16},{16,20},{20,24},{24,28},{28,0},{1,5},{5... | collective-permute-start | bytes 294920 | tf_op jit(solution)/shard_map/ppermute | solution.py:28
  114.2 4.9 %collective-permute-start.3 = (f32[4,3,8,256]{3,2,1,0:T(8,128)S(1)}, f32[4,3,8,256]{3,2,1,0:T(8,128)S(1)}, u32[]{:S(2)}, u32[]{:S(2)}) collective-permute-start(f32[4,3,8,256]{3,2,1,0:T(8,128)S(1)} %get-tuple-element.70), channel_id=1, source_target_pairs={{4,0},{8,4},{12,8},{16,12},{20,16},{24,20},{28,24},{0,28},{5,1},{9... | collective-permute-start | bytes 294920 | tf_op jit(solution)/shard_map/ppermute | solution.py:31
  119.1 6.1 %copy-start.6 = (s32[1,32,8]{1,2,0:T(8,128)S(1)}, s32[1,32,8]{1,2,0:T(8,128)}, u32[]{:S(2)}) copy-start(s32[1,32,8]{1,2,0:T(8,128)} %param.14) | copy-start | bytes 3076
  119.2 6.3 %copy-start.8 = (s32[1,32]{1,0:T(1,128)S(1)}, s32[1,32]{1,0:T(1,128)}, u32[]{:S(2)}) copy-start(s32[1,32]{1,0:T(1,128)} %param.15) | copy-start | bytes 388
  119.6 13.3 %collective-permute-start.5 = (f32[4,38,3,256]{3,0,2,1:T(4,128)S(1)}, f32[4,38,3,256]{3,0,2,1:T(4,128)S(1)}, u32[]{:S(2)}, u32[]{:S(2)}) collective-permute-start(f32[4,38,3,256]{3,0,2,1:T(4,128)S(1)} %copy.43), channel_id=1, source_target_pairs={{1,0},{2,1},{3,2},{5,4},{6,5},{7,6},{9,8},{10,9},{11,10},{13,12},{... | collective-permute-start | bytes 1400840 | tf_op jit(solution)/shard_map/ppermute | solution.py:31
  121.1 12.9 %collective-permute-start.4 = (f32[4,38,3,256]{3,0,2,1:T(4,128)S(1)}, f32[4,38,3,256]{3,0,2,1:T(4,128)S(1)}, u32[]{:S(2)}, u32[]{:S(2)}) collective-permute-start(f32[4,38,3,256]{3,0,2,1:T(4,128)S(1)} %copy.42), channel_id=1, source_target_pairs={{0,1},{1,2},{2,3},{4,5},{5,6},{6,7},{8,9},{9,10},{10,11},{12,13},{... | collective-permute-start | bytes 1400840 | tf_op jit(solution)/shard_map/ppermute | solution.py:28
  135.3 2.2 %copy-start.3 = (f32[3,32,8,256]{3,2,1,0:T(8,128)S(1)}, f32[3,32,8,256]{3,2,1,0:T(8,128)}, u32[]{:S(2)}) copy-start(f32[3,32,8,256]{3,2,1,0:T(8,128)} %param.13) | copy-start | bytes 2359300
  137.1 1.0 copy-start.2
where the time goes:
time: 175 us
  matrix products  54.4 us (31%)
  local copies, waits for them, and re-layouts  35.6 us (20%)
  blocking collectives  33.5 us (19%)
  other arithmetic  27.7 us (16%)
  waiting for transfers between devices  12.7 us (7%)
  starting transfers between devices  8.99 us (5%)
    dot_general x14, matrix products, add_step(): jnp.dot(left_side, pick_rest, preferred_element_type=jnp.float32)  52.5 us
    all_to_all x1, blocking collectives, per_device(): lax.all_to_all(outgoing, ('stream', 'span'), split_axis=0, concat_axis=0,...  33.5 us
    another operation x1, other arithmetic, per_device(): jnp.zeros((slot_count,), jnp.float32).at[slots.reshape(-1)]  21.9 us
    gather x2, local copies, waits for them, and re-layouts, per_device(): leaving = grains[:, slots] * live[None]  21.1 us
    ppermute x2, waiting for transfers between devices, padded(): lax.ppermute(lax.slice_in_dim(block, 0, width, axis=dim), axis, backward)  10.5 us
    unnamed x26, local copies, waits for them, and re-layouts  10.1 us
    ppermute x2, starting transfers between devices, padded(): lax.ppermute(lax.slice_in_dim(block, block.shape[dim] - width, None, axis...  4.75 us
  transfers between devices with their start and end apart: 6, of which 4 were waited for; matrix products, arithmetic and copies ran while one was open for 13% of the time, Pallas kernels for 0%

commit v1 on v0

v1 whole, which is shorter than its diff:
```python
import functools
import math

import jax
import jax.numpy as jnp
import numpy as np
from jax import lax
from jax.experimental import pallas as pl
from jax.experimental.pallas import tpu as pltpu
from jax.sharding import PartitionSpec as P

REACH = 3
LANES = 128

spread_cells = 1.5
drag_rate = 0.25

VMEM = pl.BlockSpec(memory_space=pltpu.VMEM)
SMEM = pl.BlockSpec(memory_space=pltpu.SMEM)
NT = (((1,), (1,)), ((), ()))
NN = (((1,), (0,)), ((), ()))


def kernel_taps():
    raw = [
        math.exp(-(k * k) / (2.0 * spread_cells * spread_cells)) for k in range(-REACH, REACH + 1)
    ]
    total = sum(raw)
    return [value / total for value in raw]


def params(mib):
    return pltpu.CompilerParams(vmem_limit_bytes=mib * 2**20)


def two_pieces(matrix):
    high = matrix.astype(jnp.bfloat16)
    low = (matrix - high.astype(np.float32)).astype(jnp.bfloat16)
    return np.stack([high, low])


def band(targets, sources):
    weights = np.array(kernel_taps() + [0.0], np.float32)
    apart = sources[None, :] - targets[:, None]
    return weights[np.where(np.abs(apart) <= REACH, apart + REACH, 2 * REACH + 1)]


def depth_operator(depth):
    cells = np.arange(depth)
    return two_pieces(band(cells, cells))


def stream_operator(rows_x, rows_y):
    ys, xs = np.divmod(np.arange(rows_x * rows_y), rows_x)
    plane, halo_y = np.divmod(np.arange(REACH * rows_y), rows_y)
    source_x = np.concatenate([xs, plane - REACH, plane + rows_x])
    source_y = np.concatenate([ys, halo_y, halo_y])
    return two_pieces(band(xs, source_x) * (ys[:, None] == source_y[None, :]))


def span_operator(rows_x, rows_y):
    xs, ys = np.divmod(np.arange(rows_x * rows_y), rows_y)
    own_y, own_x = np.divmod(np.arange(rows_x * rows_y), rows_x)
    row, halo_x = np.divmod(np.arange(REACH * rows_x), rows_x)
    source_y = np.concatenate([own_y, row - REACH, row + rows_y])
    source_x = np.concatenate([own_x, halo_x, halo_x])
    return two_pieces(band(ys, source_y) * (xs[:, None] == source_x[None, :]))


def halves(values):
    high = values.astype(jnp.bfloat16)
    return high, (values - high.astype(jnp.float32)).astype(jnp.bfloat16)


def dot(left, right, dims=NN):
    return lax.dot_general(left, right, dims, preferred_element_type=jnp.float32)


def leave_kernel(grains_ref, slots_ref, counts_ref, down_ref, up_ref, kept_ref, tail, high_rows, low_rows, gone):
    slot_count = grains_ref.shape[1]
    records = grains_ref.shape[0]
    width = slots_ref.shape[1]
    tiles = slot_count // LANES
    groups = width // LANES
    unroll = 16 if tiles % 16 == 0 else 1
    rest = records - 8

    tail[...] = jnp.zeros_like(tail)

    def fill(i, carry):
        lanes = pl.ds(pl.multiple_of(i * LANES, LANES), LANES)
        tail[0:rest, lanes] = grains_ref[8:records, lanes]
        return carry

    lax.fori_loop(0, tiles, fill, 0)

    lane = lax.broadcasted_iota(jnp.int32, (8, LANES), 1)
    for which, out_ref in ((0, down_ref), (1, up_ref)):
        live_count = counts_ref[0, which]

        def group(g, carry):
            lanes = pl.ds(pl.multiple_of(g * LANES, LANES), LANES)
            slot = jnp.broadcast_to(slots_ref[which:which + 1, lanes], (8, LANES))
            tile_of = lax.shift_right_logical(slot, 7)
            lane_of = lax.bitwise_and(slot, LANES - 1)

            def scan(h, found):
                first, second = found
                for k in range(unroll):
                    tile = h * unroll + k
                    there = pl.ds(pl.multiple_of(tile * LANES, LANES), LANES)
                    hit = tile_of == tile
                    one = jnp.take_along_axis(grains_ref[0:8, there], lane_of, axis=1, mode="promise_in_bounds")
                    two = jnp.take_along_axis(tail[:, there], lane_of, axis=1, mode="promise_in_bounds")
                    first = jnp.where(hit, one, first)
                    second = jnp.where(hit, two, second)
                return first, second

            zero = jnp.zeros((8, LANES), jnp.float32)
            first, second = lax.fori_loop(0, tiles // unroll, scan, (zero, zero))
            live = (lane + g * LANES < live_count).astype(jnp.float32)
            out_ref[0:8, lanes] = first * live
            out_ref[8:records, lanes] = (second * live)[0:rest]
            return carry

        used = lax.div(live_count + (LANES - 1), LANES)
        lax.fori_loop(0, used, group, 0)

        def blank(g, carry):
            lanes = pl.ds(pl.multiple_of(g * LANES, LANES), LANES)
            out_ref[:, lanes] = jnp.zeros((records, LANES), jnp.float32)
            return carry

        lax.fori_loop(used, groups, blank, 0)

    for which in (0, 1):
        slot = slots_ref[which:which + 1, :]
        live = lax.broadcasted_iota(jnp.int32, (1, width), 1) < counts_ref[0, which]
        tile_of = jnp.where(live, lax.shift_right_logical(slot, 7), -1)
        lane_of = lax.bitwise_and(slot, LANES - 1)
        hits = lax.broadcasted_iota(jnp.int32, (tiles, width), 0) == tile_of
        high_rows[...] = jnp.where(hits, 1.0, 0.0).astype(jnp.bfloat16)
        hits = lax.broadcasted_iota(jnp.int32, (LANES, width), 0) == lane_of
        low_rows[...] = jnp.where(hits, 1.0, 0.0).astype(jnp.bfloat16)
        counted = dot(high_rows[...], low_rows[...], NT)
        gone[...] = counted if which == 0 else gone[...] + counted

    def keep(i, carry):
        lanes = pl.ds(pl.multiple_of(i * LANES, LANES), LANES)
        kept_ref[:, lanes] = grains_ref[:, lanes] * (1.0 - gone[pl.ds(i, 1), :])
        return carry

    lax.fori_loop(0, tiles, keep, 0)


def leave(grains, slots, counts):
    records, slot_count = grains.shape
    width = slots.shape[1]
    tiles = slot_count // LANES
    return pl.pallas_call(
        leave_kernel,
        out_shape=(
            jax.ShapeDtypeStruct((records, width), jnp.float32),
            jax.ShapeDtypeStruct((records, width), jnp.float32),
            jax.ShapeDtypeStruct((records, slot_count), jnp.float32),
        ),
        in_specs=[VMEM, VMEM, SMEM],
        out_specs=(VMEM, VMEM, VMEM),
        scratch_shapes=[
            pltpu.VMEM((8, slot_count), jnp.float32),
            pltpu.VMEM((tiles, width), jnp.bfloat16),
            pltpu.VMEM((LANES, width), jnp.bfloat16),
            pltpu.VMEM((tiles, LANES), jnp.float32),
        ],
        compiler_params=params(40),
        name="leave",
    )(grains, slots, counts)


def deposit_kernel(
    channels, rows_x, rows_y, chunk, kept_ref, below_ref, above_ref, cells_ref, depth_ref,
    field_ref, low_ref, high_ref, left, right, total,
):
    columns = rows_x * rows_y
    depth = depth_ref.shape[1]
    plane = rows_y * depth
    count = len(channels)
    row = lax.broadcasted_iota(jnp.int32, (16, LANES), 0).astype(jnp.float32)
    zero = jnp.zeros((16, LANES), jnp.bfloat16)
    one = jnp.ones((16, LANES), jnp.bfloat16)
    total[...] = jnp.zeros_like(total)

    def wide(values):
        return jnp.broadcast_to(values, (16, LANES)).astype(jnp.bfloat16)

    def add(source_ref, start, cell_start):
        for j in range(chunk // LANES):
            lanes = pl.ds(start + j * LANES, LANES)
            here = slice(j * LANES, (j + 1) * LANES)
            cell = cells_ref[:, pl.ds(cell_start + j * LANES, LANES)]
            radius = source_ref[9:10, lanes]
            volume = 4.18879 * (radius * radius * radius)
            parts = [
                wide(volume if c == 0 else volume * source_ref[2 + c:3 + c, lanes]) for c in channels
            ]
            x = lax.div(cell, plane)
            rest = lax.rem(cell, plane)
            y = lax.div(rest, depth)
            column = wide((y * rows_x + x).astype(jnp.float32))
            level = wide(lax.rem(rest, depth).astype(jnp.float32))
            for k in range(columns // 16):
                hit = (row + 16.0 * k).astype(jnp.bfloat16) == column
                for c in range(count):
                    left[c * columns + 16 * k:c * columns + 16 * k + 16, here] = jnp.where(hit, parts[c], zero)
            for k in range(depth // 16):
                hit = (row + 16.0 * k).astype(jnp.bfloat16) == level
                right[16 * k:16 * k + 16, here] = jnp.where(hit, one, zero)
        total[...] += dot(left[...], right[...], NT)

    def over(source_ref, offset):
        def step(i, carry):
            start = pl.multiple_of(i * chunk, chunk)
            add(source_ref, start, pl.multiple_of(start + offset, chunk))
            return carry

        lax.fori_loop(0, source_ref.shape[1] // chunk, step, 0)

    over(kept_ref, 0)
    over(below_ref, kept_ref.shape[1])
    over(above_ref, kept_ref.shape[1] + below_ref.shape[1])

    high, low = halves(total[...])
    field_ref[...] = dot(high, depth_ref[0]) + (dot(high, depth_ref[1]) + dot(low, depth_ref[0]))
    for c in range(count):
        for k in range(REACH):
            for y in range(rows_y):
                to = (c * REACH + k) * rows_y + y
                first = c * columns + y * rows_x + k
                last = first + rows_x - REACH
                low_ref[to:to + 1, :] = field_ref[first:first + 1, :]
                high_ref[to:to + 1, :] = field_ref[last:last + 1, :]


def deposit(channels, rows_x, rows_y, kept, below, above, cells, depth_op, chunk):
    columns = rows_x * rows_y
    depth = depth_op.shape[1]
    count = len(channels)
    halo = count * REACH * rows_y
    return pl.pallas_call(
        functools.partial(deposit_kernel, channels, rows_x, rows_y, chunk),
        out_shape=(
            jax.ShapeDtypeStruct((count * columns, depth), jnp.float32),
            jax.ShapeDtypeStruct((halo, depth), jnp.float32),
            jax.ShapeDtypeStruct((halo, depth), jnp.float32),
        ),
        in_specs=[VMEM] * 5,
        out_specs=(VMEM, VMEM, VMEM),
        scratch_shapes=[
            pltpu.VMEM((count * columns, chunk), jnp.bfloat16),
            pltpu.VMEM((depth, chunk), jnp.bfloat16),
            pltpu.VMEM((count * columns, depth), jnp.float32),
        ],
        compiler_params=params(40),
        name="deposit",
    )(kept, below, above, cells, depth_op)


def mix(operator_ref, pieces):
    total = None
    start = 0
    for piece in pieces:
        size = piece.shape[0]
        take = slice(start, start + size)
        high, low = halves(piece)
        value = dot(operator_ref[0, :, take], high) + (
            dot(operator_ref[1, :, take], high) + dot(operator_ref[0, :, take], low)
        )
        total = value if total is None else total + value
        start += size
    return total


def stream_kernel(count, own_ref, before_ref, after_ref, operator_ref, field_ref, low_ref, high_ref):
    columns = own_ref.shape[0] // count
    halo = before_ref.shape[0] // count
    edge = low_ref.shape[0] // count
    for c in range(count):
        own = slice(c * columns, (c + 1) * columns)
        side = slice(c * halo, (c + 1) * halo)
        value = mix(operator_ref, [own_ref[own, :], jnp.concatenate([before_ref[side, :], after_ref[side, :]], axis=0)])
        field_ref[own, :] = value
        low_ref[c * edge:(c + 1) * edge, :] = value[0:edge]
        high_ref[c * edge:(c + 1) * edge, :] = value[columns - edge:columns]


def stream_pass(count, rows_x, own, before, after, operator):
    edge = count * REACH * rows_x
    depth = own.shape[1]
    return pl.pallas_call(
        functools.partial(stream_kernel, count),
        out_shape=(
            jax.ShapeDtypeStruct(own.shape, jnp.float32),
            jax.ShapeDtypeStruct((edge, depth), jnp.float32),
            jax.ShapeDtypeStruct((edge, depth), jnp.float32),
        ),
        in_specs=[VMEM] * 4,
        out_specs=(VMEM, VMEM, VMEM),
        compiler_params=params(40),
        name="stream_pass",
    )(own, before, after, operator)


def span_kernel(count, rows_q, own_ref, before_ref, after_ref, operator_ref, fluid_ref, picks_ref, solid_ref, out_ref):
    columns = own_ref.shape[0] // count
    edge = before_ref.shape[0] // count
    slots = picks_ref.shape[0]
    choose = picks_ref[...] == lax.broadcasted_iota(jnp.int32, (slots, columns), 1)
    choose = jnp.where(choose, 1.0, 0.0).astype(jnp.bfloat16)
    solids = []
    for c in range(count):
        own = slice(c * columns, (c + 1) * columns)
        side = slice(c * edge, (c + 1) * edge)
        value = mix(operator_ref, [own_ref[own, :], before_ref[side, :], after_ref[side, :]])
        solid_ref[own, :] = value
        solids.append(value)
    for c in range(count):
        if c + 1 < count:
            flow = fluid_ref[c * columns:(c + 1) * columns, :]
            value = flow + drag_rate * (solids[c + 1] - solids[0] * flow)
        else:
            value = 1.0 / (1.0 + solids[0])
        first, rest = halves(value)
        second, third = halves(value - first.astype(jnp.float32))
        sent = dot(choose, first) + (dot(choose, second) + dot(choose, third))
        out_ref[:, c * rows_q:(c + 1) * rows_q, :] = sent.reshape(slots // rows_q, rows_q, -1)


def span_pass(count, own, before, after, operator, fluid, picks, peers, rows_q):
    depth = own.shape[1]
    return pl.pallas_call(
        functools.partial(span_kernel, count, rows_q),
        out_shape=(
            jax.ShapeDtypeStruct(own.shape, jnp.float32),
            jax.ShapeDtypeStruct((peers, count * rows_q, depth), jnp.float32),
        ),
        in_specs=[VMEM] * 6,
        out_specs=(VMEM, VMEM),
        compiler_params=params(40),
        name="span_pass",
    )(own, before, after, operator, fluid, picks)


def shift(value, axis, steps, periodic):
    count = lax.axis_size(axis)
    pairs = [
        (source, (source + steps) % count)
        for source in range(count)
        if periodic or 0 <= source + steps < count
    ]
    return lax.ppermute(value, axis, pairs)


def per_device(grains, send_slots, send_counts, cell_index, fluid, block_slots, block_counts):
    rows_x, rows_y, depth = fluid.shape[1:]
    columns = rows_x * rows_y
    width = send_slots.shape[2]
    peers, rows_q = block_slots.shape[1:]

    down, up, kept = leave(grains, send_slots[0], send_counts)
    below = shift(down, "stream", 1, True)
    above = shift(up, "stream", -1, True)
    grains_after = jnp.concatenate([kept, below, above], axis=1)

    alive = lax.broadcasted_iota(jnp.int32, (peers, rows_q), 1) < block_counts[0][:, None]
    picks = jnp.where(alive, block_slots[0], -1).reshape(peers * rows_q, 1)

    depth_op = jnp.asarray(depth_operator(depth))
    stream_op = jnp.asarray(stream_operator(rows_x, rows_y))
    span_op = jnp.asarray(span_operator(rows_x, rows_y))
    cells = cell_index.reshape(1, -1)
    chunk = math.gcd(grains.shape[1], math.gcd(width, 2048))

    field, low, high = deposit((0, 1, 2, 3), rows_x, rows_y, kept, below, above, cells, depth_op, chunk)
    before = shift(high, "stream", 1, True)
    after = shift(low, "stream", -1, True)
    field, low, high = stream_pass(4, rows_x, field, before, after, stream_op)
    before = shift(high, "span", 1, False)
    after = shift(low, "span", -1, False)
    solid, outgoing = span_pass(
        4, field, before, after, span_op, fluid.reshape(3 * columns, depth), picks, peers, rows_q
    )
    arrived = lax.all_to_all(outgoing, ("stream", "span"), split_axis=0, concat_axis=0, tiled=True)
    received = arrived.reshape(peers, 4, rows_q, depth).transpose(0, 2, 1, 3)
    return grains_after, solid.reshape(4, rows_x, rows_y, depth), received[None]


def solution(mesh):
    return jax.shard_map(
        per_device,
        mesh=mesh,
        in_specs=(
            P(None, ("stream", "span")),
            P(("stream", "span"), None, None),
            P(("stream", "span"), None),
            P(("stream", "span")),
            P(None, "stream", "span", None),
            P(("stream", "span"), None, None),
            P(("stream", "span"), None),
        ),
        out_specs=(
            P(None, ("stream", "span")),
            P(None, "stream", "span", None),
            P(("stream", "span"), None, None, None, None),
        ),
        check_vma=False,
    )
```

time: 175 us -> 135 us (0.77)
  matrix products: 54.4 us -> 0 us
  Pallas kernels: 0 us -> 52.7 us
  blocking collectives: 33.5 us -> 0 us
  waiting for transfers between devices: 12.7 us -> 39.2 us
  other arithmetic: 27.7 us -> 3.61 us
  local copies, waits for them, and re-layouts: 35.6 us -> 16.5 us
  starting transfers between devices: 8.99 us -> 22.2 us
    dot_general x15 -> x0, matrix products: 54.4 us -> none  [the longest x14 52.5 us: add_step(): jnp.dot(left_side, pick_rest, preferred_element_type=jnp.float32)]
    pallas_call x0 -> x4, Pallas kernels: none -> 52.7 us  [the longest x1 25.1 us: leave(): pl.pallas_call(leave_kernel, out_shape=(jax.ShapeDtypeStruct((records, wi...]
    all_to_all x1 -> x0, blocking collectives: 33.5 us -> none  [per_device(): lax.all_to_all(outgoing, ('stream', 'span'), split_axis=0, concat_axis=0,...]
    all_to_all x0 -> x1, waiting for transfers between devices: none -> 25 us  [per_device(): lax.all_to_all(outgoing, ('stream', 'span'), split_axis=0, concat_axis=0,...]
    another operation x3 -> x0, other arithmetic: 22.5 us -> none  [the longest x1 21.9 us: per_device(): jnp.zeros((slot_count,), jnp.float32).at[slots.reshape(-1)]]
    gather x3 -> x0, local copies, waits for them, and re-layouts: 22.4 us -> none  [the longest x2 21.1 us: per_device(): leaving = grains[:, slots] * live[None]]
    all_to_all x0 -> x1, starting transfers between devices: none -> 10.1 us  [per_device(): lax.all_to_all(outgoing, ('stream', 'span'), split_axis=0, concat_axis=0,...]
    ppermute x6, starting transfers between devices: 8.99 us -> 12.2 us  [shift(): return lax.ppermute(value, axis, pairs)]
  transfers between devices with their start and end apart: 6 -> 7, of which waited for: 4 -> 7; matrix products, arithmetic and copies ran while one was open for 13% -> 4% of each run, Pallas kernels for 0% -> 0%
where the time goes in v1:
time: 135 us
  Pallas kernels  52.7 us (39%)
  waiting for transfers between devices  39.2 us (29%)
  starting transfers between devices  22.2 us (16%)
  local copies, waits for them, and re-layouts  16.5 us (12%)
  other arithmetic  3.61 us (3%)
    pallas_call x1, Pallas kernels, leave(): pl.pallas_call(leave_kernel, out_shape=(jax.ShapeDtypeStruct((records, wi...  25.1 us
    all_to_all x1, waiting for transfers between devices, per_device(): lax.all_to_all(outgoing, ('stream', 'span'), split_axis=0, concat_axis=0,...  25 us
    pallas_call x1, Pallas kernels, deposit(): pl.pallas_call(functools.partial(deposit_kernel, channels, rows_x, rows_y...  22.3 us
    ppermute x6, waiting for transfers between devices, shift(): return lax.ppermute(value, axis, pairs)  14.2 us
    unnamed x37, local copies, waits for them, and re-layouts  13 us
    ppermute x6, starting transfers between devices, shift(): return lax.ppermute(value, axis, pairs)  12.2 us
    all_to_all x1, starting transfers between devices, per_device(): lax.all_to_all(outgoing, ('stream', 'span'), split_axis=0, concat_axis=0,...  10.1 us
    pallas_call x1, Pallas kernels, span_pass(): pl.pallas_call(functools.partial(span_kernel, count, rows_q), out_shape=(...  3.53 us
  transfers between devices with their start and end apart: 7, of which 7 were waited for; matrix products, arithmetic and copies ran while one was open for 4% of the time, Pallas kernels for 0%

profile of v1, /device:TPU:1, one launch (start us, length us, event | category | flops | bytes accessed | tf_op | source)
XLA Modules:
  0.0 135.0 jit_solution(15053783313679875381)
XLA Ops:
  0.6 1.4 %copy-done = f32[13,24576]{1,0:T(8,128)S(1)} copy-done((f32[13,24576]{1,0:T(8,128)S(1)}, f32[13,24576]{1,0:T(8,128)}, u32[]{:S(2)}) %copy-start) | copy-done | bytes 1277976
  3.4 25.1 %leave.1 = (f32[13,2048]{1,0:T(8,128)S(1)}, f32[13,2048]{1,0:T(8,128)S(1)}, f32[13,24576]{1,0:T(8,128)S(1)}) custom-call(f32[13,24576]{1,0:T(8,128)S(1)} %copy-done, s32[2,2048]{1,0:T(2,128)S(1)} %bitcast.13, s32[1,2]{1,0:T(1,128)S(1)} %copy-done.16), custom_call_target="tpu_custom_call" | custom-call | tf_op jit(solution)/shard_map/leave/pallas_call | solution.py:160
  28.5 2.7 %collective-permute-start = (f32[13,2048]{1,0:T(8,128)S(1)}, f32[13,2048]{1,0:T(8,128)S(1)}, u32[]{:S(2)}, u32[]{:S(2)}) collective-permute-start(f32[13,2048]{1,0:T(8,128)S(1)} %get-tuple-element.15), channel_id=1, source_target_pairs={{0,4},{4,8},{8,12},{12,16},{16,20},{20,24},{24,28},{28,0},{1,5},{5... | collective-permute-start | bytes 319496 | tf_op jit(solution)/shard_map/ppermute | solution.py:360
  31.2 2.5 %collective-permute-start.1 = (f32[13,2048]{1,0:T(8,128)S(1)}, f32[13,2048]{1,0:T(8,128)S(1)}, u32[]{:S(2)}, u32[]{:S(2)}) collective-permute-start(f32[13,2048]{1,0:T(8,128)S(1)} %get-tuple-element.16), channel_id=1, source_target_pairs={{0,28},{4,0},{8,4},{12,8},{16,12},{20,16},{24,20},{28,24},{1,29},{... | collective-permute-start | bytes 319496 | tf_op jit(solution)/shard_map/ppermute | solution.py:360
  34.4 1.7 %collective-permute-done.1.above_ref = f32[13,2048]{1,0:T(8,128)S(1)} collective-permute-done((f32[13,2048]{1,0:T(8,128)S(1)}, f32[13,2048]{1,0:T(8,128)S(1)}, u32[]{:S(2)}, u32[]{:S(2)}) %collective-permute-start.1) | collective-permute-done | bytes 106528 | tf_op jit(solution)/shard_map/ppermute | solution.py:360
  36.1 1.0 copy-done.9
  38.0 22.3 %deposit.1 = (f32[1024,256]{1,0:T(8,128)S(1)}, f32[96,256]{1,0:T(8,128)S(1)}, f32[96,256]{1,0:T(8,128)S(1)}) custom-call(f32[13,24576]{1,0:T(8,128)S(1)} %get-tuple-element.14.kept_ref, f32[13,2048]{1,0:T(8,128)S(1)} %collective-permute-done.below_ref, f32[13,2048]{1,0:T(8,128)S(1)} %collective-permute-done.1.above_ref, s32[1,28672]{1,0:T(1,128)S(1)} %bitcast.12, ...), custom_call_target="tpu_custom_call" | custom-call | tf_op jit(solution)/shard_map/deposit/pallas_call | solution.py:249
  61.3 3.7 %collective-permute-start.2 = (f32[96,256]{1,0:T(8,128)S(1)}, f32[96,256]{1,0:T(8,128)S(1)}, u32[]{:S(2)}, u32[]{:S(2)}) collective-permute-start(f32[96,256]{1,0:T(8,128)S(1)} %get-tuple-element.18), channel_id=1, source_target_pairs={{0,4},{4,8},{8,12},{12,16},{16,20},{20,24},{24,28},{28,0},{1,5},{5... | collective-permute-start | bytes 294920 | tf_op jit(solution)/shard_map/ppermute | solution.py:360
  65.1 1.6 %collective-permute-done.2.before_ref = f32[96,256]{1,0:T(8,128)S(1)} collective-permute-done((f32[96,256]{1,0:T(8,128)S(1)}, f32[96,256]{1,0:T(8,128)S(1)}, u32[]{:S(2)}, u32[]{:S(2)}) %collective-permute-start.2) | collective-permute-done | bytes 98336 | tf_op jit(solution)/shard_map/ppermute | solution.py:360
  67.3 4.8 %collective-permute-done.3.after_ref = f32[96,256]{1,0:T(8,128)S(1)} collective-permute-done((f32[96,256]{1,0:T(8,128)S(1)}, f32[96,256]{1,0:T(8,128)S(1)}, u32[]{:S(2)}, u32[]{:S(2)}) %collective-permute-start.3) | collective-permute-done | bytes 98336 | tf_op jit(solution)/shard_map/ppermute | solution.py:360
  72.8 1.2 copy-done.2
  74.0 1.0 copy-done.8
  76.8 1.8 %stream_pass.1 = (f32[1024,256]{1,0:T(8,128)S(1)}, f32[384,256]{1,0:T(8,128)}, f32[384,256]{1,0:T(8,128)}) custom-call(f32[1024,256]{1,0:T(8,128)S(1)} %copy-done.2, f32[96,256]{1,0:T(8,128)S(1)} %copy-done.12, f32[96,256]{1,0:T(8,128)S(1)} %copy-done.14, bf16[2,256,304]{2,1,0:T(8,128)(2,1)S(1)} %copy-done.8), custom_call_target="tpu_custom_call" | custom-call | tf_op jit(solution)/shard_map/stream_pass/pallas_call | solution.py:299
  78.6 2.0 %collective-permute-start.4 = (f32[384,256]{1,0:T(8,128)}, f32[384,256]{1,0:T(8,128)}, u32[]{:S(2)}, u32[]{:S(2)}) collective-permute-start(f32[384,256]{1,0:T(8,128)} %get-tuple-element.21), channel_id=1, source_target_pairs={{0,1},{1,2},{2,3},{4,5},{5,6},{6,7},{8,9},{9,10},{10,11},{12,13},{... | collective-permute-start | bytes 1179656 | tf_op jit(solution)/shard_map/ppermute | solution.py:360
  80.6 1.3 collective-permute-start.5
  81.9 1.3 iota_compare_fusion
  83.2 1.4 %lt.24 = pred[256,1]{1,0:T(8,128)(4,1)} reshape(pred[32,8]{1,0:T(8,128)(4,1)} %iota_compare_fusion) | data formatting | bytes 512 | tf_op jit(solution)/shard_map/lt | solution.py:374
  86.8 4.8 %collective-permute-done.5.after_ref = f32[384,256]{1,0:T(8,128)} collective-permute-done((f32[384,256]{1,0:T(8,128)}, f32[384,256]{1,0:T(8,128)}, u32[]{:S(2)}, u32[]{:S(2)}) %collective-permute-start.5) | collective-permute-done | bytes 393248 | tf_op jit(solution)/shard_map/ppermute | solution.py:360
  91.7 1.0 copy-done.5
  92.7 3.5 %span_pass.1 = (f32[1024,256]{1,0:T(8,128)}, f32[32,32,256]{2,1,0:T(8,128)S(1)}) custom-call(f32[1024,256]{1,0:T(8,128)S(1)} %get-tuple-element.20.own_ref, f32[384,256]{1,0:T(8,128)} %collective-permute-done.4.before_ref, f32[384,256]{1,0:T(8,128)} %collective-permute-done.5.after_ref, bf16[2,256,448]{2,1,0:T(8,128)(2,1)S(1)} %copy-done.5, ...), custom_call_target="tpu_custom_call" | custom-call | tf_op jit(solution)/shard_map/span_pass/pallas_call | solution.py:340
  97.2 10.1 %all-to-all-start = ((f32[32,32,256]{2,1,0:T(8,128)}), f32[32,32,256]{2,1,0:T(8,128)S(1)}, u32[]{:S(2)}, u32[]{:S(2)}) async-start(f32[32,32,256]{2,1,0:T(8,128)} %copy-done.3), calls=%async_computation | async-start | bytes 2097152 | tf_op jit(solution)/shard_map/all_to_all | solution.py:392
  107.3 1.3 pad_maximum_fusion
  108.6 25.0 %all-to-all-done = f32[32,32,256]{2,1,0:T(8,128)S(1)} async-done(((f32[32,32,256]{2,1,0:T(8,128)}), f32[32,32,256]{2,1,0:T(8,128)S(1)}, u32[]{:S(2)}, u32[]{:S(2)}) %all-to-all-start) | async-done | bytes 1048608 | tf_op jit(solution)/shard_map/all_to_all | solution.py:392
  133.6 1.4 %copy.20 = f32[32,4,8,256]{3,1,2,0:T(4,128)} copy(f32[32,4,8,256]{3,2,1,0:T(8,128)S(1)} %bitcast.14) | data formatting | bytes 2097152 | tf_op jit(solution)/shard_map/reshape | solution.py:393
  (37 shorter events, 10.3 us)
Async XLA Ops:
  0.6 1.4 %copy-start = (f32[13,24576]{1,0:T(8,128)S(1)}, f32[13,24576]{1,0:T(8,128)}, u32[]{:S(2)}) copy-start(f32[13,24576]{1,0:T(8,128)} %grains_ref.1) | copy-start | bytes 3833860
  2.0 0.7 copy-start.15
  2.8 0.7 copy-start.16
  3.4 61.6 %copy-start.17 = (s32[1,32,8]{1,2,0:T(8,128)S(1)}, s32[1,32,8]{1,2,0:T(8,128)}, u32[]{:S(2)}) copy-start(s32[1,32,8]{1,2,0:T(8,128)} %param.15) | copy-start | bytes 3076
  28.5 5.9 %collective-permute-start = (f32[13,2048]{1,0:T(8,128)S(1)}, f32[13,2048]{1,0:T(8,128)S(1)}, u32[]{:S(2)}, u32[]{:S(2)}) collective-permute-start(f32[13,2048]{1,0:T(8,128)S(1)} %get-tuple-element.15), channel_id=1, source_target_pairs={{0,4},{4,8},{8,12},{12,16},{16,20},{20,24},{24,28},{28,0},{1,5},{5... | collective-permute-start | bytes 319496 | tf_op jit(solution)/shard_map/ppermute | solution.py:360
  31.2 5.0 %collective-permute-start.1 = (f32[13,2048]{1,0:T(8,128)S(1)}, f32[13,2048]{1,0:T(8,128)S(1)}, u32[]{:S(2)}, u32[]{:S(2)}) collective-permute-start(f32[13,2048]{1,0:T(8,128)S(1)} %get-tuple-element.16), channel_id=1, source_target_pairs={{0,28},{4,0},{8,4},{12,8},{16,12},{20,16},{24,20},{28,24},{1,29},{... | collective-permute-start | bytes 319496 | tf_op jit(solution)/shard_map/ppermute | solution.py:360
  36.1 24.2 %copy-start.6 = (f32[13,2048]{1,0:T(8,128)}, f32[13,2048]{1,0:T(8,128)S(1)}, u32[]{:S(2)}) copy-start(f32[13,2048]{1,0:T(8,128)S(1)} %collective-permute-done.1.above_ref) | copy-start | bytes 319492
  36.1 1.0 copy-start.9
  37.1 0.9 copy-start.10
  38.0 53.6 %copy-start.4 = (f32[3,32,8,256]{3,2,1,0:T(8,128)S(1)}, f32[3,32,8,256]{3,2,1,0:T(8,128)}, u32[]{:S(2)}) copy-start(f32[3,32,8,256]{3,2,1,0:T(8,128)} %param.14) | copy-start | bytes 2359300
  60.3 1.0 copy-start.1
  61.3 5.3 %collective-permute-start.2 = (f32[96,256]{1,0:T(8,128)S(1)}, f32[96,256]{1,0:T(8,128)S(1)}, u32[]{:S(2)}, u32[]{:S(2)}) collective-permute-start(f32[96,256]{1,0:T(8,128)S(1)} %get-tuple-element.18), channel_id=1, source_target_pairs={{0,4},{4,8},{8,12},{12,16},{16,20},{20,24},{24,28},{28,0},{1,5},{5... | collective-permute-start | bytes 294920 | tf_op jit(solution)/shard_map/ppermute | solution.py:360
  65.0 7.1 %collective-permute-start.3 = (f32[96,256]{1,0:T(8,128)S(1)}, f32[96,256]{1,0:T(8,128)S(1)}, u32[]{:S(2)}, u32[]{:S(2)}) collective-permute-start(f32[96,256]{1,0:T(8,128)S(1)} %get-tuple-element.19), channel_id=1, source_target_pairs={{0,28},{4,0},{8,4},{12,8},{16,12},{20,16},{24,20},{28,24},{1,29},{... | collective-permute-start | bytes 294920 | tf_op jit(solution)/shard_map/ppermute | solution.py:360
  66.6 0.6 copy-start.11
  72.7 1.2 copy-start.2
  74.0 1.0 copy-start.8
  75.0 0.9 copy-start.12
  75.9 0.9 copy-start.14
  78.6 8.2 %collective-permute-start.4 = (f32[384,256]{1,0:T(8,128)}, f32[384,256]{1,0:T(8,128)}, u32[]{:S(2)}, u32[]{:S(2)}) collective-permute-start(f32[384,256]{1,0:T(8,128)} %get-tuple-element.21), channel_id=1, source_target_pairs={{0,1},{1,2},{2,3},{4,5},{5,6},{6,7},{8,9},{9,10},{10,11},{12,13},{... | collective-permute-start | bytes 1179656 | tf_op jit(solution)/shard_map/ppermute | solution.py:360
  80.6 11.0 %collective-permute-start.5 = (f32[384,256]{1,0:T(8,128)}, f32[384,256]{1,0:T(8,128)}, u32[]{:S(2)}, u32[]{:S(2)}) collective-permute-start(f32[384,256]{1,0:T(8,128)} %get-tuple-element.22), channel_id=1, source_target_pairs={{1,0},{2,1},{3,2},{5,4},{6,5},{7,6},{9,8},{10,9},{11,10},{13,12},{... | collective-permute-start | bytes 1179656 | tf_op jit(solution)/shard_map/ppermute | solution.py:360
  91.7 1.0 copy-start.5
  96.2 1.0 copy-start.3
  97.2 10.1 %copy-start.7 = (f32[13,2048]{1,0:T(8,128)S(1)}, f32[13,2048]{1,0:T(8,128)}, u32[]{:S(2)}) copy-start(f32[13,2048]{1,0:T(8,128)} %copy-done.6) | copy-start | bytes 319492
  97.2 36.4 %all-to-all-start = ((f32[32,32,256]{2,1,0:T(8,128)}), f32[32,32,256]{2,1,0:T(8,128)S(1)}, u32[]{:S(2)}, u32[]{:S(2)}) async-start(f32[32,32,256]{2,1,0:T(8,128)} %copy-done.3), calls=%async_computation | async-start | bytes 2097152 | tf_op jit(solution)/shard_map/all_to_all | solution.py:392
  (1 other events, 0.6 us)

commit v2 on v0

v2 whole, which is shorter than its diff:
```python
import functools
import math

import jax
import jax.numpy as jnp
from jax import lax
from jax.experimental import pallas as pl
from jax.experimental.pallas import tpu as pltpu
from jax.sharding import PartitionSpec as P

REACH = 3
LANES = 128
RECORD = 16

spread_cells = 1.5
drag_rate = 0.25

VMEM = pl.BlockSpec(memory_space=pltpu.VMEM)
ANY = pl.BlockSpec(memory_space=pl.ANY)
HBM = pl.BlockSpec(memory_space=pltpu.HBM)
NT = (((1,), (1,)), ((), ()))
NN = (((1,), (0,)), ((), ()))

QUANT_ROW = (0, 3, 4, 5)
COLUMN_ROW = 6
LEVEL_ROW = 7


def kernel_taps():
    raw = [
        math.exp(-(k * k) / (2.0 * spread_cells * spread_cells)) for k in range(-REACH, REACH + 1)
    ]
    total = sum(raw)
    return [value / total for value in raw]


def params(mib):
    return pltpu.CompilerParams(vmem_limit_bytes=mib * 2**20)


def cost(micros):
    return pl.CostEstimate(flops=0, bytes_accessed=int(micros * 3.0e6), transcendentals=0)


def split(values, size):
    if size & (size - 1):
        return lax.div(values, size), lax.rem(values, size)
    return lax.shift_right_logical(values, size.bit_length() - 1), lax.bitwise_and(values, size - 1)


def halves(values):
    high = values.astype(jnp.bfloat16)
    return high, (values - high.astype(jnp.float32)).astype(jnp.bfloat16)


def dot(left, right, dims=NN):
    return lax.dot_general(left, right, dims, preferred_element_type=jnp.float32)


def wide(values):
    return jnp.broadcast_to(values, (16, LANES)).astype(jnp.bfloat16)


def lane_tile(i):
    return pl.ds(pl.multiple_of(i * LANES, LANES), LANES)


def in_hbm(*values):
    return tuple(pltpu.with_memory_space_constraint(value, pltpu.HBM) for value in values)


def leave_kernel(
    grains_ref, slots_hbm, counts_hbm, down_ref, up_ref, stage, table, picked, slots_v, slots_s, counts_s, sems
):
    records, slot_count = grains_ref.shape
    width = down_ref.shape[1]
    rows = table.shape[0]
    parts = slot_count // rows if slot_count % rows == 0 else slot_count // rows + 1
    copies = [
        pltpu.make_async_copy(slots_hbm, slots_v, sems.at[0]),
        pltpu.make_async_copy(slots_hbm, slots_s, sems.at[1]),
        pltpu.make_async_copy(counts_hbm, counts_s, sems.at[2]),
    ]
    for copy in copies:
        copy.start()

    for part in range(parts):
        size = min(rows, slot_count - part * rows)
        here = slice(part * rows, part * rows + size)
        stage[part * RECORD:part * RECORD + 8, 0:size] = grains_ref[0:8, here]
        stage[part * RECORD + 8:part * RECORD + records, 0:size] = grains_ref[8:records, here]
    for block in range(rows // LANES):
        here = slice(block * LANES, (block + 1) * LANES)
        table[here, :] = jnp.transpose(stage[:, here])
    for copy in copies:
        copy.wait()

    run = picked.shape[0]
    lane = lax.broadcasted_iota(jnp.int32, (8, LANES), 1)
    for which, out_ref in ((0, down_ref), (1, up_ref)):
        live_count = counts_s[0, which]

        def gather(i, carry):
            base = i * run
            for k in range(run):
                row = lax.bitwise_and(slots_s[which, base + k], rows - 1)
                picked[k:k + 1, :] = table[pl.ds(row, 1), :]
            for piece in range(run // LANES):
                lanes = pl.ds(pl.multiple_of(base + piece * LANES, LANES), LANES)
                turned = jnp.transpose(picked[piece * LANES:(piece + 1) * LANES, :])
                slot = jnp.broadcast_to(slots_v[which:which + 1, lanes], (8, LANES))
                part_of = lax.shift_right_logical(slot, rows.bit_length() - 1)
                live = lane + (base + piece * LANES) < live_count
                first = jnp.zeros((8, LANES), jnp.float32)
                second = first
                for part in range(parts):
                    hit = jnp.logical_and(live, part_of == part)
                    first = jnp.where(hit, turned[part * RECORD:part * RECORD + 8], first)
                    second = jnp.where(hit, turned[part * RECORD + 8:part * RECORD + 16], second)
                out_ref[0:8, lanes] = first
                out_ref[8:records, lanes] = second[0:records - 8]
            return carry

        used = lax.div(live_count + (run - 1), run)
        lax.fori_loop(0, used, gather, 0)

        def blank(i, carry):
            lanes = pl.ds(pl.multiple_of(i * run, LANES), run)
            out_ref[:, lanes] = jnp.zeros((records, run), jnp.float32)
            return carry

        lax.fori_loop(used, width // run, blank, 0)


def leave(grains, slots, counts):
    records, slot_count = grains.shape
    width = slots.shape[1]
    rows = max(LANES, 1 << (-(-slot_count // 8) - 1).bit_length())
    run = 2 * LANES if width % (2 * LANES) == 0 else LANES
    out = jax.ShapeDtypeStruct((records, width), jnp.float32)
    return pl.pallas_call(
        leave_kernel,
        out_shape=(out, out),
        in_specs=[VMEM, HBM, HBM],
        out_specs=(VMEM, VMEM),
        scratch_shapes=[
            pltpu.VMEM((LANES, rows), jnp.float32),
            pltpu.VMEM((rows, LANES), jnp.float32),
            pltpu.VMEM((run, LANES), jnp.float32),
            pltpu.VMEM(slots.shape, jnp.int32),
            pltpu.SMEM(slots.shape, jnp.int32),
            pltpu.SMEM(counts.shape, jnp.int32),
            pltpu.SemaphoreType.DMA((3,)),
        ],
        compiler_params=params(16),
        cost_estimate=cost(8),
        name="leave",
    )(grains, *in_hbm(slots, counts))


def weights_at(apart):
    taps = kernel_taps()[REACH:]
    apart = jnp.abs(apart)
    value = jnp.where(apart == 0, taps[0], 0.0)
    for k in range(1, REACH + 1):
        value = jnp.where(apart == k, taps[k], value)
    return value


def put_operator(out_ref, start, value):
    high, low = halves(value)
    stop = start + value.shape[1]
    out_ref[0, :, start:stop] = high
    out_ref[1, :, start:stop] = low


def keep_kernel(
    rows_x, rows_y, depth, grains_ref, slots_hbm, counts_hbm, cells_hbm, picks_hbm, alive_hbm,
    after_ref, quant_ref, depth_ref, stream_ref, span_ref, choose_ref,
    slots_v, counts_s, cells_v, picks_v, alive_v, high_rows, low_rows, gone, sems,
):
    records, slot_count = grains_ref.shape
    total = after_ref.shape[1]
    width = slots_v.shape[1]
    tiles = slot_count // LANES
    columns = rows_x * rows_y
    sources = (slots_hbm, counts_hbm, cells_hbm, picks_hbm, alive_hbm)
    targets = (slots_v, counts_s, cells_v, picks_v, alive_v)
    copies = [
        pltpu.make_async_copy(source, target, sems.at[i])
        for i, (source, target) in enumerate(zip(sources, targets))
    ]
    for copy in copies:
        copy.start()

    target = lax.broadcasted_iota(jnp.int32, (depth, depth), 0)
    source = lax.broadcasted_iota(jnp.int32, (depth, depth), 1)
    put_operator(depth_ref, 0, weights_at(target - source))

    own = (columns, columns)
    target_y, target_x = split(lax.broadcasted_iota(jnp.int32, own, 0), rows_x)
    source_y, source_x = split(lax.broadcasted_iota(jnp.int32, own, 1), rows_x)
    put_operator(stream_ref, 0, jnp.where(target_y == source_y, weights_at(target_x - source_x), 0.0))
    side = (columns, 2 * REACH * rows_y)
    target_y, target_x = split(lax.broadcasted_iota(jnp.int32, side, 0), rows_x)
    plane, source_y = split(lax.broadcasted_iota(jnp.int32, side, 1), rows_y)
    source_x = jnp.where(plane < REACH, plane - REACH, plane - REACH + rows_x)
    put_operator(stream_ref, columns, jnp.where(target_y == source_y, weights_at(target_x - source_x), 0.0))

    target_x, target_y = split(lax.broadcasted_iota(jnp.int32, own, 0), rows_y)
    source_y, source_x = split(lax.broadcasted_iota(jnp.int32, own, 1), rows_x)
    put_operator(span_ref, 0, jnp.where(target_x == source_x, weights_at(target_y - source_y), 0.0))
    side = (columns, 2 * REACH * rows_x)
    target_x, target_y = split(lax.broadcasted_iota(jnp.int32, side, 0), rows_y)
    row, source_x = split(lax.broadcasted_iota(jnp.int32, side, 1), rows_x)
    source_y = jnp.where(row < REACH, row - REACH, row - REACH + rows_y)
    put_operator(span_ref, columns, jnp.where(target_x == source_x, weights_at(target_y - source_y), 0.0))

    for copy in copies:
        copy.wait()

    rows_q, peers = picks_v.shape
    alive = lax.broadcasted_iota(jnp.int32, (rows_q, peers), 0) < alive_v[...]
    picks = jnp.where(alive, picks_v[...], -1)
    place_e, place_q = split(lax.broadcasted_iota(jnp.int32, (peers * rows_q, peers), 0), rows_q)
    here = place_e == lax.broadcasted_iota(jnp.int32, (peers * rows_q, peers), 1)
    column = lax.broadcasted_iota(jnp.int32, (columns, peers), 0)
    chosen = None
    for q in range(rows_q):
        place = jnp.where(jnp.logical_and(here, place_q == q), 1.0, 0.0).astype(jnp.bfloat16)
        named = jnp.where(column == picks[q:q + 1, :], 1.0, 0.0).astype(jnp.bfloat16)
        value = dot(place, named, NT)
        chosen = value if chosen is None else chosen + value
    choose_ref[...] = chosen.astype(jnp.bfloat16)

    row16 = lax.broadcasted_iota(jnp.int32, (16, LANES), 0).astype(jnp.float32)
    lane = lax.broadcasted_iota(jnp.int32, (1, LANES), 1)
    zero = jnp.zeros((16, LANES), jnp.bfloat16)
    one = jnp.ones((16, LANES), jnp.bfloat16)
    for which in (0, 1):

        def mark(i, carry):
            lanes = lane_tile(i)
            to = pl.ds(pl.multiple_of(which * width + i * LANES, LANES), LANES)
            slot = slots_v[which:which + 1, lanes]
            tile_of, lane_of = split(slot, LANES)
            tile_of = jnp.where(lane + i * LANES < counts_s[0, which], tile_of, -1)
            tile_of = wide(tile_of.astype(jnp.float32))
            lane_of = wide(lane_of.astype(jnp.float32))
            for k in range(high_rows.shape[0] // 16):
                hit = (row16 + 16.0 * k).astype(jnp.bfloat16) == tile_of
                high_rows[16 * k:16 * k + 16, to] = jnp.where(hit, one, zero)
            for k in range(LANES // 16):
                hit = (row16 + 16.0 * k).astype(jnp.bfloat16) == lane_of
                low_rows[16 * k:16 * k + 16, to] = jnp.where(hit, one, zero)
            return carry

        lax.fori_loop(0, width // LANES, mark, 0, unroll=4)
    gone[...] = dot(high_rows[...], low_rows[...], NT)

    row8 = lax.broadcasted_iota(jnp.int32, (8, LANES), 0)

    def place(cell):
        x, rest = split(cell, rows_y * depth)
        y, level = split(rest, depth)
        return (y * rows_x + x).astype(jnp.float32), level.astype(jnp.float32)

    def keep(i, carry):
        lanes = lane_tile(i)
        stay = 1.0 - gone[pl.ds(i, 1), :]
        head = grains_ref[0:8, lanes] * stay
        rest = grains_ref[8:records, lanes] * stay
        after_ref[0:8, lanes] = head
        after_ref[8:records, lanes] = rest
        radius = rest[1:2]
        volume = 4.18879 * (radius * radius * radius)
        col, lev = place(cells_v[:, lanes])
        value = jnp.where(row8 == QUANT_ROW[0], volume, volume * head)
        value = jnp.where(row8 == COLUMN_ROW, col, value)
        quant_ref[:, lanes] = jnp.where(row8 == LEVEL_ROW, lev, value)
        return carry

    lax.fori_loop(0, tiles, keep, 0, unroll=8)

    def arrivals(i, carry):
        lanes = lane_tile(i)
        col, lev = place(cells_v[:, lanes])
        quant_ref[:, lanes] = jnp.where(row8 == COLUMN_ROW, col, lev)
        return carry

    lax.fori_loop(tiles, total // LANES, arrivals, 0, unroll=8)


def keep(grains, slots, counts, cells, picks, alive, rows_x, rows_y, depth):
    records, slot_count = grains.shape
    total = cells.shape[1]
    columns = rows_x * rows_y
    marks = -(-(slot_count // LANES) // 16) * 16
    f32, bf16, i32 = jnp.float32, jnp.bfloat16, jnp.int32
    return pl.pallas_call(
        functools.partial(keep_kernel, rows_x, rows_y, depth),
        out_shape=(
            jax.ShapeDtypeStruct((records, total), f32),
            jax.ShapeDtypeStruct((8, total), f32),
            jax.ShapeDtypeStruct((2, depth, depth), bf16),
            jax.ShapeDtypeStruct((2, columns, columns + 2 * REACH * rows_y), bf16),
            jax.ShapeDtypeStruct((2, columns, columns + 2 * REACH * rows_x), bf16),
            jax.ShapeDtypeStruct((picks.size, columns), bf16),
        ),
        in_specs=[VMEM] + [HBM] * 5,
        out_specs=(VMEM,) * 6,
        scratch_shapes=[
            pltpu.VMEM(slots.shape, i32),
            pltpu.SMEM(counts.shape, i32),
            pltpu.VMEM(cells.shape, i32),
            pltpu.VMEM(picks.shape, i32),
            pltpu.VMEM(alive.shape, i32),
            pltpu.VMEM((marks, 2 * slots.shape[1]), bf16),
            pltpu.VMEM((LANES, 2 * slots.shape[1]), bf16),
            pltpu.VMEM((marks, LANES), f32),
            pltpu.SemaphoreType.DMA((5,)),
        ],
        compiler_params=params(20),
        cost_estimate=cost(4),
        name="keep",
    )(grains, *in_hbm(slots, counts, cells, picks, alive))


def join_kernel(after_in, quant_in, below_ref, above_ref, after_ref, quant_ref, sems):
    records, width = below_ref.shape
    start = after_ref.shape[1] - 2 * width
    row8 = lax.broadcasted_iota(jnp.int32, (8, LANES), 0)
    copies = []
    for n, arrived in enumerate((below_ref, above_ref)):
        to = after_ref.at[:, pl.ds(start + n * width, width)]
        copies.append(pltpu.make_async_copy(arrived, to, sems.at[n]))
        copies[n].start()
    for n, arrived in enumerate((below_ref, above_ref)):

        def step(i, carry):
            lanes = lane_tile(i)
            to = pl.ds(pl.multiple_of(start + n * width + i * LANES, LANES), LANES)
            head = arrived[0:8, lanes]
            radius = arrived[9:10, lanes]
            volume = 4.18879 * (radius * radius * radius)
            value = jnp.where(row8 == QUANT_ROW[0], volume, volume * head)
            quant_ref[:, to] = jnp.where(row8 >= COLUMN_ROW, quant_in[:, to], value)
            return carry

        lax.fori_loop(0, width // LANES, step, 0, unroll=8)
    for copy in copies:
        copy.wait()


def join(after, quant, below, above):
    return pl.pallas_call(
        join_kernel,
        out_shape=(
            jax.ShapeDtypeStruct(after.shape, after.dtype),
            jax.ShapeDtypeStruct(quant.shape, quant.dtype),
        ),
        in_specs=[HBM, VMEM, VMEM, VMEM],
        out_specs=(HBM, VMEM),
        scratch_shapes=[pltpu.SemaphoreType.DMA((2,))],
        input_output_aliases={0: 0, 1: 1},
        compiler_params=params(16),
        cost_estimate=cost(1),
        name="join",
    )(after, quant, below, above)


def deposit_kernel(channels, rows_x, rows_y, chunk, span, begins, ends, earlier, *refs):
    refs = list(refs)
    quant_ref = refs.pop(0)
    partial_ref = None if begins else refs.pop(0)
    depth_ref = refs.pop(0) if ends else None
    del refs[:earlier]
    field_ref = refs.pop(0)
    low_ref, high_ref = (refs.pop(0), refs.pop(0)) if ends else (None, None)
    left_a, left_b, right_a, right_b, total = refs
    first, last = span
    columns = rows_x * rows_y
    depth = total.shape[1]
    count = len(channels)
    row16 = lax.broadcasted_iota(jnp.int32, (16, LANES), 0).astype(jnp.float32)
    zero = jnp.zeros((16, LANES), jnp.bfloat16)
    one = jnp.ones((16, LANES), jnp.bfloat16)
    total[...] = jnp.zeros_like(total) if begins else partial_ref[...]

    def build(left, right, step):
        for j in range(chunk // LANES):
            here = slice(j * LANES, (j + 1) * LANES)
            lanes = pl.ds(pl.multiple_of(step * chunk + j * LANES, LANES), LANES)
            parts = [wide(quant_ref[QUANT_ROW[c]:QUANT_ROW[c] + 1, lanes]) for c in channels]
            column = wide(quant_ref[COLUMN_ROW:COLUMN_ROW + 1, lanes])
            level = wide(quant_ref[LEVEL_ROW:LEVEL_ROW + 1, lanes])
            for k in range(columns // 16):
                hit = (row16 + 16.0 * k).astype(jnp.bfloat16) == column
                for c in range(count):
                    left[c * columns + 16 * k:c * columns + 16 * k + 16, here] = jnp.where(hit, parts[c], zero)
            for k in range(depth // 16):
                hit = (row16 + 16.0 * k).astype(jnp.bfloat16) == level
                right[16 * k:16 * k + 16, here] = jnp.where(hit, one, zero)

    build(left_a, right_a, first)

    def two(i, carry):
        now = first + 2 * i
        build(left_b, right_b, now + 1)
        total[...] += dot(left_a[...], right_a[...], NT)
        build(left_a, right_a, jnp.minimum(now + 2, last - 1))
        total[...] += dot(left_b[...], right_b[...], NT)
        return carry

    lax.fori_loop(0, (last - first) // 2, two, 0)
    if (last - first) % 2:
        total[...] += dot(left_a[...], right_a[...], NT)

    if not ends:
        field_ref[...] = total[...]
        return
    high, low = halves(total[...])
    field_ref[...] = dot(high, depth_ref[0]) + (dot(high, depth_ref[1]) + dot(low, depth_ref[0]))
    for c in range(count):
        for k in range(REACH):
            for y in range(rows_y):
                to = (c * REACH + k) * rows_y + y
                low_row = c * columns + y * rows_x + k
                high_row = low_row + rows_x - REACH
                low_ref[to:to + 1, :] = field_ref[low_row:low_row + 1, :]
                high_ref[to:to + 1, :] = field_ref[high_row:high_row + 1, :]


def deposit(channels, rows_x, rows_y, depth, chunk, span, quant, partial, depth_op, earlier):
    columns = rows_x * rows_y
    count = len(channels)
    begins, ends = partial is None, depth_op is not None
    field = jax.ShapeDtypeStruct((count * columns, depth), jnp.float32)
    halo = jax.ShapeDtypeStruct((count * REACH * rows_y, depth), jnp.float32)
    operands = [quant] + ([] if begins else [partial]) + ([depth_op] if ends else [])
    outs = (field, halo, halo) if ends else (field,)
    left = pltpu.VMEM((count * columns, chunk), jnp.bfloat16)
    right = pltpu.VMEM((depth, chunk), jnp.bfloat16)
    return pl.pallas_call(
        functools.partial(deposit_kernel, channels, rows_x, rows_y, chunk, span, begins, ends, len(earlier)),
        out_shape=outs,
        in_specs=[VMEM] * len(operands) + [ANY] * len(earlier),
        out_specs=(VMEM,) * len(outs),
        scratch_shapes=[left, left, right, right, pltpu.VMEM(field.shape, jnp.float32)],
        compiler_params=params(20),
        cost_estimate=cost(0.4 * count * (span[1] - span[0])),
        name="deposit",
    )(*operands, *earlier)


def mix(operator_ref, pieces):
    total = None
    start = 0
    for piece in pieces:
        take = slice(start, start + piece.shape[0])
        high, low = halves(piece)
        value = dot(operator_ref[0, :, take], high) + (
            dot(operator_ref[1, :, take], high) + dot(operator_ref[0, :, take], low)
        )
        total = value if total is None else total + value
        start += piece.shape[0]
    return total


def stream_kernel(count, own_ref, before_ref, after_ref, operator_ref, *refs):
    field_ref, low_ref, high_ref = refs[-3:]
    columns = own_ref.shape[0] // count
    halo = before_ref.shape[0] // count
    edge = low_ref.shape[0] // count
    for c in range(count):
        own = slice(c * columns, (c + 1) * columns)
        side = slice(c * halo, (c + 1) * halo)
        value = mix(operator_ref, [own_ref[own, :], jnp.concatenate([before_ref[side, :], after_ref[side, :]], axis=0)])
        field_ref[own, :] = value
        low_ref[c * edge:(c + 1) * edge, :] = value[0:edge]
        high_ref[c * edge:(c + 1) * edge, :] = value[columns - edge:columns]


def stream_pass(count, rows_x, own, before, after, operator, earlier):
    edge = jax.ShapeDtypeStruct((count * REACH * rows_x, own.shape[1]), jnp.float32)
    return pl.pallas_call(
        functools.partial(stream_kernel, count),
        out_shape=(jax.ShapeDtypeStruct(own.shape, jnp.float32), edge, edge),
        in_specs=[VMEM] * 4 + [ANY] * len(earlier),
        out_specs=(VMEM,) * 3,
        compiler_params=params(12),
        cost_estimate=cost(0.4 * count),
        name="stream_pass",
    )(own, before, after, operator, *earlier)


def span_kernel(channels, rows_q, *refs):
    refs = list(refs)
    own_ref, before_ref, after_ref, operator_ref, choose_ref, fluid_ref = refs[:6]
    base_ref = None if 0 in channels else refs[6]
    solid_ref, out_ref = refs[-2:]
    count = len(channels)
    columns = own_ref.shape[0] // count
    edge = before_ref.shape[0] // count
    choose = choose_ref[...]
    solids = {}
    for n, c in enumerate(channels):
        own = slice(n * columns, (n + 1) * columns)
        side = slice(n * edge, (n + 1) * edge)
        value = mix(operator_ref, [own_ref[own, :], jnp.concatenate([before_ref[side, :], after_ref[side, :]], axis=0)])
        solid_ref[own, :] = value
        solids[c] = value
    base = solids[0] if base_ref is None else base_ref[0:columns, :]
    for n, c in enumerate(channels):
        if c == 0:
            value = 1.0 / (1.0 + base)
        else:
            flow = fluid_ref[(c - 1) * columns:c * columns, :]
            value = flow + drag_rate * (solids[c] - base * flow)
        first, rest = halves(value)
        second, third = halves(value - first.astype(jnp.float32))
        sent = dot(choose, first) + (dot(choose, second) + dot(choose, third))
        out_ref[:, :, count - 1 - n, :] = sent.reshape(sent.shape[0] // rows_q, rows_q, -1)


def span_pass(channels, own, before, after, operator, choose, fluid, base, peers, rows_q, earlier):
    count = len(channels)
    operands = [own, before, after, operator, choose, fluid] + ([] if base is None else [base])
    return pl.pallas_call(
        functools.partial(span_kernel, channels, rows_q),
        out_shape=(
            jax.ShapeDtypeStruct(own.shape, jnp.float32),
            jax.ShapeDtypeStruct((peers, rows_q, count, own.shape[1]), jnp.float32),
        ),
        in_specs=[VMEM] * len(operands) + [ANY] * len(earlier),
        out_specs=(VMEM, VMEM),
        compiler_params=params(16),
        cost_estimate=cost(0.8 * count),
        name="span_pass",
    )(*operands, *earlier)


def shift(value, axis, steps, periodic):
    count = lax.axis_size(axis)
    pairs = [
        (source, (source + steps) % count)
        for source in range(count)
        if periodic or 0 <= source + steps < count
    ]
    return lax.ppermute(value, axis, pairs)


def per_device(grains, send_slots, send_counts, cell_index, fluid, block_slots, block_counts):
    rows_x, rows_y, depth = fluid.shape[1:]
    columns = rows_x * rows_y
    width = send_slots.shape[2]
    peers, rows_q = block_slots.shape[1:]
    total = cell_index.shape[0]
    axes = ("stream", "span")

    down, up = leave(grains, send_slots[0], send_counts)
    below = shift(down, "stream", 1, True)
    above = shift(up, "stream", -1, True)
    after, quant, depth_op, stream_op, span_op, choose = keep(
        grains, send_slots[0], send_counts, cell_index.reshape(1, -1),
        block_slots[0].T, block_counts, rows_x, rows_y, depth,
    )
    grains_after, quant = join(after, quant, below, above)

    chunk = math.gcd(total, 2048)
    steps = total // chunk
    middle = steps // 4 * 2
    flow = fluid.reshape(3 * columns, depth)

    def add(channels, span, partial, last, earlier=()):
        return deposit(
            channels, rows_x, rows_y, depth, chunk, span, quant, partial, depth_op if last else None, earlier
        )

    def stream(field, low, high, earlier):
        before = shift(high, "stream", 1, True)
        after = shift(low, "stream", -1, True)
        return stream_pass(field.shape[0] // columns, rows_x, field, before, after, stream_op, earlier)

    def span(channels, field, low, high, base, earlier):
        before = shift(high, "span", 1, False)
        after = shift(low, "span", -1, False)
        return span_pass(
            channels, field, before, after, span_op, choose, flow, base, peers, rows_q, earlier
        )

    def exchange(outgoing):
        return lax.all_to_all(outgoing, axes, split_axis=0, concat_axis=0, tiled=True)

    outer = add((0, 3), (0, steps), None, True)
    (inner,) = add((2, 1), (0, middle), None, False)
    outer = stream(*outer, (inner,))
    inner = add((2, 1), (middle, steps), inner, True, outer[:1])
    solid_outer, outgoing_outer = span((0, 3), *outer, None, inner[:1])
    arrived_outer = exchange(outgoing_outer)
    inner = stream(*inner, (outgoing_outer,))
    solid_inner, outgoing_inner = span((2, 1), *inner, solid_outer, ())
    arrived_inner = exchange(outgoing_inner)

    solid = jnp.concatenate(
        [solid_outer[:columns], solid_inner[columns:], solid_inner[:columns], solid_outer[columns:]], axis=0
    ).reshape(4, rows_x, rows_y, depth)
    received = jnp.concatenate([arrived_inner, arrived_outer], axis=2)
    return grains_after, solid, received[None]


def solution(mesh):
    return jax.shard_map(
        per_device,
        mesh=mesh,
        in_specs=(
            P(None, ("stream", "span")),
            P(("stream", "span"), None, None),
            P(("stream", "span"), None),
            P(("stream", "span")),
            P(None, "stream", "span", None),
            P(("stream", "span"), None, None),
            P(("stream", "span"), None),
        ),
        out_specs=(
            P(None, ("stream", "span")),
            P(None, "stream", "span", None),
            P(("stream", "span"), None, None, None, None),
        ),
        check_vma=False,
    )
```

time: 175 us -> 104 us (0.59)
  matrix products: 54.4 us -> 0 us
  Pallas kernels: 0 us -> 44.3 us
  local copies, waits for them, and re-layouts: 35.6 us -> 1.48 us
  blocking collectives: 33.5 us -> 0 us
  other arithmetic: 27.7 us -> 2.52 us
  starting transfers between devices: 8.99 us -> 28.6 us
  waiting for transfers between devices: 12.7 us -> 25.5 us
    dot_general x15 -> x0, matrix products: 54.4 us -> none  [the longest x14 52.5 us: add_step(): jnp.dot(left_side, pick_rest, preferred_element_type=jnp.float32)]
    pallas_call x0 -> x10, Pallas kernels: none -> 44.3 us  [the longest x3 24.1 us: deposit(): pl.pallas_call(functools.partial(deposit_kernel, channels, rows_x, rows_y...]
    all_to_all x1 -> x0, blocking collectives: 33.5 us -> none  [per_device(): lax.all_to_all(outgoing, ('stream', 'span'), split_axis=0, concat_axis=0,...]
    another operation x3 -> x0, other arithmetic: 22.5 us -> none  [the longest x1 21.9 us: per_device(): jnp.zeros((slot_count,), jnp.float32).at[slots.reshape(-1)]]
    gather x3 -> x0, local copies, waits for them, and re-layouts: 22.4 us -> none  [the longest x2 21.1 us: per_device(): leaving = grains[:, slots] * live[None]]
    all_to_all x0 -> x2, starting transfers between devices: none -> 16.2 us  [exchange(): lax.all_to_all(outgoing, axes, split_axis=0, concat_axis=0, tiled=True)]
    all_to_all x0 -> x2, waiting for transfers between devices: none -> 14.2 us  [exchange(): lax.all_to_all(outgoing, axes, split_axis=0, concat_axis=0, tiled=True)]
    unnamed x26 -> x6, local copies, waits for them, and re-layouts: 10.1 us -> 1.41 us
  transfers between devices with their start and end apart: 6 -> 12, of which waited for: 4 -> 5; matrix products, arithmetic and copies ran while one was open for 13% -> 1% of each run, Pallas kernels for 0% -> 20%
where the time goes in v2:
time: 104 us; the launch traced here: 103 us
  Pallas kernels  44.3 us (43%)
  starting transfers between devices  28.6 us (28%)
  waiting for transfers between devices  25.5 us (25%)
  other arithmetic  2.52 us (2%)
  local copies, waits for them, and re-layouts  1.48 us (1%)
    pallas_call x3, Pallas kernels, deposit(): pl.pallas_call(functools.partial(deposit_kernel, channels, rows_x, rows_y...  24.1 us
    all_to_all x2, starting transfers between devices, exchange(): lax.all_to_all(outgoing, axes, split_axis=0, concat_axis=0, tiled=True)  16.2 us
    all_to_all x2, waiting for transfers between devices, exchange(): lax.all_to_all(outgoing, axes, split_axis=0, concat_axis=0, tiled=True)  14.2 us
    ppermute x10, starting transfers between devices, shift(): return lax.ppermute(value, axis, pairs)  12.5 us
    ppermute x10, waiting for transfers between devices, shift(): return lax.ppermute(value, axis, pairs)  11.3 us
    pallas_call x1, Pallas kernels, leave(): pl.pallas_call(leave_kernel, out_shape=(out, out), in_specs=[VMEM, HBM, H...  9.18 us
    pallas_call x1, Pallas kernels, keep(): pl.pallas_call(functools.partial(keep_kernel, rows_x, rows_y, depth), out...  5.3 us
    pallas_call x2, Pallas kernels, span_pass(): pl.pallas_call(functools.partial(span_kernel, channels, rows_q), out_shap...  3.83 us
  transfers between devices with their start and end apart: 12, of which 5 were waited for; matrix products, arithmetic and copies ran while one was open for 1% of the time, Pallas kernels for 20%

profile of v2, /device:TPU:1, one launch (start us, length us, event | category | flops | bytes accessed | tf_op | source)
XLA Modules:
  0.0 103.3 jit_solution(2944708960371553965)
XLA Ops:
  0.6 1.4 %copy-done = f32[13,24576]{1,0:T(8,128)S(1)} copy-done((f32[13,24576]{1,0:T(8,128)S(1)}, f32[13,24576]{1,0:T(8,128)}, u32[]{:S(2)}) %copy-start) | copy-done | bytes 1277976
  2.0 9.2 %leave.1 = (f32[13,2048]{1,0:T(8,128)S(1)}, f32[13,2048]{1,0:T(8,128)S(1)}) custom-call(f32[13,24576]{1,0:T(8,128)S(1)} %copy-done, s32[2,2048]{1,0:T(2,128)} %bitcast.13, s32[1,2]{1,0:T(1,128)} %counts_hbm.3), custom_call_target="tpu_custom_call" | custom-call | bytes 24000000 | tf_op jit(solution)/shard_map/leave/pallas_call | solution.py:141
  11.8 5.3 %keep.1 = (f32[13,28672]{1,0:T(8,128)}, f32[8,28672]{1,0:T(8,128)S(1)}, bf16[2,256,256]{2,1,0:T(8,128)(2,1)S(1)}, bf16[2,256,304]{2,1,0:T(8,128)(2,1)S(1)}, bf16...) custom-call(f32[13,24576]{1,0:T(8,128)S(1)} %copy-done.1, s32[2,2048]{1,0:T(2,128)} %bitcast.14, ...), custom_call_target="tpu_custom_call" | custom-call | bytes 12000000 | tf_op jit(solution)/shard_map/keep/pallas_call | solution.py:300
  17.1 0.7 join.1
  17.9 11.6 %deposit.3 = (f32[512,256]{1,0:T(8,128)S(1)}, f32[48,256]{1,0:T(8,128)S(1)}, f32[48,256]{1,0:T(8,128)S(1)}) custom-call(f32[8,28672]{1,0:T(8,128)S(1)} %get-tuple-element.34.refs_0_, bf16[2,256,256]{2,1,0:T(8,128)(2,1)S(1)} %get-tuple-element.35.refs_1_.refs_2_), custom_call_target="tpu_custom_call" | custom-call | bytes 33600000 | tf_op jit(solution)/shard_map/deposit/pallas_call | solution.py:444
  29.5 1.4 %collective-permute-start.2 = (f32[48,256]{1,0:T(8,128)S(1)}, f32[48,256]{1,0:T(8,128)S(1)}, u32[]{:S(2)}, u32[]{:S(2)}) collective-permute-start(f32[48,256]{1,0:T(8,128)S(1)} %get-tuple-element.37), channel_id=1, source_target_pairs={{0,4},{4,8},{8,12},{12,16},{16,20},{20,24},{24,28},{28,0},{1,5},{5... | collective-permute-start | bytes 147464 | tf_op jit(solution)/shard_map/ppermute | solution.py:550
  31.0 5.3 %deposit.4.refs_0_.refs_1_ = f32[512,256]{1,0:T(8,128)S(1)} custom-call(f32[8,28672]{1,0:T(8,128)S(1)} %get-tuple-element.34.refs_0_), custom_call_target="tpu_custom_call" | custom-call | bytes 14400000 | tf_op jit(solution)/shard_map/deposit/pallas_call | solution.py:444
  36.9 3.4 %collective-permute-start.4 = (f32[192,256]{1,0:T(8,128)S(1)}, f32[192,256]{1,0:T(8,128)S(1)}, u32[]{:S(2)}, u32[]{:S(2)}) collective-permute-start(f32[192,256]{1,0:T(8,128)S(1)} %get-tuple-element.41), channel_id=1, source_target_pairs={{0,1},{1,2},{2,3},{4,5},{5,6},{6,7},{8,9},{9,10},{10,11},{12,13},{... | collective-permute-start | bytes 589832 | tf_op jit(solution)/shard_map/ppermute | solution.py:550
  40.3 1.3 %collective-permute-start.5 = (f32[192,256]{1,0:T(8,128)S(1)}, f32[192,256]{1,0:T(8,128)S(1)}, u32[]{:S(2)}, u32[]{:S(2)}) collective-permute-start(f32[192,256]{1,0:T(8,128)S(1)} %get-tuple-element.42), channel_id=1, source_target_pairs={{1,0},{2,1},{3,2},{5,4},{6,5},{7,6},{9,8},{10,9},{11,10},{13,12},{... | collective-permute-start | bytes 589832 | tf_op jit(solution)/shard_map/ppermute | solution.py:550
  41.6 7.2 %deposit.5 = (f32[512,256]{1,0:T(8,128)S(1)}, f32[48,256]{1,0:T(8,128)S(1)}, f32[48,256]{1,0:T(8,128)S(1)}) custom-call(f32[8,28672]{1,0:T(8,128)S(1)} %get-tuple-element.34.refs_0_, f32[512,256]{1,0:T(8,128)S(1)} %deposit.4.refs_0_.refs_1_, bf16[2,256,256]{2,1,0:T(8,128)(2,1)S(1)} %get-tuple-element.35.refs_1_.refs_2_, ...), custom_call_target="tpu_custom_call" | custom-call | bytes 19200000 | tf_op jit(solution)/shard_map/deposit/pallas_call | solution.py:444
  48.8 1.9 %span_pass.2 = (f32[512,256]{1,0:T(8,128)S(1)}, f32[32,8,2,256]{3,2,1,0:T(2,128)}) custom-call(f32[512,256]{1,0:T(8,128)S(1)} %get-tuple-element.40.refs_3_.refs_0_, f32[192,256]{1,0:T(8,128)S(1)} %collective-permute-done.4.refs_1_, f32[192,256]{1,0:T(8,128)S(1)} %collective-permute-done.5.refs_2_, bf16[2,256,448]{2,1,0:T(8,128)(2,1)S(1)} %get-tuple-element.43.refs_3_, ...), custom_call_target="tpu_custom_call" | custom-call | bytes 4800000 | tf_op jit(solution)/shard_map/span_pass/pallas_call | solution.py:529
  50.7 9.1 %all-to-all-start.1 = ((f32[32,8,2,256]{3,2,1,0:T(2,128)}), f32[32,8,2,256]{3,2,1,0:T(2,128)S(1)}, u32[]{:S(2)}, u32[]{:S(2)}) async-start(f32[32,8,2,256]{3,2,1,0:T(2,128)} %get-tuple-element.49.refs_0_), calls=%async_computation.1 | async-start | bytes 1048576 | tf_op jit(solution)/shard_map/all_to_all | solution.py:593
  59.9 1.7 %collective-permute-start.6 = (f32[48,256]{1,0:T(8,128)S(1)}, f32[48,256]{1,0:T(8,128)S(1)}, u32[]{:S(2)}, u32[]{:S(2)}) collective-permute-start(f32[48,256]{1,0:T(8,128)S(1)} %get-tuple-element.47), channel_id=1, source_target_pairs={{0,4},{4,8},{8,12},{12,16},{16,20},{20,24},{24,28},{28,0},{1,5},{5... | collective-permute-start | bytes 147464 | tf_op jit(solution)/shard_map/ppermute | solution.py:550
  61.6 1.4 %collective-permute-done.6.before_ref = f32[48,256]{1,0:T(8,128)S(1)} collective-permute-done((f32[48,256]{1,0:T(8,128)S(1)}, f32[48,256]{1,0:T(8,128)S(1)}, u32[]{:S(2)}, u32[]{:S(2)}) %collective-permute-start.6) | collective-permute-done | bytes 49184 | tf_op jit(solution)/shard_map/ppermute | solution.py:550
  63.0 3.9 %collective-permute-done.7.after_ref = f32[48,256]{1,0:T(8,128)S(1)} collective-permute-done((f32[48,256]{1,0:T(8,128)S(1)}, f32[48,256]{1,0:T(8,128)S(1)}, u32[]{:S(2)}, u32[]{:S(2)}) %collective-permute-start.7) | collective-permute-done | bytes 49184 | tf_op jit(solution)/shard_map/ppermute | solution.py:550
  67.4 2.7 %collective-permute-start.8 = (f32[192,256]{1,0:T(8,128)S(1)}, f32[192,256]{1,0:T(8,128)S(1)}, u32[]{:S(2)}, u32[]{:S(2)}) collective-permute-start(f32[192,256]{1,0:T(8,128)S(1)} %get-tuple-element.51), channel_id=1, source_target_pairs={{0,1},{1,2},{2,3},{4,5},{5,6},{6,7},{8,9},{9,10},{10,11},{12,13},{... | collective-permute-start | bytes 589832 | tf_op jit(solution)/shard_map/ppermute | solution.py:550
  70.2 1.3 %collective-permute-start.9 = (f32[192,256]{1,0:T(8,128)S(1)}, f32[192,256]{1,0:T(8,128)S(1)}, u32[]{:S(2)}, u32[]{:S(2)}) collective-permute-start(f32[192,256]{1,0:T(8,128)S(1)} %get-tuple-element.52), channel_id=1, source_target_pairs={{1,0},{2,1},{3,2},{5,4},{6,5},{7,6},{9,8},{10,9},{11,10},{13,12},{... | collective-permute-start | bytes 589832 | tf_op jit(solution)/shard_map/ppermute | solution.py:550
  71.5 2.2 %collective-permute-done.8.refs_1_ = f32[192,256]{1,0:T(8,128)S(1)} collective-permute-done((f32[192,256]{1,0:T(8,128)S(1)}, f32[192,256]{1,0:T(8,128)S(1)}, u32[]{:S(2)}, u32[]{:S(2)}) %collective-permute-start.8) | collective-permute-done | bytes 196640 | tf_op jit(solution)/shard_map/ppermute | solution.py:550
  73.7 3.8 %collective-permute-done.9.refs_2_ = f32[192,256]{1,0:T(8,128)S(1)} collective-permute-done((f32[192,256]{1,0:T(8,128)S(1)}, f32[192,256]{1,0:T(8,128)S(1)}, u32[]{:S(2)}, u32[]{:S(2)}) %collective-permute-start.9) | collective-permute-done | bytes 196640 | tf_op jit(solution)/shard_map/ppermute | solution.py:550
  77.5 1.9 %span_pass.3 = (f32[512,256]{1,0:T(8,128)S(1)}, f32[32,8,2,256]{3,2,1,0:T(2,128)}) custom-call(f32[512,256]{1,0:T(8,128)S(1)} %get-tuple-element.50.refs_0_, f32[192,256]{1,0:T(8,128)S(1)} %collective-permute-done.8.refs_1_, f32[192,256]{1,0:T(8,128)S(1)} %collective-permute-done.9.refs_2_, bf16[2,256,448]{2,1,0:T(8,128)(2,1)S(1)} %get-tuple-element.43.refs_3_, ...), custom_call_target="tpu_custom_call" | custom-call | bytes 4800000 | tf_op jit(solution)/shard_map/span_pass/pallas_call | solution.py:529
  79.5 7.0 %all-to-all-start = ((f32[32,8,2,256]{3,2,1,0:T(2,128)}), f32[32,8,2,256]{3,2,1,0:T(2,128)S(1)}, u32[]{:S(2)}, u32[]{:S(2)}) async-start(f32[32,8,2,256]{3,2,1,0:T(2,128)} %get-tuple-element.54), calls=%async_computation | async-start | bytes 1048576 | tf_op jit(solution)/shard_map/all_to_all | solution.py:593
  86.6 1.0 %pad_maximum_fusion = f32[1024,256]{1,0:T(8,128)} fusion(f32[256,256]{1,0:T(8,128)S(1)} %get-tuple-element.56, f32[256,256]{1,0:T(8,128)S(1)} %get-tuple-element.58, f32[256,256]{1,0:T(8,128)S(1)} %get-tuple-element.57, f32[256,256]{1,0:T(8,128)S(1)} %get-tuple-element.55), kind=kLoop, calls=%fused_computation | loop fusion | flops 786432 | bytes 2097152 | tf_op jit(solution)/shard_map/concatenate | solution.py:605
  87.6 14.2 %all-to-all-done = f32[32,8,2,256]{3,2,1,0:T(2,128)S(1)} async-done(((f32[32,8,2,256]{3,2,1,0:T(2,128)}), f32[32,8,2,256]{3,2,1,0:T(2,128)S(1)}, u32[]{:S(2)}, u32[]{:S(2)}) %all-to-all-start) | async-done | bytes 524320 | tf_op jit(solution)/shard_map/all_to_all | solution.py:593
  101.8 1.5 %maximum_bitcast_fusion = f32[1,32,8,4,256]{4,3,2,1,0:T(4,128)} fusion(f32[32,8,2,256]{3,2,1,0:T(2,128)S(1)} %all-to-all-done.1, f32[32,8,2,256]{3,2,1,0:T(2,128)S(1)} %all-to-all-done), kind=kLoop, calls=%fused_computation.1 | loop fusion | flops 262144 | bytes 2097152 | tf_op jit(solution)/shard_map/broadcast_in_dim | solution.py:609
  (20 shorter events, 2.0 us)
Async XLA Ops:
  0.6 1.4 %copy-start = (f32[13,24576]{1,0:T(8,128)S(1)}, f32[13,24576]{1,0:T(8,128)}, u32[]{:S(2)}) copy-start(f32[13,24576]{1,0:T(8,128)} %grains_ref.3) | copy-start | bytes 3833860
  2.0 9.8 %copy-start.1 = (f32[13,24576]{1,0:T(8,128)S(1)}, f32[13,24576]{1,0:T(8,128)}, u32[]{:S(2)}) copy-start(f32[13,24576]{1,0:T(8,128)} %grains_ref.3) | copy-start | bytes 3833860
  11.2 5.9 %collective-permute-start = (f32[13,2048]{1,0:T(8,128)S(1)}, f32[13,2048]{1,0:T(8,128)S(1)}, u32[]{:S(2)}, u32[]{:S(2)}) collective-permute-start(f32[13,2048]{1,0:T(8,128)S(1)} %get-tuple-element.31), channel_id=1, source_target_pairs={{0,4},{4,8},{8,12},{12,16},{16,20},{20,24},{24,28},{28,0},{1,5},{5... | collective-permute-start | bytes 319496 | tf_op jit(solution)/shard_map/ppermute | solution.py:550
  11.3 5.8 %collective-permute-start.1 = (f32[13,2048]{1,0:T(8,128)S(1)}, f32[13,2048]{1,0:T(8,128)S(1)}, u32[]{:S(2)}, u32[]{:S(2)}) collective-permute-start(f32[13,2048]{1,0:T(8,128)S(1)} %get-tuple-element.32), channel_id=1, source_target_pairs={{0,28},{4,0},{8,4},{12,8},{16,12},{20,16},{24,20},{28,24},{1,29},{... | collective-permute-start | bytes 319496 | tf_op jit(solution)/shard_map/ppermute | solution.py:550
  29.5 6.8 %collective-permute-start.2 = (f32[48,256]{1,0:T(8,128)S(1)}, f32[48,256]{1,0:T(8,128)S(1)}, u32[]{:S(2)}, u32[]{:S(2)}) collective-permute-start(f32[48,256]{1,0:T(8,128)S(1)} %get-tuple-element.37), channel_id=1, source_target_pairs={{0,4},{4,8},{8,12},{12,16},{16,20},{20,24},{24,28},{28,0},{1,5},{5... | collective-permute-start | bytes 147464 | tf_op jit(solution)/shard_map/ppermute | solution.py:550
  30.8 5.5 %collective-permute-start.3 = (f32[48,256]{1,0:T(8,128)S(1)}, f32[48,256]{1,0:T(8,128)S(1)}, u32[]{:S(2)}, u32[]{:S(2)}) collective-permute-start(f32[48,256]{1,0:T(8,128)S(1)} %get-tuple-element.38), channel_id=1, source_target_pairs={{0,28},{4,0},{8,4},{12,8},{16,12},{20,16},{24,20},{28,24},{1,29},{... | collective-permute-start | bytes 147464 | tf_op jit(solution)/shard_map/ppermute | solution.py:550
  36.3 12.5 %copy-start.2 = (f32[3,32,8,256]{3,2,1,0:T(8,128)S(1)}, f32[3,32,8,256]{3,2,1,0:T(8,128)}, u32[]{:S(2)}) copy-start(f32[3,32,8,256]{3,2,1,0:T(8,128)} %param.11) | copy-start | bytes 2359300
  36.9 11.9 %collective-permute-start.4 = (f32[192,256]{1,0:T(8,128)S(1)}, f32[192,256]{1,0:T(8,128)S(1)}, u32[]{:S(2)}, u32[]{:S(2)}) collective-permute-start(f32[192,256]{1,0:T(8,128)S(1)} %get-tuple-element.41), channel_id=1, source_target_pairs={{0,1},{1,2},{2,3},{4,5},{5,6},{6,7},{8,9},{9,10},{10,11},{12,13},{... | collective-permute-start | bytes 589832 | tf_op jit(solution)/shard_map/ppermute | solution.py:550
  40.3 8.5 %collective-permute-start.5 = (f32[192,256]{1,0:T(8,128)S(1)}, f32[192,256]{1,0:T(8,128)S(1)}, u32[]{:S(2)}, u32[]{:S(2)}) collective-permute-start(f32[192,256]{1,0:T(8,128)S(1)} %get-tuple-element.42), channel_id=1, source_target_pairs={{1,0},{2,1},{3,2},{5,4},{6,5},{7,6},{9,8},{10,9},{11,10},{13,12},{... | collective-permute-start | bytes 589832 | tf_op jit(solution)/shard_map/ppermute | solution.py:550
  50.7 28.7 %all-to-all-start.1 = ((f32[32,8,2,256]{3,2,1,0:T(2,128)}), f32[32,8,2,256]{3,2,1,0:T(2,128)S(1)}, u32[]{:S(2)}, u32[]{:S(2)}) async-start(f32[32,8,2,256]{3,2,1,0:T(2,128)} %get-tuple-element.49.refs_0_), calls=%async_computation.1 | async-start | bytes 1048576 | tf_op jit(solution)/shard_map/all_to_all | solution.py:593
  59.9 3.1 %collective-permute-start.6 = (f32[48,256]{1,0:T(8,128)S(1)}, f32[48,256]{1,0:T(8,128)S(1)}, u32[]{:S(2)}, u32[]{:S(2)}) collective-permute-start(f32[48,256]{1,0:T(8,128)S(1)} %get-tuple-element.47), channel_id=1, source_target_pairs={{0,4},{4,8},{8,12},{12,16},{16,20},{20,24},{24,28},{28,0},{1,5},{5... | collective-permute-start | bytes 147464 | tf_op jit(solution)/shard_map/ppermute | solution.py:550
  61.6 5.3 %collective-permute-start.7 = (f32[48,256]{1,0:T(8,128)S(1)}, f32[48,256]{1,0:T(8,128)S(1)}, u32[]{:S(2)}, u32[]{:S(2)}) collective-permute-start(f32[48,256]{1,0:T(8,128)S(1)} %get-tuple-element.48), channel_id=1, source_target_pairs={{0,28},{4,0},{8,4},{12,8},{16,12},{20,16},{24,20},{28,24},{1,29},{... | collective-permute-start | bytes 147464 | tf_op jit(solution)/shard_map/ppermute | solution.py:550
  67.4 6.3 %collective-permute-start.8 = (f32[192,256]{1,0:T(8,128)S(1)}, f32[192,256]{1,0:T(8,128)S(1)}, u32[]{:S(2)}, u32[]{:S(2)}) collective-permute-start(f32[192,256]{1,0:T(8,128)S(1)} %get-tuple-element.51), channel_id=1, source_target_pairs={{0,1},{1,2},{2,3},{4,5},{5,6},{6,7},{8,9},{9,10},{10,11},{12,13},{... | collective-permute-start | bytes 589832 | tf_op jit(solution)/shard_map/ppermute | solution.py:550
  70.2 7.3 %collective-permute-start.9 = (f32[192,256]{1,0:T(8,128)S(1)}, f32[192,256]{1,0:T(8,128)S(1)}, u32[]{:S(2)}, u32[]{:S(2)}) collective-permute-start(f32[192,256]{1,0:T(8,128)S(1)} %get-tuple-element.52), channel_id=1, source_target_pairs={{1,0},{2,1},{3,2},{5,4},{6,5},{7,6},{9,8},{10,9},{11,10},{13,12},{... | collective-permute-start | bytes 589832 | tf_op jit(solution)/shard_map/ppermute | solution.py:550
  79.5 22.3 %all-to-all-start = ((f32[32,8,2,256]{3,2,1,0:T(2,128)}), f32[32,8,2,256]{3,2,1,0:T(2,128)S(1)}, u32[]{:S(2)}, u32[]{:S(2)}) async-start(f32[32,8,2,256]{3,2,1,0:T(2,128)} %get-tuple-element.54), calls=%async_computation | async-start | bytes 1048576 | tf_op jit(solution)/shard_map/all_to_all | solution.py:593

commit v3 on v2

--- a/solution.py
+++ b/solution.py
@@ -69,20 +69,28 @@
     return tuple(pltpu.with_memory_space_constraint(value, pltpu.HBM) for value in values)
 
 
+def is_odd(axis):
+    return lax.rem(lax.axis_index(axis), 2)
+
+
 def leave_kernel(
-    grains_ref, slots_hbm, counts_hbm, down_ref, up_ref, stage, table, picked, slots_v, slots_s, counts_s, sems
+    rows_x, rows_y, grains_hbm, slots_hbm, counts_hbm, first_ref, second_ref, depth_ref, stream_ref, span_ref,
+    grains_ref, stage, table, picked, slots_v, slots_s, counts_s, sems,
 ):
     records, slot_count = grains_ref.shape
-    width = down_ref.shape[1]
+    width = first_ref.shape[1]
     rows = table.shape[0]
-    parts = slot_count // rows if slot_count % rows == 0 else slot_count // rows + 1
+    parts = -(-slot_count // rows)
+    sources = (grains_hbm, slots_hbm, slots_hbm, counts_hbm)
+    targets = (grains_ref, slots_v, slots_s, counts_s)
     copies = [
-        pltpu.make_async_copy(slots_hbm, slots_v, sems.at[0]),
-        pltpu.make_async_copy(slots_hbm, slots_s, sems.at[1]),
-        pltpu.make_async_copy(counts_hbm, counts_s, sems.at[2]),
+        pltpu.make_async_copy(source, target, sems.at[i])
+        for i, (source, target) in enumerate(zip(sources, targets))
     ]
     for copy in copies:
         copy.start()
+    build_operators(rows_x, rows_y, depth_ref, stream_ref, span_ref)
+    copies[0].wait()
 
     for part in range(parts):
         size = min(rows, slot_count - part * rows)
@@ -92,12 +100,13 @@
     for block in range(rows // LANES):
         here = slice(block * LANES, (block + 1) * LANES)
         table[here, :] = jnp.transpose(stage[:, here])
-    for copy in copies:
+    for copy in copies[1:]:
         copy.wait()
 
     run = picked.shape[0]
     lane = lax.broadcasted_iota(jnp.int32, (8, LANES), 1)
-    for which, out_ref in ((0, down_ref), (1, up_ref)):
+    odd = is_odd("stream")
+    for which, out_ref in ((odd, first_ref), (1 - odd, second_ref)):
         live_count = counts_s[0, which]
 
         def gather(i, carry):
@@ -108,7 +117,8 @@
             for piece in range(run // LANES):
                 lanes = pl.ds(pl.multiple_of(base + piece * LANES, LANES), LANES)
                 turned = jnp.transpose(picked[piece * LANES:(piece + 1) * LANES, :])
-                slot = jnp.broadcast_to(slots_v[which:which + 1, lanes], (8, LANES))
+                slot = jnp.where(which == 0, slots_v[0:1, lanes], slots_v[1:2, lanes])
+                slot = jnp.broadcast_to(slot, (8, LANES))
                 part_of = lax.shift_right_logical(slot, rows.bit_length() - 1)
                 live = lane + (base + piece * LANES) < live_count
                 first = jnp.zeros((8, LANES), jnp.float32)
@@ -132,30 +142,39 @@
         lax.fori_loop(used, width // run, blank, 0)
 
 
-def leave(grains, slots, counts):
+def leave(grains, slots, counts, rows_x, rows_y, depth):
     records, slot_count = grains.shape
     width = slots.shape[1]
+    columns = rows_x * rows_y
     rows = max(LANES, 1 << (-(-slot_count // 8) - 1).bit_length())
     run = 2 * LANES if width % (2 * LANES) == 0 else LANES
     out = jax.ShapeDtypeStruct((records, width), jnp.float32)
+    bf16 = jnp.bfloat16
     return pl.pallas_call(
-        leave_kernel,
-        out_shape=(out, out),
-        in_specs=[VMEM, HBM, HBM],
-        out_specs=(VMEM, VMEM),
+        functools.partial(leave_kernel, rows_x, rows_y),
+        out_shape=(
+            out,
+            out,
+            jax.ShapeDtypeStruct((2, depth, depth), bf16),
+            jax.ShapeDtypeStruct((2, columns, columns + 2 * REACH * rows_y), bf16),
+            jax.ShapeDtypeStruct((2, columns, columns + 2 * REACH * rows_x), bf16),
+        ),
+        in_specs=[HBM] * 3,
+        out_specs=(VMEM,) * 5,
         scratch_shapes=[
+            pltpu.VMEM(grains.shape, jnp.float32),
             pltpu.VMEM((LANES, rows), jnp.float32),
             pltpu.VMEM((rows, LANES), jnp.float32),
             pltpu.VMEM((run, LANES), jnp.float32),
             pltpu.VMEM(slots.shape, jnp.int32),
             pltpu.SMEM(slots.shape, jnp.int32),
             pltpu.SMEM(counts.shape, jnp.int32),
-            pltpu.SemaphoreType.DMA((3,)),
+            pltpu.SemaphoreType.DMA((4,)),
         ],
         compiler_params=params(16),
         cost_estimate=cost(8),
         name="leave",
-    )(grains, *in_hbm(slots, counts))
+    )(*in_hbm(grains, slots, counts))
 
 
 def weights_at(apart):
@@ -174,25 +193,9 @@
     out_ref[1, :, start:stop] = low
 
 
-def keep_kernel(
-    rows_x, rows_y, depth, grains_ref, slots_hbm, counts_hbm, cells_hbm, picks_hbm, alive_hbm,
-    after_ref, quant_ref, depth_ref, stream_ref, span_ref, choose_ref,
-    slots_v, counts_s, cells_v, picks_v, alive_v, high_rows, low_rows, gone, sems,
-):
-    records, slot_count = grains_ref.shape
-    total = after_ref.shape[1]
-    width = slots_v.shape[1]
-    tiles = slot_count // LANES
+def build_operators(rows_x, rows_y, depth_ref, stream_ref, span_ref):
     columns = rows_x * rows_y
-    sources = (slots_hbm, counts_hbm, cells_hbm, picks_hbm, alive_hbm)
-    targets = (slots_v, counts_s, cells_v, picks_v, alive_v)
-    copies = [
-        pltpu.make_async_copy(source, target, sems.at[i])
-        for i, (source, target) in enumerate(zip(sources, targets))
-    ]
-    for copy in copies:
-        copy.start()
-
+    depth = depth_ref.shape[1]
     target = lax.broadcasted_iota(jnp.int32, (depth, depth), 0)
     source = lax.broadcasted_iota(jnp.int32, (depth, depth), 1)
     put_operator(depth_ref, 0, weights_at(target - source))
@@ -215,6 +218,27 @@
     row, source_x = split(lax.broadcasted_iota(jnp.int32, side, 1), rows_x)
     source_y = jnp.where(row < REACH, row - REACH, row - REACH + rows_y)
     put_operator(span_ref, columns, jnp.where(target_x == source_x, weights_at(target_y - source_y), 0.0))
+
+
+def keep_kernel(
+    rows_x, rows_y, depth, grains_ref, slots_hbm, counts_hbm, cells_hbm, picks_hbm, alive_hbm,
+    after_hbm, quant_ref, choose_ref,
+    slots_v, counts_s, cells_v, picks_v, alive_v, high_rows, low_rows, gone, kept, sems,
+):
+    records, slot_count = grains_ref.shape
+    total = quant_ref.shape[1]
+    width = slots_v.shape[1]
+    tiles = slot_count // LANES
+    columns = rows_x * rows_y
+    pieces = 4
+    sources = (slots_hbm, counts_hbm, cells_hbm, picks_hbm, alive_hbm)
+    targets = (slots_v, counts_s, cells_v, picks_v, alive_v)
+    copies = [
+        pltpu.make_async_copy(source, target, sems.at[i])
+        for i, (source, target) in enumerate(zip(sources, targets))
+    ]
+    for copy in copies:
+        copy.start()
 
     for copy in copies:
         copy.wait()
@@ -270,8 +294,8 @@
         stay = 1.0 - gone[pl.ds(i, 1), :]
         head = grains_ref[0:8, lanes] * stay
         rest = grains_ref[8:records, lanes] * stay
-        after_ref[0:8, lanes] = head
-        after_ref[8:records, lanes] = rest
+        kept[0:8, lanes] = head
+        kept[8:records, lanes] = rest
         radius = rest[1:2]
         volume = 4.18879 * (radius * radius * radius)
         col, lev = place(cells_v[:, lanes])
@@ -280,7 +304,14 @@
         quant_ref[:, lanes] = jnp.where(row8 == LEVEL_ROW, lev, value)
         return carry
 
-    lax.fori_loop(0, tiles, keep, 0, unroll=8)
+    writes = []
+    for n in range(pieces):
+        first = tiles * n // pieces
+        last = tiles * (n + 1) // pieces
+        lax.fori_loop(first, last, keep, 0, unroll=8)
+        here = pl.ds(first * LANES, (last - first) * LANES)
+        writes.append(pltpu.make_async_copy(kept.at[:, here], after_hbm.at[:, here], sems.at[len(copies) + n]))
+        writes[n].start()
 
     def arrivals(i, carry):
         lanes = lane_tile(i)
@@ -289,6 +320,8 @@
         return carry
 
     lax.fori_loop(tiles, total // LANES, arrivals, 0, unroll=8)
+    for write in writes:
+        write.wait()
 
 
 def keep(grains, slots, counts, cells, picks, alive, rows_x, rows_y, depth):
@@ -302,13 +335,10 @@
         out_shape=(
             jax.ShapeDtypeStruct((records, total), f32),
             jax.ShapeDtypeStruct((8, total), f32),
-            jax.ShapeDtypeStruct((2, depth, depth), bf16),
-            jax.ShapeDtypeStruct((2, columns, columns + 2 * REACH * rows_y), bf16),
-            jax.ShapeDtypeStruct((2, columns, columns + 2 * REACH * rows_x), bf16),
             jax.ShapeDtypeStruct((picks.size, columns), bf16),
         ),
         in_specs=[VMEM] + [HBM] * 5,
-        out_specs=(VMEM,) * 6,
+        out_specs=(HBM, VMEM, VMEM),
         scratch_shapes=[
             pltpu.VMEM(slots.shape, i32),
             pltpu.SMEM(counts.shape, i32),
@@ -318,7 +348,8 @@
             pltpu.VMEM((marks, 2 * slots.shape[1]), bf16),
             pltpu.VMEM((LANES, 2 * slots.shape[1]), bf16),
             pltpu.VMEM((marks, LANES), f32),
-            pltpu.SemaphoreType.DMA((5,)),
+            pltpu.VMEM(grains.shape, f32),
+            pltpu.SemaphoreType.DMA((9,)),
         ],
         compiler_params=params(20),
         cost_estimate=cost(4),
@@ -326,20 +357,23 @@
     )(grains, *in_hbm(slots, counts, cells, picks, alive))
 
 
-def join_kernel(after_in, quant_in, below_ref, above_ref, after_ref, quant_ref, sems):
-    records, width = below_ref.shape
+def join_kernel(after_in, quant_in, first_ref, second_ref, after_ref, quant_ref, sems):
+    records, width = first_ref.shape
     start = after_ref.shape[1] - 2 * width
     row8 = lax.broadcasted_iota(jnp.int32, (8, LANES), 0)
+    odd = is_odd("stream")
     copies = []
-    for n, arrived in enumerate((below_ref, above_ref)):
-        to = after_ref.at[:, pl.ds(start + n * width, width)]
+    for n, arrived in enumerate((first_ref, second_ref)):
+        place = pl.multiple_of(start + (1 - odd if n == 0 else odd) * width, LANES)
+        to = after_ref.at[:, pl.ds(place, width)]
         copies.append(pltpu.make_async_copy(arrived, to, sems.at[n]))
         copies[n].start()
-    for n, arrived in enumerate((below_ref, above_ref)):
+    for n, arrived in enumerate((first_ref, second_ref)):
 
         def step(i, carry):
             lanes = lane_tile(i)
-            to = pl.ds(pl.multiple_of(start + n * width + i * LANES, LANES), LANES)
+            place = start + (1 - odd if n == 0 else odd) * width
+            to = pl.ds(pl.multiple_of(place + i * LANES, LANES), LANES)
             head = arrived[0:8, lanes]
             radius = arrived[9:10, lanes]
             volume = 4.18879 * (radius * radius * radius)
@@ -352,7 +386,7 @@
         copy.wait()
 
 
-def join(after, quant, below, above):
+def join(after, quant, first, second):
     return pl.pallas_call(
         join_kernel,
         out_shape=(
@@ -366,7 +400,7 @@
         compiler_params=params(16),
         cost_estimate=cost(1),
         name="join",
-    )(after, quant, below, above)
+    )(*in_hbm(after), quant, first, second)
 
 
 def deposit_kernel(channels, rows_x, rows_y, chunk, span, begins, ends, earlier, *refs):
@@ -376,9 +410,9 @@
     depth_ref = refs.pop(0) if ends else None
     del refs[:earlier]
     field_ref = refs.pop(0)
-    low_ref, high_ref = (refs.pop(0), refs.pop(0)) if ends else (None, None)
+    first_ref, second_ref = (refs.pop(0), refs.pop(0)) if ends else (None, None)
     left_a, left_b, right_a, right_b, total = refs
-    first, last = span
+    begin, end = span
     columns = rows_x * rows_y
     depth = total.shape[1]
     count = len(channels)
@@ -402,18 +436,18 @@
                 hit = (row16 + 16.0 * k).astype(jnp.bfloat16) == level
                 right[16 * k:16 * k + 16, here] = jnp.where(hit, one, zero)
 
-    build(left_a, right_a, first)
+    build(left_a, right_a, begin)
 
     def two(i, carry):
-        now = first + 2 * i
+        now = begin + 2 * i
         build(left_b, right_b, now + 1)
         total[...] += dot(left_a[...], right_a[...], NT)
-        build(left_a, right_a, jnp.minimum(now + 2, last - 1))
+        build(left_a, right_a, jnp.minimum(now + 2, end - 1))
         total[...] += dot(left_b[...], right_b[...], NT)
         return carry
 
-    lax.fori_loop(0, (last - first) // 2, two, 0)
-    if (last - first) % 2:
+    lax.fori_loop(0, (end - begin) // 2, two, 0)
+    if (end - begin) % 2:
         total[...] += dot(left_a[...], right_a[...], NT)
 
     if not ends:
@@ -421,14 +455,16 @@
         return
     high, low = halves(total[...])
     field_ref[...] = dot(high, depth_ref[0]) + (dot(high, depth_ref[1]) + dot(low, depth_ref[0]))
+    odd = is_odd("stream")
+    first_x = (1 - odd) * (rows_x - REACH)
+    second_x = odd * (rows_x - REACH)
     for c in range(count):
         for k in range(REACH):
             for y in range(rows_y):
                 to = (c * REACH + k) * rows_y + y
-                low_row = c * columns + y * rows_x + k
-                high_row = low_row + rows_x - REACH
-                low_ref[to:to + 1, :] = field_ref[low_row:low_row + 1, :]
-                high_ref[to:to + 1, :] = field_ref[high_row:high_row + 1, :]
+                row = c * columns + y * rows_x + k
+                first_ref[to:to + 1, :] = field_ref[pl.ds(row + first_x, 1), :]
+                second_ref[to:to + 1, :] = field_ref[pl.ds(row + second_x, 1), :]
 
 
 def deposit(channels, rows_x, rows_y, depth, chunk, span, quant, partial, depth_op, earlier):
@@ -467,21 +503,28 @@
     return total
 
 
-def stream_kernel(count, own_ref, before_ref, after_ref, operator_ref, *refs):
-    field_ref, low_ref, high_ref = refs[-3:]
+def sides(axis, first, second):
+    odd = is_odd(axis) == 1
+    return jnp.concatenate([jnp.where(odd, first, second), jnp.where(odd, second, first)], axis=0)
+
+
+def stream_kernel(count, own_ref, first_in, second_in, operator_ref, *refs):
+    field_ref, first_ref, second_ref = refs[-3:]
     columns = own_ref.shape[0] // count
-    halo = before_ref.shape[0] // count
-    edge = low_ref.shape[0] // count
+    halo = first_in.shape[0] // count
+    edge = first_ref.shape[0] // count
+    odd = is_odd("span") == 1
     for c in range(count):
         own = slice(c * columns, (c + 1) * columns)
         side = slice(c * halo, (c + 1) * halo)
-        value = mix(operator_ref, [own_ref[own, :], jnp.concatenate([before_ref[side, :], after_ref[side, :]], axis=0)])
+        value = mix(operator_ref, [own_ref[own, :], sides("stream", first_in[side, :], second_in[side, :])])
         field_ref[own, :] = value
-        low_ref[c * edge:(c + 1) * edge, :] = value[0:edge]
-        high_ref[c * edge:(c + 1) * edge, :] = value[columns - edge:columns]
-
-
-def stream_pass(count, rows_x, own, before, after, operator, earlier):
+        low, high = value[0:edge], value[columns - edge:columns]
+        first_ref[c * edge:(c + 1) * edge, :] = jnp.where(odd, low, high)
+        second_ref[c * edge:(c + 1) * edge, :] = jnp.where(odd, high, low)
+
+
+def stream_pass(count, rows_x, own, first, second, operator, earlier):
     edge = jax.ShapeDtypeStruct((count * REACH * rows_x, own.shape[1]), jnp.float32)
     return pl.pallas_call(
         functools.partial(stream_kernel, count),
@@ -491,23 +534,23 @@
         compiler_params=params(12),
         cost_estimate=cost(0.4 * count),
         name="stream_pass",
-    )(own, before, after, operator, *earlier)
+    )(own, first, second, operator, *earlier)
 
 
 def span_kernel(channels, rows_q, *refs):
     refs = list(refs)
-    own_ref, before_ref, after_ref, operator_ref, choose_ref, fluid_ref = refs[:6]
+    own_ref, first_in, second_in, operator_ref, choose_ref, fluid_ref = refs[:6]
     base_ref = None if 0 in channels else refs[6]
     solid_ref, out_ref = refs[-2:]
     count = len(channels)
     columns = own_ref.shape[0] // count
-    edge = before_ref.shape[0] // count
+    edge = first_in.shape[0] // count
     choose = choose_ref[...]
     solids = {}
     for n, c in enumerate(channels):
         own = slice(n * columns, (n + 1) * columns)
         side = slice(n * edge, (n + 1) * edge)
-        value = mix(operator_ref, [own_ref[own, :], jnp.concatenate([before_ref[side, :], after_ref[side, :]], axis=0)])
+        value = mix(operator_ref, [own_ref[own, :], sides("span", first_in[side, :], second_in[side, :])])
         solid_ref[own, :] = value
         solids[c] = value
     base = solids[0] if base_ref is None else base_ref[0:columns, :]
@@ -523,9 +566,9 @@
         out_ref[:, :, count - 1 - n, :] = sent.reshape(sent.shape[0] // rows_q, rows_q, -1)
 
 
-def span_pass(channels, own, before, after, operator, choose, fluid, base, peers, rows_q, earlier):
+def span_pass(channels, own, first, second, operator, choose, fluid, base, peers, rows_q, earlier):
     count = len(channels)
-    operands = [own, before, after, operator, choose, fluid] + ([] if base is None else [base])
+    operands = [own, first, second, operator, choose, fluid] + ([] if base is None else [base])
     return pl.pallas_call(
         functools.partial(span_kernel, channels, rows_q),
         out_shape=(
@@ -540,14 +583,14 @@
     )(*operands, *earlier)
 
 
-def shift(value, axis, steps, periodic):
+def swap(first, second, axis, periodic):
     count = lax.axis_size(axis)
-    pairs = [
-        (source, (source + steps) % count)
-        for source in range(count)
-        if periodic or 0 <= source + steps < count
-    ]
-    return lax.ppermute(value, axis, pairs)
+    assert count % 2 == 0
+    pairs = [(source, source ^ 1) for source in range(count)]
+    others = [(source, (source + 1 if source % 2 else source - 1) % count) for source in range(count)]
+    if not periodic:
+        others = [pair for pair in others if abs(pair[0] - pair[1]) == 1]
+    return lax.ppermute(first, axis, pairs), lax.ppermute(second, axis, others)
 
 
 def per_device(grains, send_slots, send_counts, cell_index, fluid, block_slots, block_counts):
@@ -558,18 +601,19 @@
     total = cell_index.shape[0]
     axes = ("stream", "span")
 
-    down, up = leave(grains, send_slots[0], send_counts)
-    below = shift(down, "stream", 1, True)
-    above = shift(up, "stream", -1, True)
-    after, quant, depth_op, stream_op, span_op, choose = keep(
+    *leaving, depth_op, stream_op, span_op = leave(
+        grains, send_slots[0], send_counts, rows_x, rows_y, depth
+    )
+    arrived = swap(*leaving, "stream", True)
+    after, quant, choose = keep(
         grains, send_slots[0], send_counts, cell_index.reshape(1, -1),
         block_slots[0].T, block_counts, rows_x, rows_y, depth,
     )
-    grains_after, quant = join(after, quant, below, above)
+    grains_after, quant = join(after, quant, *arrived)
 
     chunk = math.gcd(total, 2048)
     steps = total // chunk
-    middle = steps // 4 * 2
+    middle = steps // 4
     flow = fluid.reshape(3 * columns, depth)
 
     def add(channels, span, partial, last, earlier=()):
@@ -577,17 +621,13 @@
             channels, rows_x, rows_y, depth, chunk, span, quant, partial, depth_op if last else None, earlier
         )
 
-    def stream(field, low, high, earlier):
-        before = shift(high, "stream", 1, True)
-        after = shift(low, "stream", -1, True)
-        return stream_pass(field.shape[0] // columns, rows_x, field, before, after, stream_op, earlier)
-
-    def span(channels, field, low, high, base, earlier):
-        before = shift(high, "span", 1, False)
-        after = shift(low, "span", -1, False)
-        return span_pass(
-            channels, field, before, after, span_op, choose, flow, base, peers, rows_q, earlier
-        )
+    def stream(field, first, second, earlier):
+        halos = swap(first, second, "stream", True)
+        return stream_pass(field.shape[0] // columns, rows_x, field, *halos, stream_op, earlier)
+
+    def span(channels, field, first, second, base, earlier):
+        halos = swap(first, second, "span", False)
+        return span_pass(channels, field, *halos, span_op, choose, flow, base, peers, rows_q, earlier)
 
     def exchange(outgoing):
         return lax.all_to_all(outgoing, axes, split_axis=0, concat_axis=0, tiled=True)
@@ -597,8 +637,9 @@
     outer = stream(*outer, (inner,))
     inner = add((2, 1), (middle, steps), inner, True, outer[:1])
     solid_outer, outgoing_outer = span((0, 3), *outer, None, inner[:1])
+    inner = stream(*inner, (solid_outer,))
+    outgoing_outer, inner = lax.optimization_barrier((outgoing_outer, inner))
     arrived_outer = exchange(outgoing_outer)
-    inner = stream(*inner, (outgoing_outer,))
     solid_inner, outgoing_inner = span((2, 1), *inner, solid_outer, ())
     arrived_inner = exchange(outgoing_inner)
 

time: 104 us -> 101 us (0.971)
  waiting for transfers between devices: 25.5 us -> 29.3 us
  starting transfers between devices: 28.6 us -> 25.3 us
  Pallas kernels: 44.3 us -> 42.7 us
  local copies, waits for them, and re-layouts: 1.48 us -> 0.09 us
    all_to_all x2, starting transfers between devices: 16.2 us -> 11.4 us  [exchange(): lax.all_to_all(outgoing, axes, split_axis=0, concat_axis=0, tiled=True)]
    ppermute x10, waiting for transfers between devices: 11.3 us -> 15.2 us  [the longest x5 12.7 us: swap(): lax.ppermute(first, axis, pairs)]
    ppermute x10, starting transfers between devices: 12.5 us -> 13.9 us  [the longest x5 11.1 us: swap(): lax.ppermute(first, axis, pairs)]
    unnamed x6 -> x4, local copies, waits for them, and re-layouts: 1.41 us -> 0.01 us
  transfers between devices with their start and end apart: 12 -> 12, of which waited for: 5 -> 5; matrix products, arithmetic and copies ran while one was open for 1% -> 1% of each run, Pallas kernels for 20% -> 21%
where the time goes in v3:
time: 101 us
  Pallas kernels  42.7 us (42%)
  waiting for transfers between devices  29.3 us (29%)
  starting transfers between devices  25.3 us (25%)
  other arithmetic  2.52 us (2%)
    pallas_call x3, Pallas kernels, deposit(): pl.pallas_call(functools.partial(deposit_kernel, channels, rows_x, rows_y...  24 us
    all_to_all x2, waiting for transfers between devices, exchange(): lax.all_to_all(outgoing, axes, split_axis=0, concat_axis=0, tiled=True)  14.2 us
    ppermute x5, waiting for transfers between devices, swap(): lax.ppermute(first, axis, pairs)  12.7 us
    all_to_all x2, starting transfers between devices, exchange(): lax.all_to_all(outgoing, axes, split_axis=0, concat_axis=0, tiled=True)  11.4 us
    ppermute x5, starting transfers between devices, swap(): lax.ppermute(first, axis, pairs)  11.1 us
    pallas_call x1, Pallas kernels, leave(): pl.pallas_call(functools.partial(leave_kernel, rows_x, rows_y), out_shape...  8.15 us
    pallas_call x1, Pallas kernels, keep(): pl.pallas_call(functools.partial(keep_kernel, rows_x, rows_y, depth), out...  4.75 us
    pallas_call x2, Pallas kernels, span_pass(): pl.pallas_call(functools.partial(span_kernel, channels, rows_q), out_shap...  3.83 us
  transfers between devices with their start and end apart: 12, of which 5 were waited for; matrix products, arithmetic and copies ran while one was open for 1% of the time, Pallas kernels for 21%

profile of v3, /device:TPU:1, one launch (start us, length us, event | category | flops | bytes accessed | tf_op | source)
XLA Modules:
  0.0 100.7 jit_solution(10298186020365452959)
XLA Ops:
  0.6 8.2 %leave.1 = (f32[13,2048]{1,0:T(8,128)S(1)}, f32[13,2048]{1,0:T(8,128)S(1)}, bf16[2,256,256]{2,1,0:T(8,128)(2,1)S(1)}, bf16[2,256,304]{2,1,0:T(8,128)(2,1)S(1)}, bf16[2,256,448]{2,1,0:T(8,128)(2,1)S(1)}) custom-call(f32[13,24576]{1,0:T(8,128)} %grains_hbm.1, s32[2,2048]{1,0:T(2,128)} %bitcast.13, s32[1,2]{1,0:T(1,128)} %counts_hbm.3), custom_call_target="tpu_custom_call" | custom-call | bytes 24000000 | tf_op jit(solution)/shard_map/leave/pallas_call | solution.py:153
  8.8 1.6 %collective-permute-start = (f32[13,2048]{1,0:T(8,128)S(1)}, f32[13,2048]{1,0:T(8,128)S(1)}, u32[]{:S(2)}, u32[]{:S(2)}) collective-permute-start(f32[13,2048]{1,0:T(8,128)S(1)} %get-tuple-element.35), channel_id=1, source_target_pairs={{0,4},{4,0},{8,12},{12,8},{16,20},{20,16},{24,28},{28,24},{1,5},{5... | collective-permute-start | bytes 319496 | tf_op jit(solution)/shard_map/ppermute | solution.py:593
  10.8 4.8 %keep.1 = (f32[13,28672]{1,0:T(8,128)}, f32[8,28672]{1,0:T(8,128)S(1)}, bf16[256,256]{1,0:T(8,128)(2,1)S(1)}) custom-call(f32[13,24576]{1,0:T(8,128)S(1)} %copy-done, s32[2,2048]{1,0:T(2,128)} %bitcast.14, s32[1,2]{1,0:T(1,128)} %counts_hbm.3, s32[1,28672]{1,0:T(1,128)} %bitcast.12, s32[8,32]{1,0:T(8,128)} %bitcast.15, s32[1,32]{1,0:T(1,128)} %alive_hbm.1), custom_call_target="tpu_custom_call" | custom-call | bytes 12000000 | tf_op jit(solution)/shard_map/keep/pallas_call | solution.py:333
  15.7 0.7 join.1
  16.4 11.7 %deposit.3 = (f32[512,256]{1,0:T(8,128)S(1)}, f32[48,256]{1,0:T(8,128)S(1)}, f32[48,256]{1,0:T(8,128)S(1)}) custom-call(f32[8,28672]{1,0:T(8,128)S(1)} %get-tuple-element.38.refs_0_, bf16[2,256,256]{2,1,0:T(8,128)(2,1)S(1)} %get-tuple-element.39.refs_1_.refs_2_), custom_call_target="tpu_custom_call" | custom-call | bytes 33600000 | tf_op jit(solution)/shard_map/deposit/pallas_call | solution.py:480
  28.1 2.8 %collective-permute-start.2 = (f32[48,256]{1,0:T(8,128)S(1)}, f32[48,256]{1,0:T(8,128)S(1)}, u32[]{:S(2)}, u32[]{:S(2)}) collective-permute-start(f32[48,256]{1,0:T(8,128)S(1)} %get-tuple-element.41), channel_id=1, source_target_pairs={{0,4},{4,0},{8,12},{12,8},{16,20},{20,16},{24,28},{28,24},{1,5},{5... | collective-permute-start | bytes 147464 | tf_op jit(solution)/shard_map/ppermute | solution.py:593
  31.0 2.6 %deposit.4.refs_0_.refs_1_ = f32[512,256]{1,0:T(8,128)S(1)} custom-call(f32[8,28672]{1,0:T(8,128)S(1)} %get-tuple-element.38.refs_0_), custom_call_target="tpu_custom_call" | custom-call | bytes 7200000 | tf_op jit(solution)/shard_map/deposit/pallas_call | solution.py:480
  33.6 1.2 %collective-permute-done.3.second_in = f32[48,256]{1,0:T(8,128)S(1)} collective-permute-done((f32[48,256]{1,0:T(8,128)S(1)}, f32[48,256]{1,0:T(8,128)S(1)}, u32[]{:S(2)}, u32[]{:S(2)}) %collective-permute-start.3) | collective-permute-done | bytes 49184 | tf_op jit(solution)/shard_map/ppermute | solution.py:593
  35.4 3.8 %collective-permute-start.4 = (f32[192,256]{1,0:T(8,128)S(1)}, f32[192,256]{1,0:T(8,128)S(1)}, u32[]{:S(2)}, u32[]{:S(2)}) collective-permute-start(f32[192,256]{1,0:T(8,128)S(1)} %get-tuple-element.45), channel_id=1, source_target_pairs={{0,1},{1,0},{2,3},{3,2},{4,5},{5,4},{6,7},{7,6},{8,9},{9,8},{10,11... | collective-permute-start | bytes 589832 | tf_op jit(solution)/shard_map/ppermute | solution.py:593
  39.3 0.8 collective-permute-start.5
  40.1 9.7 %deposit.5 = (f32[512,256]{1,0:T(8,128)S(1)}, f32[48,256]{1,0:T(8,128)S(1)}, f32[48,256]{1,0:T(8,128)S(1)}) custom-call(f32[8,28672]{1,0:T(8,128)S(1)} %get-tuple-element.38.refs_0_, f32[512,256]{1,0:T(8,128)S(1)} %deposit.4.refs_0_.refs_1_, bf16[2,256,256]{2,1,0:T(8,128)(2,1)S(1)} %get-tuple-element.39.refs_1_.refs_2_, ...), custom_call_target="tpu_custom_call" | custom-call | bytes 26400000 | tf_op jit(solution)/shard_map/deposit/pallas_call | solution.py:480
  49.8 1.3 %collective-permute-start.6 = (f32[48,256]{1,0:T(8,128)S(1)}, f32[48,256]{1,0:T(8,128)S(1)}, u32[]{:S(2)}, u32[]{:S(2)}) collective-permute-start(f32[48,256]{1,0:T(8,128)S(1)} %get-tuple-element.52), channel_id=1, source_target_pairs={{0,4},{4,0},{8,12},{12,8},{16,20},{20,16},{24,28},{28,24},{1,5},{5... | collective-permute-start | bytes 147464 | tf_op jit(solution)/shard_map/ppermute | solution.py:593
  51.1 0.9 collective-permute-start.7
  52.1 1.9 %span_pass.2 = (f32[512,256]{1,0:T(8,128)S(1)}, f32[32,8,2,256]{3,2,1,0:T(2,128)}) custom-call(f32[512,256]{1,0:T(8,128)S(1)} %get-tuple-element.44.refs_3_.refs_0_, f32[192,256]{1,0:T(8,128)S(1)} %collective-permute-done.4.refs_1_, f32[192,256]{1,0:T(8,128)S(1)} %collective-permute-done.5.refs_2_, bf16[2,256,448]{2,1,0:T(8,128)(2,1)S(1)} %get-tuple-element.47.refs_3_, ...), custom_call_target="tpu_custom_call" | custom-call | bytes 4800000 | tf_op jit(solution)/shard_map/span_pass/pallas_call | solution.py:572
  54.0 1.2 %collective-permute-done.7.second_in = f32[48,256]{1,0:T(8,128)S(1)} collective-permute-done((f32[48,256]{1,0:T(8,128)S(1)}, f32[48,256]{1,0:T(8,128)S(1)}, u32[]{:S(2)}, u32[]{:S(2)}) %collective-permute-start.7) | collective-permute-done | bytes 49184 | tf_op jit(solution)/shard_map/ppermute | solution.py:593
  55.8 4.2 %all-to-all-start.1 = ((f32[32,8,2,256]{3,2,1,0:T(2,128)}), f32[32,8,2,256]{3,2,1,0:T(2,128)S(1)}, u32[]{:S(2)}, u32[]{:S(2)}) async-start(f32[32,8,2,256]{3,2,1,0:T(2,128)} %get-tuple-element.62), calls=%async_computation.1 | async-start | bytes 1048576 | tf_op jit(solution)/shard_map/all_to_all | solution.py:633
  60.0 1.5 %collective-permute-start.8 = (f32[192,256]{1,0:T(8,128)S(1)}, f32[192,256]{1,0:T(8,128)S(1)}, u32[]{:S(2)}, u32[]{:S(2)}) collective-permute-start(f32[192,256]{1,0:T(8,128)S(1)} %get-tuple-element.58), channel_id=1, source_target_pairs={{0,1},{1,0},{2,3},{3,2},{4,5},{5,4},{6,7},{7,6},{8,9},{9,8},{10,11... | collective-permute-start | bytes 589832 | tf_op jit(solution)/shard_map/ppermute | solution.py:593
  61.4 0.7 collective-permute-start.9
  62.1 12.7 %collective-permute-done.8.refs_1_ = f32[192,256]{1,0:T(8,128)S(1)} collective-permute-done((f32[192,256]{1,0:T(8,128)S(1)}, f32[192,256]{1,0:T(8,128)S(1)}, u32[]{:S(2)}, u32[]{:S(2)}) %collective-permute-start.8) | collective-permute-done | bytes 196640 | tf_op jit(solution)/shard_map/ppermute | solution.py:593
  74.8 1.9 %span_pass.3 = (f32[512,256]{1,0:T(8,128)S(1)}, f32[32,8,2,256]{3,2,1,0:T(2,128)}) custom-call(f32[512,256]{1,0:T(8,128)S(1)} %get-tuple-element.57.refs_0_, f32[192,256]{1,0:T(8,128)S(1)} %collective-permute-done.8.refs_1_, f32[192,256]{1,0:T(8,128)S(1)} %collective-permute-done.9.refs_2_, bf16[2,256,448]{2,1,0:T(8,128)(2,1)S(1)} %get-tuple-element.47.refs_3_, ...), custom_call_target="tpu_custom_call" | custom-call | bytes 4800000 | tf_op jit(solution)/shard_map/span_pass/pallas_call | solution.py:572
  76.7 7.2 %all-to-all-start = ((f32[32,8,2,256]{3,2,1,0:T(2,128)}), f32[32,8,2,256]{3,2,1,0:T(2,128)S(1)}, u32[]{:S(2)}, u32[]{:S(2)}) async-start(f32[32,8,2,256]{3,2,1,0:T(2,128)} %get-tuple-element.61), calls=%async_computation | async-start | bytes 1048576 | tf_op jit(solution)/shard_map/all_to_all | solution.py:633
  84.0 1.0 %pad_maximum_fusion = f32[1024,256]{1,0:T(8,128)} fusion(f32[256,256]{1,0:T(8,128)S(1)} %get-tuple-element.64, f32[256,256]{1,0:T(8,128)S(1)} %get-tuple-element.67, f32[256,256]{1,0:T(8,128)S(1)} %get-tuple-element.68, f32[256,256]{1,0:T(8,128)S(1)} %get-tuple-element.63), kind=kLoop, calls=%fused_computation | loop fusion | flops 786432 | bytes 2097152 | tf_op jit(solution)/shard_map/concatenate | solution.py:646
  85.0 14.2 %all-to-all-done = f32[32,8,2,256]{3,2,1,0:T(2,128)S(1)} async-done(((f32[32,8,2,256]{3,2,1,0:T(2,128)}), f32[32,8,2,256]{3,2,1,0:T(2,128)S(1)}, u32[]{:S(2)}, u32[]{:S(2)}) %all-to-all-start) | async-done | bytes 524320 | tf_op jit(solution)/shard_map/all_to_all | solution.py:633
  99.2 1.5 %maximum_bitcast_fusion = f32[1,32,8,4,256]{4,3,2,1,0:T(4,128)} fusion(f32[32,8,2,256]{3,2,1,0:T(2,128)S(1)} %all-to-all-done.1, f32[32,8,2,256]{3,2,1,0:T(2,128)S(1)} %all-to-all-done), kind=kLoop, calls=%fused_computation.1 | loop fusion | flops 262144 | bytes 2097152 | tf_op jit(solution)/shard_map/broadcast_in_dim | solution.py:650
  (17 shorter events, 1.8 us)
Async XLA Ops:
  0.6 10.2 %copy-start = (f32[13,24576]{1,0:T(8,128)S(1)}, f32[13,24576]{1,0:T(8,128)}, u32[]{:S(2)}) copy-start(f32[13,24576]{1,0:T(8,128)} %grains_hbm.1) | copy-start | bytes 3833860
  8.8 6.8 %collective-permute-start = (f32[13,2048]{1,0:T(8,128)S(1)}, f32[13,2048]{1,0:T(8,128)S(1)}, u32[]{:S(2)}, u32[]{:S(2)}) collective-permute-start(f32[13,2048]{1,0:T(8,128)S(1)} %get-tuple-element.35), channel_id=1, source_target_pairs={{0,4},{4,0},{8,12},{12,8},{16,20},{20,16},{24,28},{28,24},{1,5},{5... | collective-permute-start | bytes 319496 | tf_op jit(solution)/shard_map/ppermute | solution.py:593
  10.4 5.3 %collective-permute-start.1 = (f32[13,2048]{1,0:T(8,128)S(1)}, f32[13,2048]{1,0:T(8,128)S(1)}, u32[]{:S(2)}, u32[]{:S(2)}) collective-permute-start(f32[13,2048]{1,0:T(8,128)S(1)} %get-tuple-element.36), channel_id=1, source_target_pairs={{0,28},{4,8},{8,4},{12,16},{16,12},{20,24},{24,20},{28,0},{1,29},{... | collective-permute-start | bytes 319496 | tf_op jit(solution)/shard_map/ppermute | solution.py:593
  28.1 5.5 %collective-permute-start.2 = (f32[48,256]{1,0:T(8,128)S(1)}, f32[48,256]{1,0:T(8,128)S(1)}, u32[]{:S(2)}, u32[]{:S(2)}) collective-permute-start(f32[48,256]{1,0:T(8,128)S(1)} %get-tuple-element.41), channel_id=1, source_target_pairs={{0,4},{4,0},{8,12},{12,8},{16,20},{20,16},{24,28},{28,24},{1,5},{5... | collective-permute-start | bytes 147464 | tf_op jit(solution)/shard_map/ppermute | solution.py:593
  31.0 3.8 %collective-permute-start.3 = (f32[48,256]{1,0:T(8,128)S(1)}, f32[48,256]{1,0:T(8,128)S(1)}, u32[]{:S(2)}, u32[]{:S(2)}) collective-permute-start(f32[48,256]{1,0:T(8,128)S(1)} %get-tuple-element.42), channel_id=1, source_target_pairs={{0,28},{4,8},{8,4},{12,16},{16,12},{20,24},{24,20},{28,0},{1,29},{... | collective-permute-start | bytes 147464 | tf_op jit(solution)/shard_map/ppermute | solution.py:593
  34.8 17.3 %copy-start.1 = (f32[3,32,8,256]{3,2,1,0:T(8,128)S(1)}, f32[3,32,8,256]{3,2,1,0:T(8,128)}, u32[]{:S(2)}) copy-start(f32[3,32,8,256]{3,2,1,0:T(8,128)} %param.11) | copy-start | bytes 2359300
  35.4 16.7 %collective-permute-start.4 = (f32[192,256]{1,0:T(8,128)S(1)}, f32[192,256]{1,0:T(8,128)S(1)}, u32[]{:S(2)}, u32[]{:S(2)}) collective-permute-start(f32[192,256]{1,0:T(8,128)S(1)} %get-tuple-element.45), channel_id=1, source_target_pairs={{0,1},{1,0},{2,3},{3,2},{4,5},{5,4},{6,7},{7,6},{8,9},{9,8},{10,11... | collective-permute-start | bytes 589832 | tf_op jit(solution)/shard_map/ppermute | solution.py:593
  39.3 12.8 %collective-permute-start.5 = (f32[192,256]{1,0:T(8,128)S(1)}, f32[192,256]{1,0:T(8,128)S(1)}, u32[]{:S(2)}, u32[]{:S(2)}) collective-permute-start(f32[192,256]{1,0:T(8,128)S(1)} %get-tuple-element.46), channel_id=1, source_target_pairs={{1,2},{2,1},{5,6},{6,5},{9,10},{10,9},{13,14},{14,13},{17,18},{18,... | collective-permute-start | bytes 589832 | tf_op jit(solution)/shard_map/ppermute | solution.py:593
  49.8 4.2 %collective-permute-start.6 = (f32[48,256]{1,0:T(8,128)S(1)}, f32[48,256]{1,0:T(8,128)S(1)}, u32[]{:S(2)}, u32[]{:S(2)}) collective-permute-start(f32[48,256]{1,0:T(8,128)S(1)} %get-tuple-element.52), channel_id=1, source_target_pairs={{0,4},{4,0},{8,12},{12,8},{16,20},{20,16},{24,28},{28,24},{1,5},{5... | collective-permute-start | bytes 147464 | tf_op jit(solution)/shard_map/ppermute | solution.py:593
  51.1 4.1 %collective-permute-start.7 = (f32[48,256]{1,0:T(8,128)S(1)}, f32[48,256]{1,0:T(8,128)S(1)}, u32[]{:S(2)}, u32[]{:S(2)}) collective-permute-start(f32[48,256]{1,0:T(8,128)S(1)} %get-tuple-element.53), channel_id=1, source_target_pairs={{0,28},{4,8},{8,4},{12,16},{16,12},{20,24},{24,20},{28,0},{1,29},{... | collective-permute-start | bytes 147464 | tf_op jit(solution)/shard_map/ppermute | solution.py:593
  55.8 20.9 %all-to-all-start.1 = ((f32[32,8,2,256]{3,2,1,0:T(2,128)}), f32[32,8,2,256]{3,2,1,0:T(2,128)S(1)}, u32[]{:S(2)}, u32[]{:S(2)}) async-start(f32[32,8,2,256]{3,2,1,0:T(2,128)} %get-tuple-element.62), calls=%async_computation.1 | async-start | bytes 1048576 | tf_op jit(solution)/shard_map/all_to_all | solution.py:633
  60.0 14.8 %collective-permute-start.8 = (f32[192,256]{1,0:T(8,128)S(1)}, f32[192,256]{1,0:T(8,128)S(1)}, u32[]{:S(2)}, u32[]{:S(2)}) collective-permute-start(f32[192,256]{1,0:T(8,128)S(1)} %get-tuple-element.58), channel_id=1, source_target_pairs={{0,1},{1,0},{2,3},{3,2},{4,5},{5,4},{6,7},{7,6},{8,9},{9,8},{10,11... | collective-permute-start | bytes 589832 | tf_op jit(solution)/shard_map/ppermute | solution.py:593
  61.4 13.3 %collective-permute-start.9 = (f32[192,256]{1,0:T(8,128)S(1)}, f32[192,256]{1,0:T(8,128)S(1)}, u32[]{:S(2)}, u32[]{:S(2)}) collective-permute-start(f32[192,256]{1,0:T(8,128)S(1)} %get-tuple-element.59), channel_id=1, source_target_pairs={{1,2},{2,1},{5,6},{6,5},{9,10},{10,9},{13,14},{14,13},{17,18},{18,... | collective-permute-start | bytes 589832 | tf_op jit(solution)/shard_map/ppermute | solution.py:593
  76.7 22.5 %all-to-all-start = ((f32[32,8,2,256]{3,2,1,0:T(2,128)}), f32[32,8,2,256]{3,2,1,0:T(2,128)S(1)}, u32[]{:S(2)}, u32[]{:S(2)}) async-start(f32[32,8,2,256]{3,2,1,0:T(2,128)} %get-tuple-element.61), calls=%async_computation | async-start | bytes 1048576 | tf_op jit(solution)/shard_map/all_to_all | solution.py:633

commit v4 on v3

--- a/solution.py
+++ b/solution.py
@@ -74,15 +74,16 @@
 
 
 def leave_kernel(
-    rows_x, rows_y, grains_hbm, slots_hbm, counts_hbm, first_ref, second_ref, depth_ref, stream_ref, span_ref,
-    grains_ref, stage, table, picked, slots_v, slots_s, counts_s, sems,
+    rows_x, rows_y, grains_hbm, slots_hbm, counts_hbm, cells_hbm, picks_hbm, alive_hbm,
+    first_ref, second_ref, depth_ref, stream_ref, span_ref, choose_ref, marks_ref, cells_ref,
+    grains_ref, stage, table, picked, slots_v, slots_s, counts_s, picks_v, alive_v, sems,
 ):
     records, slot_count = grains_ref.shape
     width = first_ref.shape[1]
     rows = table.shape[0]
     parts = -(-slot_count // rows)
-    sources = (grains_hbm, slots_hbm, slots_hbm, counts_hbm)
-    targets = (grains_ref, slots_v, slots_s, counts_s)
+    sources = (grains_hbm, slots_hbm, slots_hbm, counts_hbm, picks_hbm, alive_hbm, cells_hbm)
+    targets = (grains_ref, slots_v, slots_s, counts_s, picks_v, alive_v, cells_ref)
     copies = [
         pltpu.make_async_copy(source, target, sems.at[i])
         for i, (source, target) in enumerate(zip(sources, targets))
@@ -102,6 +103,10 @@
         table[here, :] = jnp.transpose(stage[:, here])
     for copy in copies[1:]:
         copy.wait()
+    build_choice(picks_v, alive_v, choose_ref)
+    for which in (0, 1):
+        live = lax.broadcasted_iota(jnp.int32, (1, width), 1) < counts_s[0, which]
+        marks_ref[which:which + 1, :] = jnp.where(live, slots_v[which:which + 1, :], -1)
 
     run = picked.shape[0]
     lane = lax.broadcasted_iota(jnp.int32, (8, LANES), 1)
@@ -142,7 +147,7 @@
         lax.fori_loop(used, width // run, blank, 0)
 
 
-def leave(grains, slots, counts, rows_x, rows_y, depth):
+def leave(grains, slots, counts, cells, picks, alive, rows_x, rows_y, depth):
     records, slot_count = grains.shape
     width = slots.shape[1]
     columns = rows_x * rows_y
@@ -158,9 +163,12 @@
             jax.ShapeDtypeStruct((2, depth, depth), bf16),
             jax.ShapeDtypeStruct((2, columns, columns + 2 * REACH * rows_y), bf16),
             jax.ShapeDtypeStruct((2, columns, columns + 2 * REACH * rows_x), bf16),
+            jax.ShapeDtypeStruct((picks.size, columns), bf16),
+            jax.ShapeDtypeStruct(slots.shape, jnp.int32),
+            jax.ShapeDtypeStruct(cells.shape, jnp.int32),
         ),
-        in_specs=[HBM] * 3,
-        out_specs=(VMEM,) * 5,
+        in_specs=[HBM] * 6,
+        out_specs=(VMEM,) * 8,
         scratch_shapes=[
             pltpu.VMEM(grains.shape, jnp.float32),
             pltpu.VMEM((LANES, rows), jnp.float32),
@@ -169,12 +177,14 @@
             pltpu.VMEM(slots.shape, jnp.int32),
             pltpu.SMEM(slots.shape, jnp.int32),
             pltpu.SMEM(counts.shape, jnp.int32),
-            pltpu.SemaphoreType.DMA((4,)),
+            pltpu.VMEM(picks.shape, jnp.int32),
+            pltpu.VMEM(alive.shape, jnp.int32),
+            pltpu.SemaphoreType.DMA((7,)),
         ],
         compiler_params=params(16),
         cost_estimate=cost(8),
         name="leave",
-    )(*in_hbm(grains, slots, counts))
+    )(*in_hbm(grains, slots, counts, cells, picks, alive))
 
 
 def weights_at(apart):
@@ -191,6 +201,21 @@
     stop = start + value.shape[1]
     out_ref[0, :, start:stop] = high
     out_ref[1, :, start:stop] = low
+
+
+def build_choice(picks_ref, alive_ref, choose_ref):
+    rows_q, peers = picks_ref.shape
+    slots, columns = choose_ref.shape
+    alive = lax.broadcasted_iota(jnp.int32, (rows_q, peers), 0) < alive_ref[...]
+    picks = jnp.where(alive, picks_ref[...], -1).astype(jnp.float32).astype(jnp.bfloat16)
+    place_e, _ = split(lax.broadcasted_iota(jnp.int32, (slots, peers), 0), rows_q)
+    here = place_e == lax.broadcasted_iota(jnp.int32, (slots, peers), 1)
+    named = dot(jnp.where(here, 1.0, 0.0).astype(jnp.bfloat16), picks, NT)
+    _, place_q = split(lax.broadcasted_iota(jnp.int32, (slots, rows_q), 0), rows_q)
+    mine = place_q == lax.broadcasted_iota(jnp.int32, (slots, rows_q), 1)
+    named = jnp.sum(jnp.where(mine, named, 0.0), axis=1, keepdims=True)
+    hit = named == lax.broadcasted_iota(jnp.int32, (slots, columns), 1).astype(jnp.float32)
+    choose_ref[...] = jnp.where(hit, 1.0, 0.0).astype(jnp.bfloat16)
 
 
 def build_operators(rows_x, rows_y, depth_ref, stream_ref, span_ref):
@@ -221,54 +246,26 @@
 
 
 def keep_kernel(
-    rows_x, rows_y, depth, grains_ref, slots_hbm, counts_hbm, cells_hbm, picks_hbm, alive_hbm,
-    after_hbm, quant_ref, choose_ref,
-    slots_v, counts_s, cells_v, picks_v, alive_v, high_rows, low_rows, gone, kept, sems,
+    rows_x, rows_y, depth, grains_ref, marks_ref, cells_ref, after_hbm, quant_ref,
+    high_rows, low_rows, gone, kept, sems,
 ):
     records, slot_count = grains_ref.shape
     total = quant_ref.shape[1]
-    width = slots_v.shape[1]
+    width = marks_ref.shape[1]
     tiles = slot_count // LANES
-    columns = rows_x * rows_y
-    pieces = 4
-    sources = (slots_hbm, counts_hbm, cells_hbm, picks_hbm, alive_hbm)
-    targets = (slots_v, counts_s, cells_v, picks_v, alive_v)
-    copies = [
-        pltpu.make_async_copy(source, target, sems.at[i])
-        for i, (source, target) in enumerate(zip(sources, targets))
-    ]
-    for copy in copies:
-        copy.start()
-
-    for copy in copies:
-        copy.wait()
-
-    rows_q, peers = picks_v.shape
-    alive = lax.broadcasted_iota(jnp.int32, (rows_q, peers), 0) < alive_v[...]
-    picks = jnp.where(alive, picks_v[...], -1)
-    place_e, place_q = split(lax.broadcasted_iota(jnp.int32, (peers * rows_q, peers), 0), rows_q)
-    here = place_e == lax.broadcasted_iota(jnp.int32, (peers * rows_q, peers), 1)
-    column = lax.broadcasted_iota(jnp.int32, (columns, peers), 0)
-    chosen = None
-    for q in range(rows_q):
-        place = jnp.where(jnp.logical_and(here, place_q == q), 1.0, 0.0).astype(jnp.bfloat16)
-        named = jnp.where(column == picks[q:q + 1, :], 1.0, 0.0).astype(jnp.bfloat16)
-        value = dot(place, named, NT)
-        chosen = value if chosen is None else chosen + value
-    choose_ref[...] = chosen.astype(jnp.bfloat16)
+    pieces = sems.shape[0]
 
     row16 = lax.broadcasted_iota(jnp.int32, (16, LANES), 0).astype(jnp.float32)
-    lane = lax.broadcasted_iota(jnp.int32, (1, LANES), 1)
     zero = jnp.zeros((16, LANES), jnp.bfloat16)
     one = jnp.ones((16, LANES), jnp.bfloat16)
     for which in (0, 1):
 
-        def mark(i, carry):
+        def put(i, carry):
             lanes = lane_tile(i)
             to = pl.ds(pl.multiple_of(which * width + i * LANES, LANES), LANES)
-            slot = slots_v[which:which + 1, lanes]
-            tile_of, lane_of = split(slot, LANES)
-            tile_of = jnp.where(lane + i * LANES < counts_s[0, which], tile_of, -1)
+            mark = marks_ref[which:which + 1, lanes]
+            tile_of, lane_of = split(mark, LANES)
+            tile_of = jnp.where(mark < 0, -1, tile_of)
             tile_of = wide(tile_of.astype(jnp.float32))
             lane_of = wide(lane_of.astype(jnp.float32))
             for k in range(high_rows.shape[0] // 16):
@@ -279,7 +276,7 @@
                 low_rows[16 * k:16 * k + 16, to] = jnp.where(hit, one, zero)
             return carry
 
-        lax.fori_loop(0, width // LANES, mark, 0, unroll=4)
+        lax.fori_loop(0, width // LANES, put, 0, unroll=8)
     gone[...] = dot(high_rows[...], low_rows[...], NT)
 
     row8 = lax.broadcasted_iota(jnp.int32, (8, LANES), 0)
@@ -298,7 +295,7 @@
         kept[8:records, lanes] = rest
         radius = rest[1:2]
         volume = 4.18879 * (radius * radius * radius)
-        col, lev = place(cells_v[:, lanes])
+        col, lev = place(cells_ref[:, lanes])
         value = jnp.where(row8 == QUANT_ROW[0], volume, volume * head)
         value = jnp.where(row8 == COLUMN_ROW, col, value)
         quant_ref[:, lanes] = jnp.where(row8 == LEVEL_ROW, lev, value)
@@ -308,14 +305,14 @@
     for n in range(pieces):
         first = tiles * n // pieces
         last = tiles * (n + 1) // pieces
-        lax.fori_loop(first, last, keep, 0, unroll=8)
+        lax.fori_loop(first, last, keep, 0, unroll=16)
         here = pl.ds(first * LANES, (last - first) * LANES)
-        writes.append(pltpu.make_async_copy(kept.at[:, here], after_hbm.at[:, here], sems.at[len(copies) + n]))
+        writes.append(pltpu.make_async_copy(kept.at[:, here], after_hbm.at[:, here], sems.at[n]))
         writes[n].start()
 
     def arrivals(i, carry):
         lanes = lane_tile(i)
-        col, lev = place(cells_v[:, lanes])
+        col, lev = place(cells_ref[:, lanes])
         quant_ref[:, lanes] = jnp.where(row8 == COLUMN_ROW, col, lev)
         return carry
 
@@ -324,37 +321,27 @@
         write.wait()
 
 
-def keep(grains, slots, counts, cells, picks, alive, rows_x, rows_y, depth):
+def keep(grains, marks, cells, rows_x, rows_y, depth):
     records, slot_count = grains.shape
     total = cells.shape[1]
-    columns = rows_x * rows_y
-    marks = -(-(slot_count // LANES) // 16) * 16
-    f32, bf16, i32 = jnp.float32, jnp.bfloat16, jnp.int32
+    rows = -(-(slot_count // LANES) // 16) * 16
+    f32, bf16 = jnp.float32, jnp.bfloat16
     return pl.pallas_call(
         functools.partial(keep_kernel, rows_x, rows_y, depth),
-        out_shape=(
-            jax.ShapeDtypeStruct((records, total), f32),
-            jax.ShapeDtypeStruct((8, total), f32),
-            jax.ShapeDtypeStruct((picks.size, columns), bf16),
-        ),
-        in_specs=[VMEM] + [HBM] * 5,
-        out_specs=(HBM, VMEM, VMEM),
+        out_shape=(jax.ShapeDtypeStruct((records, total), f32), jax.ShapeDtypeStruct((8, total), f32)),
+        in_specs=[VMEM] * 3,
+        out_specs=(HBM, VMEM),
         scratch_shapes=[
-            pltpu.VMEM(slots.shape, i32),
-            pltpu.SMEM(counts.shape, i32),
-            pltpu.VMEM(cells.shape, i32),
-            pltpu.VMEM(picks.shape, i32),
-            pltpu.VMEM(alive.shape, i32),
-            pltpu.VMEM((marks, 2 * slots.shape[1]), bf16),
-            pltpu.VMEM((LANES, 2 * slots.shape[1]), bf16),
-            pltpu.VMEM((marks, LANES), f32),
+            pltpu.VMEM((rows, 2 * marks.shape[1]), bf16),
+            pltpu.VMEM((LANES, 2 * marks.shape[1]), bf16),
+            pltpu.VMEM((rows, LANES), f32),
             pltpu.VMEM(grains.shape, f32),
-            pltpu.SemaphoreType.DMA((9,)),
+            pltpu.SemaphoreType.DMA((4,)),
         ],
         compiler_params=params(20),
         cost_estimate=cost(4),
         name="keep",
-    )(grains, *in_hbm(slots, counts, cells, picks, alive))
+    )(grains, marks, cells)
 
 
 def join_kernel(after_in, quant_in, first_ref, second_ref, after_ref, quant_ref, sems):
@@ -403,7 +390,7 @@
     )(*in_hbm(after), quant, first, second)
 
 
-def deposit_kernel(channels, rows_x, rows_y, chunk, span, begins, ends, earlier, *refs):
+def deposit_kernel(channels, rows_x, rows_y, chunk, span, begins, ends, direct, earlier, *refs):
     refs = list(refs)
     quant_ref = refs.pop(0)
     partial_ref = None if begins else refs.pop(0)
@@ -411,7 +398,7 @@
     del refs[:earlier]
     field_ref = refs.pop(0)
     first_ref, second_ref = (refs.pop(0), refs.pop(0)) if ends else (None, None)
-    left_a, left_b, right_a, right_b, total = refs
+    total = refs.pop(-1)
     begin, end = span
     columns = rows_x * rows_y
     depth = total.shape[1]
@@ -436,19 +423,47 @@
                 hit = (row16 + 16.0 * k).astype(jnp.bfloat16) == level
                 right[16 * k:16 * k + 16, here] = jnp.where(hit, one, zero)
 
-    build(left_a, right_a, begin)
-
-    def two(i, carry):
-        now = begin + 2 * i
-        build(left_b, right_b, now + 1)
-        total[...] += dot(left_a[...], right_a[...], NT)
-        build(left_a, right_a, jnp.minimum(now + 2, end - 1))
-        total[...] += dot(left_b[...], right_b[...], NT)
-        return carry
-
-    lax.fori_loop(0, (end - begin) // 2, two, 0)
-    if (end - begin) % 2:
-        total[...] += dot(left_a[...], right_a[...], NT)
+    def product(start, size):
+        lefts = [[] for _ in range(count * columns // 16)]
+        rights = [[] for _ in range(depth // 16)]
+        for j in range(size // LANES):
+            lanes = pl.ds(pl.multiple_of(start + j * LANES, LANES), LANES)
+            parts = [wide(quant_ref[QUANT_ROW[c]:QUANT_ROW[c] + 1, lanes]) for c in channels]
+            column = wide(quant_ref[COLUMN_ROW:COLUMN_ROW + 1, lanes])
+            level = wide(quant_ref[LEVEL_ROW:LEVEL_ROW + 1, lanes])
+            for k in range(columns // 16):
+                hit = (row16 + 16.0 * k).astype(jnp.bfloat16) == column
+                for c in range(count):
+                    lefts[c * columns // 16 + k].append(jnp.where(hit, parts[c], zero))
+            for k in range(depth // 16):
+                hit = (row16 + 16.0 * k).astype(jnp.bfloat16) == level
+                rights[k].append(jnp.where(hit, one, zero))
+        left = jnp.concatenate([jnp.concatenate(row, axis=1) for row in lefts], axis=0)
+        right = jnp.concatenate([jnp.concatenate(row, axis=1) for row in rights], axis=0)
+        return dot(left, right, NT)
+
+    if direct:
+
+        def one_step(i, carry):
+            total[...] += product(i * direct, direct)
+            return carry
+
+        lax.fori_loop(begin * chunk // direct, end * chunk // direct, one_step, 0)
+    else:
+        left_a, left_b, right_a, right_b = refs
+        build(left_a, right_a, begin)
+
+        def two(i, carry):
+            now = begin + 2 * i
+            build(left_b, right_b, now + 1)
+            total[...] += dot(left_a[...], right_a[...], NT)
+            build(left_a, right_a, jnp.minimum(now + 2, end - 1))
+            total[...] += dot(left_b[...], right_b[...], NT)
+            return carry
+
+        lax.fori_loop(0, (end - begin) // 2, two, 0)
+        if (end - begin) % 2:
+            total[...] += dot(left_a[...], right_a[...], NT)
 
     if not ends:
         field_ref[...] = total[...]
@@ -467,7 +482,7 @@
                 second_ref[to:to + 1, :] = field_ref[pl.ds(row + second_x, 1), :]
 
 
-def deposit(channels, rows_x, rows_y, depth, chunk, span, quant, partial, depth_op, earlier):
+def deposit(channels, rows_x, rows_y, depth, chunk, span, direct, quant, partial, depth_op, earlier):
     columns = rows_x * rows_y
     count = len(channels)
     begins, ends = partial is None, depth_op is not None
@@ -478,11 +493,11 @@
     left = pltpu.VMEM((count * columns, chunk), jnp.bfloat16)
     right = pltpu.VMEM((depth, chunk), jnp.bfloat16)
     return pl.pallas_call(
-        functools.partial(deposit_kernel, channels, rows_x, rows_y, chunk, span, begins, ends, len(earlier)),
+        functools.partial(deposit_kernel, channels, rows_x, rows_y, chunk, span, begins, ends, direct, len(earlier)),
         out_shape=outs,
         in_specs=[VMEM] * len(operands) + [ANY] * len(earlier),
         out_specs=(VMEM,) * len(outs),
-        scratch_shapes=[left, left, right, right, pltpu.VMEM(field.shape, jnp.float32)],
+        scratch_shapes=([] if direct else [left, left, right, right]) + [pltpu.VMEM(field.shape, jnp.float32)],
         compiler_params=params(20),
         cost_estimate=cost(0.4 * count * (span[1] - span[0])),
         name="deposit",
@@ -601,24 +616,23 @@
     total = cell_index.shape[0]
     axes = ("stream", "span")
 
-    *leaving, depth_op, stream_op, span_op = leave(
-        grains, send_slots[0], send_counts, rows_x, rows_y, depth
+    first, second, depth_op, stream_op, span_op, choose, marks, cells = leave(
+        grains, send_slots[0], send_counts, cell_index.reshape(1, -1), block_slots[0].T, block_counts,
+        rows_x, rows_y, depth,
     )
-    arrived = swap(*leaving, "stream", True)
-    after, quant, choose = keep(
-        grains, send_slots[0], send_counts, cell_index.reshape(1, -1),
-        block_slots[0].T, block_counts, rows_x, rows_y, depth,
-    )
+    arrived = swap(first, second, "stream", True)
+    after, quant = keep(grains, marks, cells, rows_x, rows_y, depth)
     grains_after, quant = join(after, quant, *arrived)
 
     chunk = math.gcd(total, 2048)
     steps = total // chunk
-    middle = steps // 4
+    early = steps // 4
+    middle = steps * 5 // 7
     flow = fluid.reshape(3 * columns, depth)
 
-    def add(channels, span, partial, last, earlier=()):
+    def add(channels, span, direct, partial, last, earlier=()):
         return deposit(
-            channels, rows_x, rows_y, depth, chunk, span, quant, partial, depth_op if last else None, earlier
+            channels, rows_x, rows_y, depth, chunk, span, direct, quant, partial, depth_op if last else None, earlier
         )
 
     def stream(field, first, second, earlier):
@@ -632,16 +646,17 @@
     def exchange(outgoing):
         return lax.all_to_all(outgoing, axes, split_axis=0, concat_axis=0, tiled=True)
 
-    outer = add((0, 3), (0, steps), None, True)
-    (inner,) = add((2, 1), (0, middle), None, False)
+    direct = chunk // 2
+    outer = add((0, 3), (0, steps), 0, None, True)
+    (inner,) = add((2, 1), (0, early), direct, None, False)
     outer = stream(*outer, (inner,))
-    inner = add((2, 1), (middle, steps), inner, True, outer[:1])
-    solid_outer, outgoing_outer = span((0, 3), *outer, None, inner[:1])
-    inner = stream(*inner, (solid_outer,))
-    outgoing_outer, inner = lax.optimization_barrier((outgoing_outer, inner))
-    arrived_outer = exchange(outgoing_outer)
-    solid_inner, outgoing_inner = span((2, 1), *inner, solid_outer, ())
-    arrived_inner = exchange(outgoing_inner)
+    (inner,) = add((2, 1), (early, middle), direct, inner, False, outer[:1])
+    solid_outer, outgoing = span((0, 3), *outer, None, (inner,))
+    arrived_outer = exchange(outgoing)
+    inner = add((2, 1), (middle, steps), direct, inner, True, (outgoing,))
+    inner = stream(*inner, ())
+    solid_inner, outgoing = span((2, 1), *inner, solid_outer, ())
+    arrived_inner = exchange(outgoing)
 
     solid = jnp.concatenate(
         [solid_outer[:columns], solid_inner[columns:], solid_inner[:columns], solid_outer[columns:]], axis=0

time: 101 us -> 97.1 us (0.961)
  waiting for transfers between devices: 29.3 us -> 24.6 us
  starting transfers between devices: 25.3 us -> 24.2 us
  other arithmetic: 2.52 us -> 3.56 us
    ppermute x5, waiting for transfers between devices: 12.7 us -> 5.04 us  [swap(): lax.ppermute(first, axis, pairs)]
    ppermute x5, waiting for transfers between devices: 2.5 us -> 5.4 us  [swap(): lax.ppermute(second, axis, others)]
    ppermute x5, starting transfers between devices: 11.1 us -> 8.42 us  [swap(): lax.ppermute(first, axis, pairs)]
    pallas_call x1, Pallas kernels: 4.75 us -> 2.77 us  [keep(): pl.pallas_call(functools.partial(keep_kernel, rows_x, rows_y, depth), out...]
    pallas_call x3 -> x4, Pallas kernels: 24 us -> 25.7 us  [deposit(): pl.pallas_call(functools.partial(deposit_kernel, channels, rows_x, rows_y...]
    all_to_all x2, starting transfers between devices: 11.4 us -> 12.8 us  [exchange(): lax.all_to_all(outgoing, axes, split_axis=0, concat_axis=0, tiled=True)]
    broadcast_in_dim x1, other arithmetic: 1.48 us -> 2.52 us  [per_device(): return (grains_after, solid, received[None])]
  transfers between devices with their start and end apart: 12 -> 12, of which waited for: 5 -> 5; matrix products, arithmetic and copies ran while one was open for 1% -> 1% of each run, Pallas kernels for 21% -> 20%
where the time goes in v4:
time: 97.1 us; the launch traced here: 96.7 us
  Pallas kernels  43.4 us (45%)
  waiting for transfers between devices  24.6 us (25%)
  starting transfers between devices  24.2 us (25%)
  other arithmetic  3.56 us (4%)
    pallas_call x4, Pallas kernels, deposit(): pl.pallas_call(functools.partial(deposit_kernel, channels, rows_x, rows_y...  25.7 us
    all_to_all x2, waiting for transfers between devices, exchange(): lax.all_to_all(outgoing, axes, split_axis=0, concat_axis=0, tiled=True)  14.2 us
    all_to_all x2, starting transfers between devices, exchange(): lax.all_to_all(outgoing, axes, split_axis=0, concat_axis=0, tiled=True)  12.8 us
    pallas_call x1, Pallas kernels, leave(): pl.pallas_call(functools.partial(leave_kernel, rows_x, rows_y), out_shape...  9.14 us
    ppermute x5, starting transfers between devices, swap(): lax.ppermute(first, axis, pairs)  8.42 us
    ppermute x5, waiting for transfers between devices, swap(): lax.ppermute(second, axis, others)  5.4 us
    ppermute x5, waiting for transfers between devices, swap(): lax.ppermute(first, axis, pairs)  5.04 us
    pallas_call x2, Pallas kernels, span_pass(): pl.pallas_call(functools.partial(span_kernel, channels, rows_q), out_shap...  3.83 us
  transfers between devices with their start and end apart: 12, of which 5 were waited for; matrix products, arithmetic and copies ran while one was open for 1% of the time, Pallas kernels for 20%

profile of v4, /device:TPU:1, one launch (start us, length us, event | category | flops | bytes accessed | tf_op | source)
XLA Modules:
  0.0 96.7 jit_solution(7859282021332032913)
XLA Ops:
  0.6 9.1 %leave.1 = (f32[13,2048]{1,0:T(8,128)S(1)}, f32[13,2048]{1,0:T(8,128)S(1)}, bf16[2,256,256]{2,1,0:T(8,128)(2,1)S(1)}, bf16[2,256,304]{2,1,0:T(8,128)(2,1)S(1)}, ...) custom-call(f32[13,24576]{1,0:T(8,128)} %grains_ref.1, ...), custom_call_target="tpu_custom_call" | custom-call | bytes 24000000 | tf_op jit(solution)/shard_map/leave/pallas_call | solution.py:158
  9.8 1.6 %collective-permute-start = (f32[13,2048]{1,0:T(8,128)S(1)}, f32[13,2048]{1,0:T(8,128)S(1)}, u32[]{:S(2)}, u32[]{:S(2)}) collective-permute-start(f32[13,2048]{1,0:T(8,128)S(1)} %get-tuple-element.35), channel_id=1, source_target_pairs={{0,4},{4,0},{8,12},{12,8},{16,20},{20,16},{24,28},{28,24},{1,5},{5... | collective-permute-start | bytes 319496 | tf_op jit(solution)/shard_map/ppermute | solution.py:608
  11.6 2.8 %keep.1 = (f32[13,28672]{1,0:T(8,128)}, f32[8,28672]{1,0:T(8,128)S(1)}) custom-call(f32[13,24576]{1,0:T(8,128)S(1)} %copy-done, s32[2,2048]{1,0:T(2,128)S(1)} %get-tuple-element.31.marks_ref, s32[1,28672]{1,0:T(1,128)S(1)} %get-tuple-element.32.cells_ref), custom_call_target="tpu_custom_call" | custom-call | bytes 12000000 | tf_op jit(solution)/shard_map/keep/pallas_call | solution.py:329
  14.4 1.4 %collective-permute-done.1.second_ref = f32[13,2048]{1,0:T(8,128)S(1)} collective-permute-done((f32[13,2048]{1,0:T(8,128)S(1)}, f32[13,2048]{1,0:T(8,128)S(1)}, u32[]{:S(2)}, u32[]{:S(2)}) %collective-permute-start.1) | collective-permute-done | bytes 106528 | tf_op jit(solution)/shard_map/ppermute | solution.py:608
  15.8 0.7 join.1
  16.6 11.7 %deposit.4 = (f32[512,256]{1,0:T(8,128)S(1)}, f32[48,256]{1,0:T(8,128)S(1)}, f32[48,256]{1,0:T(8,128)S(1)}) custom-call(f32[8,28672]{1,0:T(8,128)S(1)} %get-tuple-element.38.refs_0_, bf16[2,256,256]{2,1,0:T(8,128)(2,1)S(1)} %get-tuple-element.39.refs_1_.refs_2_), custom_call_target="tpu_custom_call" | custom-call | bytes 33600000 | tf_op jit(solution)/shard_map/deposit/pallas_call | solution.py:495
  28.3 3.3 %collective-permute-start.2 = (f32[48,256]{1,0:T(8,128)S(1)}, f32[48,256]{1,0:T(8,128)S(1)}, u32[]{:S(2)}, u32[]{:S(2)}) collective-permute-start(f32[48,256]{1,0:T(8,128)S(1)} %get-tuple-element.41), channel_id=1, source_target_pairs={{0,4},{4,0},{8,12},{12,8},{16,20},{20,16},{24,28},{28,24},{1,5},{5... | collective-permute-start | bytes 147464 | tf_op jit(solution)/shard_map/ppermute | solution.py:608
  31.6 2.9 %deposit.5.refs_0_.refs_1_ = f32[512,256]{1,0:T(8,128)S(1)} custom-call(f32[8,28672]{1,0:T(8,128)S(1)} %get-tuple-element.38.refs_0_), custom_call_target="tpu_custom_call" | custom-call | bytes 7200000 | tf_op jit(solution)/shard_map/deposit/pallas_call | solution.py:495
  34.5 1.1 %collective-permute-done.3.second_in = f32[48,256]{1,0:T(8,128)S(1)} collective-permute-done((f32[48,256]{1,0:T(8,128)S(1)}, f32[48,256]{1,0:T(8,128)S(1)}, u32[]{:S(2)}, u32[]{:S(2)}) %collective-permute-start.3) | collective-permute-done | bytes 49184 | tf_op jit(solution)/shard_map/ppermute | solution.py:608
  36.2 0.9 collective-permute-start.4
  37.1 0.7 collective-permute-start.5
  37.8 6.7 %deposit.6.refs_6_.refs_1_ = f32[512,256]{1,0:T(8,128)S(1)} custom-call(f32[8,28672]{1,0:T(8,128)S(1)} %get-tuple-element.38.refs_0_, f32[512,256]{1,0:T(8,128)S(1)} %deposit.5.refs_0_.refs_1_, f32[512,256]{1,0:T(8,128)S(1)} %get-tuple-element.44.refs_2_.refs_0_), custom_call_target="tpu_custom_call" | custom-call | bytes 16800000 | tf_op jit(solution)/shard_map/deposit/pallas_call | solution.py:495
  44.6 1.9 %span_pass.2 = (f32[512,256]{1,0:T(8,128)S(1)}, f32[32,8,2,256]{3,2,1,0:T(2,128)}) custom-call(f32[512,256]{1,0:T(8,128)S(1)} %get-tuple-element.44.refs_2_.refs_0_, f32[192,256]{1,0:T(8,128)S(1)} %collective-permute-done.4.refs_1_, f32[192,256]{1,0:T(8,128)S(1)} %collective-permute-done.5.refs_2_, bf16[2,256,448]{2,1,0:T(8,128)(2,1)S(1)} %get-tuple-element.47.refs_3_, ...), custom_call_target="tpu_custom_call" | custom-call | bytes 4800000 | tf_op jit(solution)/shard_map/span_pass/pallas_call | solution.py:587
  46.5 5.8 %all-to-all-start.1 = ((f32[32,8,2,256]{3,2,1,0:T(2,128)}), f32[32,8,2,256]{3,2,1,0:T(2,128)}, u32[]{:S(2)}, u32[]{:S(2)}) async-start(f32[32,8,2,256]{3,2,1,0:T(2,128)} %get-tuple-element.50.refs_3_), calls=%async_computation.1 | async-start | bytes 1048576 | tf_op jit(solution)/shard_map/all_to_all | solution.py:647
  52.3 4.3 %deposit.7 = (f32[512,256]{1,0:T(8,128)S(1)}, f32[48,256]{1,0:T(8,128)S(1)}, f32[48,256]{1,0:T(8,128)S(1)}) custom-call(f32[8,28672]{1,0:T(8,128)S(1)} %get-tuple-element.38.refs_0_, f32[512,256]{1,0:T(8,128)S(1)} %deposit.6.refs_6_.refs_1_, bf16[2,256,256]{2,1,0:T(8,128)(2,1)S(1)} %get-tuple-element.39.refs_1_.refs_2_, ...), custom_call_target="tpu_custom_call" | custom-call | bytes 9600000 | tf_op jit(solution)/shard_map/deposit/pallas_call | solution.py:495
  57.1 1.4 %collective-permute-start.7 = (f32[48,256]{1,0:T(8,128)S(1)}, f32[48,256]{1,0:T(8,128)S(1)}, u32[]{:S(2)}, u32[]{:S(2)}) collective-permute-start(f32[48,256]{1,0:T(8,128)S(1)} %get-tuple-element.53), channel_id=1, source_target_pairs={{0,28},{4,8},{8,4},{12,16},{16,12},{20,24},{24,20},{28,0},{1,29},{... | collective-permute-start | bytes 147464 | tf_op jit(solution)/shard_map/ppermute | solution.py:608
  58.6 2.9 %collective-permute-done.7.second_in = f32[48,256]{1,0:T(8,128)S(1)} collective-permute-done((f32[48,256]{1,0:T(8,128)S(1)}, f32[48,256]{1,0:T(8,128)S(1)}, u32[]{:S(2)}, u32[]{:S(2)}) %collective-permute-start.7) | collective-permute-done | bytes 49184 | tf_op jit(solution)/shard_map/ppermute | solution.py:608
  62.0 2.2 %collective-permute-start.8 = (f32[192,256]{1,0:T(8,128)S(1)}, f32[192,256]{1,0:T(8,128)S(1)}, u32[]{:S(2)}, u32[]{:S(2)}) collective-permute-start(f32[192,256]{1,0:T(8,128)S(1)} %get-tuple-element.55), channel_id=1, source_target_pairs={{0,1},{1,0},{2,3},{3,2},{4,5},{5,4},{6,7},{7,6},{8,9},{9,8},{10,11... | collective-permute-start | bytes 589832 | tf_op jit(solution)/shard_map/ppermute | solution.py:608
  65.0 5.0 %collective-permute-done.8.refs_1_ = f32[192,256]{1,0:T(8,128)S(1)} collective-permute-done((f32[192,256]{1,0:T(8,128)S(1)}, f32[192,256]{1,0:T(8,128)S(1)}, u32[]{:S(2)}, u32[]{:S(2)}) %collective-permute-start.8) | collective-permute-done | bytes 196640 | tf_op jit(solution)/shard_map/ppermute | solution.py:608
  70.0 1.9 %span_pass.3 = (f32[512,256]{1,0:T(8,128)S(1)}, f32[32,8,2,256]{3,2,1,0:T(2,128)}) custom-call(f32[512,256]{1,0:T(8,128)S(1)} %get-tuple-element.54.refs_0_, f32[192,256]{1,0:T(8,128)S(1)} %collective-permute-done.8.refs_1_, f32[192,256]{1,0:T(8,128)S(1)} %collective-permute-done.9.refs_2_, bf16[2,256,448]{2,1,0:T(8,128)(2,1)S(1)} %get-tuple-element.47.refs_3_, ...), custom_call_target="tpu_custom_call" | custom-call | bytes 4800000 | tf_op jit(solution)/shard_map/span_pass/pallas_call | solution.py:587
  71.9 7.0 %all-to-all-start = ((f32[32,8,2,256]{3,2,1,0:T(2,128)}), f32[32,8,2,256]{3,2,1,0:T(2,128)S(1)}, u32[]{:S(2)}, u32[]{:S(2)}) async-start(f32[32,8,2,256]{3,2,1,0:T(2,128)} %get-tuple-element.58), calls=%async_computation | async-start | bytes 1048576 | tf_op jit(solution)/shard_map/all_to_all | solution.py:647
  79.0 1.0 %pad_maximum_fusion = f32[1024,256]{1,0:T(8,128)} fusion(f32[256,256]{1,0:T(8,128)S(1)} %get-tuple-element.60, f32[256,256]{1,0:T(8,128)S(1)} %get-tuple-element.62, f32[256,256]{1,0:T(8,128)S(1)} %get-tuple-element.61, f32[256,256]{1,0:T(8,128)S(1)} %get-tuple-element.59), kind=kLoop, calls=%fused_computation | loop fusion | flops 786432 | bytes 2097152 | tf_op jit(solution)/shard_map/concatenate | solution.py:661
  80.0 14.2 %all-to-all-done = f32[32,8,2,256]{3,2,1,0:T(2,128)S(1)} async-done(((f32[32,8,2,256]{3,2,1,0:T(2,128)}), f32[32,8,2,256]{3,2,1,0:T(2,128)S(1)}, u32[]{:S(2)}, u32[]{:S(2)}) %all-to-all-start) | async-done | bytes 524320 | tf_op jit(solution)/shard_map/all_to_all | solution.py:647
  94.2 2.5 %maximum_bitcast_fusion = f32[1,32,8,4,256]{4,3,2,1,0:T(4,128)} fusion(f32[32,8,2,256]{3,2,1,0:T(2,128)} %all-to-all-done.1, f32[32,8,2,256]{3,2,1,0:T(2,128)S(1)} %all-to-all-done), kind=kLoop, calls=%fused_computation.1 | loop fusion | flops 262144 | bytes 2097152 | tf_op jit(solution)/shard_map/broadcast_in_dim | solution.py:665
  (27 shorter events, 2.6 us)
Async XLA Ops:
  0.6 11.0 %copy-start = (f32[13,24576]{1,0:T(8,128)S(1)}, f32[13,24576]{1,0:T(8,128)}, u32[]{:S(2)}) copy-start(f32[13,24576]{1,0:T(8,128)} %grains_ref.1) | copy-start | bytes 3833860
  9.8 25.8 %copy-start.2 = (bf16[2,256,304]{2,1,0:T(8,128)(2,1)}, bf16[2,256,304]{2,1,0:T(8,128)(2,1)S(1)}, u32[]{:S(2)}) copy-start(bf16[2,256,304]{2,1,0:T(8,128)(2,1)S(1)} %get-tuple-element.43.operator_ref) | copy-start | bytes 933892
  9.8 34.7 %copy-start.4 = (bf16[256,256]{1,0:T(8,128)(2,1)}, bf16[256,256]{1,0:T(8,128)(2,1)S(1)}, u32[]{:S(2)}) copy-start(bf16[256,256]{1,0:T(8,128)(2,1)S(1)} %get-tuple-element.48.refs_4_) | copy-start | bytes 393220
  9.8 4.6 %collective-permute-start = (f32[13,2048]{1,0:T(8,128)S(1)}, f32[13,2048]{1,0:T(8,128)S(1)}, u32[]{:S(2)}, u32[]{:S(2)}) collective-permute-start(f32[13,2048]{1,0:T(8,128)S(1)} %get-tuple-element.35), channel_id=1, source_target_pairs={{0,4},{4,0},{8,12},{12,8},{16,20},{20,16},{24,28},{28,24},{1,5},{5... | collective-permute-start | bytes 319496 | tf_op jit(solution)/shard_map/ppermute | solution.py:608
  11.4 4.4 %collective-permute-start.1 = (f32[13,2048]{1,0:T(8,128)S(1)}, f32[13,2048]{1,0:T(8,128)S(1)}, u32[]{:S(2)}, u32[]{:S(2)}) collective-permute-start(f32[13,2048]{1,0:T(8,128)S(1)} %get-tuple-element.36), channel_id=1, source_target_pairs={{0,28},{4,8},{8,4},{12,16},{16,12},{20,24},{24,20},{28,0},{1,29},{... | collective-permute-start | bytes 319496 | tf_op jit(solution)/shard_map/ppermute | solution.py:608
  28.3 6.2 %collective-permute-start.2 = (f32[48,256]{1,0:T(8,128)S(1)}, f32[48,256]{1,0:T(8,128)S(1)}, u32[]{:S(2)}, u32[]{:S(2)}) collective-permute-start(f32[48,256]{1,0:T(8,128)S(1)} %get-tuple-element.41), channel_id=1, source_target_pairs={{0,4},{4,0},{8,12},{12,8},{16,20},{20,16},{24,28},{28,24},{1,5},{5... | collective-permute-start | bytes 147464 | tf_op jit(solution)/shard_map/ppermute | solution.py:608
  31.6 4.0 %collective-permute-start.3 = (f32[48,256]{1,0:T(8,128)S(1)}, f32[48,256]{1,0:T(8,128)S(1)}, u32[]{:S(2)}, u32[]{:S(2)}) collective-permute-start(f32[48,256]{1,0:T(8,128)S(1)} %get-tuple-element.42), channel_id=1, source_target_pairs={{0,28},{4,8},{8,4},{12,16},{16,12},{20,24},{24,20},{28,0},{1,29},{... | collective-permute-start | bytes 147464 | tf_op jit(solution)/shard_map/ppermute | solution.py:608
  35.6 9.0 %copy-start.1 = (f32[3,32,8,256]{3,2,1,0:T(8,128)S(1)}, f32[3,32,8,256]{3,2,1,0:T(8,128)}, u32[]{:S(2)}) copy-start(f32[3,32,8,256]{3,2,1,0:T(8,128)} %param.11) | copy-start | bytes 2359300
  36.2 8.3 %collective-permute-start.4 = (f32[192,256]{1,0:T(8,128)S(1)}, f32[192,256]{1,0:T(8,128)S(1)}, u32[]{:S(2)}, u32[]{:S(2)}) collective-permute-start(f32[192,256]{1,0:T(8,128)S(1)} %get-tuple-element.45), channel_id=1, source_target_pairs={{0,1},{1,0},{2,3},{3,2},{4,5},{5,4},{6,7},{7,6},{8,9},{9,8},{10,11... | collective-permute-start | bytes 589832 | tf_op jit(solution)/shard_map/ppermute | solution.py:608
  37.1 7.4 %collective-permute-start.5 = (f32[192,256]{1,0:T(8,128)S(1)}, f32[192,256]{1,0:T(8,128)S(1)}, u32[]{:S(2)}, u32[]{:S(2)}) collective-permute-start(f32[192,256]{1,0:T(8,128)S(1)} %get-tuple-element.46), channel_id=1, source_target_pairs={{1,2},{2,1},{5,6},{6,5},{9,10},{10,9},{13,14},{14,13},{17,18},{18,... | collective-permute-start | bytes 589832 | tf_op jit(solution)/shard_map/ppermute | solution.py:608
  46.5 25.5 %all-to-all-start.1 = ((f32[32,8,2,256]{3,2,1,0:T(2,128)}), f32[32,8,2,256]{3,2,1,0:T(2,128)}, u32[]{:S(2)}, u32[]{:S(2)}) async-start(f32[32,8,2,256]{3,2,1,0:T(2,128)} %get-tuple-element.50.refs_3_), calls=%async_computation.1 | async-start | bytes 1048576 | tf_op jit(solution)/shard_map/all_to_all | solution.py:647
  52.3 9.1 %copy-start.3 = (bf16[2,256,304]{2,1,0:T(8,128)(2,1)S(1)}, bf16[2,256,304]{2,1,0:T(8,128)(2,1)}, u32[]{:S(2)}) copy-start(bf16[2,256,304]{2,1,0:T(8,128)(2,1)} %copy-done.2) | copy-start | bytes 933892
  52.3 17.7 %copy-start.5 = (bf16[256,256]{1,0:T(8,128)(2,1)S(1)}, bf16[256,256]{1,0:T(8,128)(2,1)}, u32[]{:S(2)}) copy-start(bf16[256,256]{1,0:T(8,128)(2,1)} %copy-done.4) | copy-start | bytes 393220
  56.7 1.9 %collective-permute-start.6 = (f32[48,256]{1,0:T(8,128)S(1)}, f32[48,256]{1,0:T(8,128)S(1)}, u32[]{:S(2)}, u32[]{:S(2)}) collective-permute-start(f32[48,256]{1,0:T(8,128)S(1)} %get-tuple-element.52), channel_id=1, source_target_pairs={{0,4},{4,0},{8,12},{12,8},{16,20},{20,16},{24,28},{28,24},{1,5},{5... | collective-permute-start | bytes 147464 | tf_op jit(solution)/shard_map/ppermute | solution.py:608
  57.1 4.3 %collective-permute-start.7 = (f32[48,256]{1,0:T(8,128)S(1)}, f32[48,256]{1,0:T(8,128)S(1)}, u32[]{:S(2)}, u32[]{:S(2)}) collective-permute-start(f32[48,256]{1,0:T(8,128)S(1)} %get-tuple-element.53), channel_id=1, source_target_pairs={{0,28},{4,8},{8,4},{12,16},{16,12},{20,24},{24,20},{28,0},{1,29},{... | collective-permute-start | bytes 147464 | tf_op jit(solution)/shard_map/ppermute | solution.py:608
  62.0 7.9 %collective-permute-start.8 = (f32[192,256]{1,0:T(8,128)S(1)}, f32[192,256]{1,0:T(8,128)S(1)}, u32[]{:S(2)}, u32[]{:S(2)}) collective-permute-start(f32[192,256]{1,0:T(8,128)S(1)} %get-tuple-element.55), channel_id=1, source_target_pairs={{0,1},{1,0},{2,3},{3,2},{4,5},{5,4},{6,7},{7,6},{8,9},{9,8},{10,11... | collective-permute-start | bytes 589832 | tf_op jit(solution)/shard_map/ppermute | solution.py:608
  64.3 5.7 %collective-permute-start.9 = (f32[192,256]{1,0:T(8,128)S(1)}, f32[192,256]{1,0:T(8,128)S(1)}, u32[]{:S(2)}, u32[]{:S(2)}) collective-permute-start(f32[192,256]{1,0:T(8,128)S(1)} %get-tuple-element.56), channel_id=1, source_target_pairs={{1,2},{2,1},{5,6},{6,5},{9,10},{10,9},{13,14},{14,13},{17,18},{18,... | collective-permute-start | bytes 589832 | tf_op jit(solution)/shard_map/ppermute | solution.py:608
  71.9 22.3 %all-to-all-start = ((f32[32,8,2,256]{3,2,1,0:T(2,128)}), f32[32,8,2,256]{3,2,1,0:T(2,128)S(1)}, u32[]{:S(2)}, u32[]{:S(2)}) async-start(f32[32,8,2,256]{3,2,1,0:T(2,128)} %get-tuple-element.58), calls=%async_computation | async-start | bytes 1048576 | tf_op jit(solution)/shard_map/all_to_all | solution.py:647

commit v5 on v4

--- a/solution.py
+++ b/solution.py
@@ -16,7 +16,6 @@
 drag_rate = 0.25
 
 VMEM = pl.BlockSpec(memory_space=pltpu.VMEM)
-ANY = pl.BlockSpec(memory_space=pl.ANY)
 HBM = pl.BlockSpec(memory_space=pltpu.HBM)
 NT = (((1,), (1,)), ((), ()))
 NN = (((1,), (0,)), ((), ()))
@@ -152,7 +151,7 @@
     width = slots.shape[1]
     columns = rows_x * rows_y
     rows = max(LANES, 1 << (-(-slot_count // 8) - 1).bit_length())
-    run = 2 * LANES if width % (2 * LANES) == 0 else LANES
+    run = 4 * LANES if width % (4 * LANES) == 0 else LANES
     out = jax.ShapeDtypeStruct((records, width), jnp.float32)
     bf16 = jnp.bfloat16
     return pl.pallas_call(
@@ -227,22 +226,27 @@
 
     own = (columns, columns)
     target_y, target_x = split(lax.broadcasted_iota(jnp.int32, own, 0), rows_x)
+    row, source_x = split(lax.broadcasted_iota(jnp.int32, own, 1), rows_x)
+    source_y = jnp.where(row < REACH, row, jnp.where(row < 2 * REACH, row + rows_y - 2 * REACH, row - REACH))
+    put_operator(span_ref, 0, jnp.where(target_x == source_x, weights_at(target_y - source_y), 0.0))
+    side = (columns, 2 * REACH * rows_x)
+    target_y, target_x = split(lax.broadcasted_iota(jnp.int32, side, 0), rows_x)
+    row, source_x = split(lax.broadcasted_iota(jnp.int32, side, 1), rows_x)
+    source_y = jnp.where(row < REACH, row - REACH, row - REACH + rows_y)
+    put_operator(span_ref, columns, jnp.where(target_x == source_x, weights_at(target_y - source_y), 0.0))
+
+    target_x, target_y = split(lax.broadcasted_iota(jnp.int32, own, 0), rows_y)
     source_y, source_x = split(lax.broadcasted_iota(jnp.int32, own, 1), rows_x)
     put_operator(stream_ref, 0, jnp.where(target_y == source_y, weights_at(target_x - source_x), 0.0))
     side = (columns, 2 * REACH * rows_y)
-    target_y, target_x = split(lax.broadcasted_iota(jnp.int32, side, 0), rows_x)
+    target_x, target_y = split(lax.broadcasted_iota(jnp.int32, side, 0), rows_y)
     plane, source_y = split(lax.broadcasted_iota(jnp.int32, side, 1), rows_y)
     source_x = jnp.where(plane < REACH, plane - REACH, plane - REACH + rows_x)
     put_operator(stream_ref, columns, jnp.where(target_y == source_y, weights_at(target_x - source_x), 0.0))
 
-    target_x, target_y = split(lax.broadcasted_iota(jnp.int32, own, 0), rows_y)
-    source_y, source_x = split(lax.broadcasted_iota(jnp.int32, own, 1), rows_x)
-    put_operator(span_ref, 0, jnp.where(target_x == source_x, weights_at(target_y - source_y), 0.0))
-    side = (columns, 2 * REACH * rows_x)
-    target_x, target_y = split(lax.broadcasted_iota(jnp.int32, side, 0), rows_y)
-    row, source_x = split(lax.broadcasted_iota(jnp.int32, side, 1), rows_x)
-    source_y = jnp.where(row < REACH, row - REACH, row - REACH + rows_y)
-    put_operator(span_ref, columns, jnp.where(target_x == source_x, weights_at(target_y - source_y), 0.0))
+
+def row_of(y, rows_y):
+    return jnp.where(y < REACH, y, jnp.where(y < rows_y - REACH, y + REACH, y - (rows_y - 2 * REACH)))
 
 
 def keep_kernel(
@@ -284,7 +288,7 @@
     def place(cell):
         x, rest = split(cell, rows_y * depth)
         y, level = split(rest, depth)
-        return (y * rows_x + x).astype(jnp.float32), level.astype(jnp.float32)
+        return (row_of(y, rows_y) * rows_x + x).astype(jnp.float32), level.astype(jnp.float32)
 
     def keep(i, carry):
         lanes = lane_tile(i)
@@ -390,118 +394,79 @@
     )(*in_hbm(after), quant, first, second)
 
 
-def deposit_kernel(channels, rows_x, rows_y, chunk, span, begins, ends, direct, earlier, *refs):
-    refs = list(refs)
-    quant_ref = refs.pop(0)
-    partial_ref = None if begins else refs.pop(0)
-    depth_ref = refs.pop(0) if ends else None
-    del refs[:earlier]
-    field_ref = refs.pop(0)
-    first_ref, second_ref = (refs.pop(0), refs.pop(0)) if ends else (None, None)
-    total = refs.pop(-1)
-    begin, end = span
-    columns = rows_x * rows_y
-    depth = total.shape[1]
-    count = len(channels)
+def deposit_kernel(base, chunk, edges, quant_ref, depth_ref, *refs):
+    field_ref = refs[0]
+    left_a, left_b, right_a, right_b, total = refs[-5:]
+    channels = len(QUANT_ROW)
+    columns = field_ref.shape[0] // channels
+    depth = depth_ref.shape[1]
+    steps = quant_ref.shape[1] // chunk
     row16 = lax.broadcasted_iota(jnp.int32, (16, LANES), 0).astype(jnp.float32)
     zero = jnp.zeros((16, LANES), jnp.bfloat16)
     one = jnp.ones((16, LANES), jnp.bfloat16)
-    total[...] = jnp.zeros_like(total) if begins else partial_ref[...]
+    total[...] = jnp.zeros_like(total)
 
     def build(left, right, step):
         for j in range(chunk // LANES):
             here = slice(j * LANES, (j + 1) * LANES)
             lanes = pl.ds(pl.multiple_of(step * chunk + j * LANES, LANES), LANES)
-            parts = [wide(quant_ref[QUANT_ROW[c]:QUANT_ROW[c] + 1, lanes]) for c in channels]
+            parts = [wide(quant_ref[r:r + 1, lanes]) for r in QUANT_ROW]
             column = wide(quant_ref[COLUMN_ROW:COLUMN_ROW + 1, lanes])
             level = wide(quant_ref[LEVEL_ROW:LEVEL_ROW + 1, lanes])
             for k in range(columns // 16):
-                hit = (row16 + 16.0 * k).astype(jnp.bfloat16) == column
-                for c in range(count):
+                hit = (row16 + (base + 16.0 * k)).astype(jnp.bfloat16) == column
+                for c in range(channels):
                     left[c * columns + 16 * k:c * columns + 16 * k + 16, here] = jnp.where(hit, parts[c], zero)
             for k in range(depth // 16):
                 hit = (row16 + 16.0 * k).astype(jnp.bfloat16) == level
                 right[16 * k:16 * k + 16, here] = jnp.where(hit, one, zero)
 
-    def product(start, size):
-        lefts = [[] for _ in range(count * columns // 16)]
-        rights = [[] for _ in range(depth // 16)]
-        for j in range(size // LANES):
-            lanes = pl.ds(pl.multiple_of(start + j * LANES, LANES), LANES)
-            parts = [wide(quant_ref[QUANT_ROW[c]:QUANT_ROW[c] + 1, lanes]) for c in channels]
-            column = wide(quant_ref[COLUMN_ROW:COLUMN_ROW + 1, lanes])
-            level = wide(quant_ref[LEVEL_ROW:LEVEL_ROW + 1, lanes])
-            for k in range(columns // 16):
-                hit = (row16 + 16.0 * k).astype(jnp.bfloat16) == column
-                for c in range(count):
-                    lefts[c * columns // 16 + k].append(jnp.where(hit, parts[c], zero))
-            for k in range(depth // 16):
-                hit = (row16 + 16.0 * k).astype(jnp.bfloat16) == level
-                rights[k].append(jnp.where(hit, one, zero))
-        left = jnp.concatenate([jnp.concatenate(row, axis=1) for row in lefts], axis=0)
-        right = jnp.concatenate([jnp.concatenate(row, axis=1) for row in rights], axis=0)
-        return dot(left, right, NT)
-
-    if direct:
-
-        def one_step(i, carry):
-            total[...] += product(i * direct, direct)
-            return carry
-
-        lax.fori_loop(begin * chunk // direct, end * chunk // direct, one_step, 0)
-    else:
-        left_a, left_b, right_a, right_b = refs
-        build(left_a, right_a, begin)
-
-        def two(i, carry):
-            now = begin + 2 * i
-            build(left_b, right_b, now + 1)
-            total[...] += dot(left_a[...], right_a[...], NT)
-            build(left_a, right_a, jnp.minimum(now + 2, end - 1))
-            total[...] += dot(left_b[...], right_b[...], NT)
-            return carry
-
-        lax.fori_loop(0, (end - begin) // 2, two, 0)
-        if (end - begin) % 2:
-            total[...] += dot(left_a[...], right_a[...], NT)
-
-    if not ends:
-        field_ref[...] = total[...]
-        return
+    build(left_a, right_a, 0)
+
+    def two(i, carry):
+        now = 2 * i
+        build(left_b, right_b, now + 1)
+        total[...] += dot(left_a[...], right_a[...], NT)
+        build(left_a, right_a, jnp.minimum(now + 2, steps - 1))
+        total[...] += dot(left_b[...], right_b[...], NT)
+        return carry
+
+    lax.fori_loop(0, steps // 2, two, 0)
+    if steps % 2:
+        total[...] += dot(left_a[...], right_a[...], NT)
+
     high, low = halves(total[...])
     field_ref[...] = dot(high, depth_ref[0]) + (dot(high, depth_ref[1]) + dot(low, depth_ref[0]))
-    odd = is_odd("stream")
-    first_x = (1 - odd) * (rows_x - REACH)
-    second_x = odd * (rows_x - REACH)
-    for c in range(count):
-        for k in range(REACH):
-            for y in range(rows_y):
-                to = (c * REACH + k) * rows_y + y
-                row = c * columns + y * rows_x + k
-                first_ref[to:to + 1, :] = field_ref[pl.ds(row + first_x, 1), :]
-                second_ref[to:to + 1, :] = field_ref[pl.ds(row + second_x, 1), :]
-
-
-def deposit(channels, rows_x, rows_y, depth, chunk, span, direct, quant, partial, depth_op, earlier):
-    columns = rows_x * rows_y
-    count = len(channels)
-    begins, ends = partial is None, depth_op is not None
-    field = jax.ShapeDtypeStruct((count * columns, depth), jnp.float32)
-    halo = jax.ShapeDtypeStruct((count * REACH * rows_y, depth), jnp.float32)
-    operands = [quant] + ([] if begins else [partial]) + ([depth_op] if ends else [])
-    outs = (field, halo, halo) if ends else (field,)
-    left = pltpu.VMEM((count * columns, chunk), jnp.bfloat16)
+    if edges:
+        first_ref, second_ref = refs[1:3]
+        edge = columns // 2
+        odd = is_odd("span")
+        for c in range(channels):
+            to = slice(c * edge, (c + 1) * edge)
+            front = c * columns + (1 - odd) * edge
+            back = c * columns + odd * edge
+            first_ref[to, :] = field_ref[pl.ds(pl.multiple_of(front, 8), edge), :]
+            second_ref[to, :] = field_ref[pl.ds(pl.multiple_of(back, 8), edge), :]
+
+
+def deposit(base, columns, chunk, edges, quant, depth_op):
+    depth = depth_op.shape[1]
+    channels = len(QUANT_ROW)
+    field = jax.ShapeDtypeStruct((channels * columns, depth), jnp.float32)
+    edge = jax.ShapeDtypeStruct((channels * columns // 2, depth), jnp.float32)
+    outs = (field, edge, edge) if edges else (field,)
+    left = pltpu.VMEM((channels * columns, chunk), jnp.bfloat16)
     right = pltpu.VMEM((depth, chunk), jnp.bfloat16)
     return pl.pallas_call(
-        functools.partial(deposit_kernel, channels, rows_x, rows_y, chunk, span, begins, ends, direct, len(earlier)),
+        functools.partial(deposit_kernel, base, chunk, edges),
         out_shape=outs,
-        in_specs=[VMEM] * len(operands) + [ANY] * len(earlier),
+        in_specs=[VMEM, VMEM],
         out_specs=(VMEM,) * len(outs),
-        scratch_shapes=([] if direct else [left, left, right, right]) + [pltpu.VMEM(field.shape, jnp.float32)],
+        scratch_shapes=[left, left, right, right, pltpu.VMEM(field.shape, jnp.float32)],
         compiler_params=params(20),
-        cost_estimate=cost(0.4 * count * (span[1] - span[0])),
+        cost_estimate=cost(columns * 0.09),
         name="deposit",
-    )(*operands, *earlier)
+    )(quant, depth_op)
 
 
 def mix(operator_ref, pieces):
@@ -523,79 +488,84 @@
     return jnp.concatenate([jnp.where(odd, first, second), jnp.where(odd, second, first)], axis=0)
 
 
-def stream_kernel(count, own_ref, first_in, second_in, operator_ref, *refs):
-    field_ref, first_ref, second_ref = refs[-3:]
-    columns = own_ref.shape[0] // count
-    halo = first_in.shape[0] // count
-    edge = first_ref.shape[0] // count
-    odd = is_odd("span") == 1
-    for c in range(count):
+def span_kernel(rows_x, rows_y, edge_ref, inner_ref, first_in, second_in, operator_ref, field_ref, first_ref, second_ref):
+    channels = len(QUANT_ROW)
+    columns = rows_x * rows_y
+    outer = edge_ref.shape[0] // channels
+    inner = inner_ref.shape[0] // channels
+    halo = first_in.shape[0] // channels
+    odd = is_odd("stream")
+    first_x = (1 - odd) * (rows_x - REACH)
+    second_x = odd * (rows_x - REACH)
+    for c in range(channels):
+        own = [edge_ref[c * outer:(c + 1) * outer, :], inner_ref[c * inner:(c + 1) * inner, :]]
+        side = slice(c * halo, (c + 1) * halo)
+        own = jnp.concatenate(own, axis=0)
+        value = mix(operator_ref, [own, sides("span", first_in[side, :], second_in[side, :])])
+        field_ref[c * columns:(c + 1) * columns, :] = value
+    for c in range(channels):
+        for k in range(REACH):
+            for y in range(rows_y):
+                to = (c * REACH + k) * rows_y + y
+                row = c * columns + y * rows_x + k
+                first_ref[to:to + 1, :] = field_ref[pl.ds(row + first_x, 1), :]
+                second_ref[to:to + 1, :] = field_ref[pl.ds(row + second_x, 1), :]
+
+
+def span_pass(rows_x, rows_y, edge, inner, first, second, operator):
+    channels = len(QUANT_ROW)
+    depth = edge.shape[1]
+    halo = jax.ShapeDtypeStruct((channels * REACH * rows_y, depth), jnp.float32)
+    return pl.pallas_call(
+        functools.partial(span_kernel, rows_x, rows_y),
+        out_shape=(jax.ShapeDtypeStruct((channels * rows_x * rows_y, depth), jnp.float32), halo, halo),
+        in_specs=[VMEM] * 5,
+        out_specs=(VMEM,) * 3,
+        compiler_params=params(12),
+        cost_estimate=cost(1.5),
+        name="span_pass",
+    )(edge, inner, first, second, operator)
+
+
+def stream_kernel(rows_q, own_ref, first_in, second_in, operator_ref, choose_ref, fluid_ref, solid_ref, out_ref):
+    channels = len(QUANT_ROW)
+    columns = own_ref.shape[0] // channels
+    halo = first_in.shape[0] // channels
+    choose = choose_ref[...]
+    base = None
+    for c in range(channels):
         own = slice(c * columns, (c + 1) * columns)
         side = slice(c * halo, (c + 1) * halo)
-        value = mix(operator_ref, [own_ref[own, :], sides("stream", first_in[side, :], second_in[side, :])])
-        field_ref[own, :] = value
-        low, high = value[0:edge], value[columns - edge:columns]
-        first_ref[c * edge:(c + 1) * edge, :] = jnp.where(odd, low, high)
-        second_ref[c * edge:(c + 1) * edge, :] = jnp.where(odd, high, low)
-
-
-def stream_pass(count, rows_x, own, first, second, operator, earlier):
-    edge = jax.ShapeDtypeStruct((count * REACH * rows_x, own.shape[1]), jnp.float32)
-    return pl.pallas_call(
-        functools.partial(stream_kernel, count),
-        out_shape=(jax.ShapeDtypeStruct(own.shape, jnp.float32), edge, edge),
-        in_specs=[VMEM] * 4 + [ANY] * len(earlier),
-        out_specs=(VMEM,) * 3,
-        compiler_params=params(12),
-        cost_estimate=cost(0.4 * count),
-        name="stream_pass",
-    )(own, first, second, operator, *earlier)
-
-
-def span_kernel(channels, rows_q, *refs):
-    refs = list(refs)
-    own_ref, first_in, second_in, operator_ref, choose_ref, fluid_ref = refs[:6]
-    base_ref = None if 0 in channels else refs[6]
-    solid_ref, out_ref = refs[-2:]
-    count = len(channels)
-    columns = own_ref.shape[0] // count
-    edge = first_in.shape[0] // count
-    choose = choose_ref[...]
-    solids = {}
-    for n, c in enumerate(channels):
-        own = slice(n * columns, (n + 1) * columns)
-        side = slice(n * edge, (n + 1) * edge)
-        value = mix(operator_ref, [own_ref[own, :], sides("span", first_in[side, :], second_in[side, :])])
-        solid_ref[own, :] = value
-        solids[c] = value
-    base = solids[0] if base_ref is None else base_ref[0:columns, :]
-    for n, c in enumerate(channels):
+        solid = mix(operator_ref, [own_ref[own, :], sides("stream", first_in[side, :], second_in[side, :])])
+        solid_ref[own, :] = solid
         if c == 0:
+            base = solid
             value = 1.0 / (1.0 + base)
         else:
             flow = fluid_ref[(c - 1) * columns:c * columns, :]
-            value = flow + drag_rate * (solids[c] - base * flow)
+            value = flow + drag_rate * (solid - base * flow)
         first, rest = halves(value)
         second, third = halves(value - first.astype(jnp.float32))
         sent = dot(choose, first) + (dot(choose, second) + dot(choose, third))
-        out_ref[:, :, count - 1 - n, :] = sent.reshape(sent.shape[0] // rows_q, rows_q, -1)
-
-
-def span_pass(channels, own, first, second, operator, choose, fluid, base, peers, rows_q, earlier):
-    count = len(channels)
-    operands = [own, first, second, operator, choose, fluid] + ([] if base is None else [base])
+        place = (c - 1) % channels
+        out_ref[:, :, place, :] = sent.reshape(sent.shape[0] // rows_q, rows_q, -1)
+
+
+def stream_pass(peers, rows_q, own, first, second, operator, choose, fluid):
+    channels = len(QUANT_ROW)
+    depth = own.shape[1]
     return pl.pallas_call(
-        functools.partial(span_kernel, channels, rows_q),
+        functools.partial(stream_kernel, rows_q),
         out_shape=(
             jax.ShapeDtypeStruct(own.shape, jnp.float32),
-            jax.ShapeDtypeStruct((peers, rows_q, count, own.shape[1]), jnp.float32),
+            jax.ShapeDtypeStruct((peers, rows_q, channels, depth), jnp.float32),
         ),
-        in_specs=[VMEM] * len(operands) + [ANY] * len(earlier),
+        in_specs=[VMEM] * 6,
         out_specs=(VMEM, VMEM),
         compiler_params=params(16),
-        cost_estimate=cost(0.8 * count),
-        name="span_pass",
-    )(*operands, *earlier)
+        cost_estimate=cost(3.5),
+        name="stream_pass",
+    )(own, first, second, operator, choose, fluid)
 
 
 def swap(first, second, axis, periodic):
@@ -605,7 +575,8 @@
     others = [(source, (source + 1 if source % 2 else source - 1) % count) for source in range(count)]
     if not periodic:
         others = [pair for pair in others if abs(pair[0] - pair[1]) == 1]
-    return lax.ppermute(first, axis, pairs), lax.ppermute(second, axis, others)
+    second = lax.ppermute(second, axis, others)
+    return lax.ppermute(first, axis, pairs), second
 
 
 def per_device(grains, send_slots, send_counts, cell_index, fluid, block_slots, block_counts):
@@ -625,44 +596,17 @@
     grains_after, quant = join(after, quant, *arrived)
 
     chunk = math.gcd(total, 2048)
-    steps = total // chunk
-    early = steps // 4
-    middle = steps * 5 // 7
-    flow = fluid.reshape(3 * columns, depth)
-
-    def add(channels, span, direct, partial, last, earlier=()):
-        return deposit(
-            channels, rows_x, rows_y, depth, chunk, span, direct, quant, partial, depth_op if last else None, earlier
-        )
-
-    def stream(field, first, second, earlier):
-        halos = swap(first, second, "stream", True)
-        return stream_pass(field.shape[0] // columns, rows_x, field, *halos, stream_op, earlier)
-
-    def span(channels, field, first, second, base, earlier):
-        halos = swap(first, second, "span", False)
-        return span_pass(channels, field, *halos, span_op, choose, flow, base, peers, rows_q, earlier)
-
-    def exchange(outgoing):
-        return lax.all_to_all(outgoing, axes, split_axis=0, concat_axis=0, tiled=True)
-
-    direct = chunk // 2
-    outer = add((0, 3), (0, steps), 0, None, True)
-    (inner,) = add((2, 1), (0, early), direct, None, False)
-    outer = stream(*outer, (inner,))
-    (inner,) = add((2, 1), (early, middle), direct, inner, False, outer[:1])
-    solid_outer, outgoing = span((0, 3), *outer, None, (inner,))
-    arrived_outer = exchange(outgoing)
-    inner = add((2, 1), (middle, steps), direct, inner, True, (outgoing,))
-    inner = stream(*inner, ())
-    solid_inner, outgoing = span((2, 1), *inner, solid_outer, ())
-    arrived_inner = exchange(outgoing)
-
-    solid = jnp.concatenate(
-        [solid_outer[:columns], solid_inner[columns:], solid_inner[:columns], solid_outer[columns:]], axis=0
-    ).reshape(4, rows_x, rows_y, depth)
-    received = jnp.concatenate([arrived_inner, arrived_outer], axis=2)
-    return grains_after, solid, received[None]
+    faces = 2 * REACH * rows_x
+    edge, first, second = deposit(0, faces, chunk, True, quant, depth_op)
+    first, second = swap(first, second, "span", False)
+    (inner,) = deposit(faces, columns - faces, chunk, False, quant, depth_op)
+    field, *halos = span_pass(rows_x, rows_y, edge, inner, first, second, span_op)
+    halos = swap(*halos, "stream", True)
+    solid, outgoing = stream_pass(
+        peers, rows_q, field, *halos, stream_op, choose, fluid.reshape(3 * columns, depth)
+    )
+    arrived = lax.all_to_all(outgoing, axes, split_axis=0, concat_axis=0, tiled=True)
+    return grains_after, solid.reshape(4, rows_x, rows_y, depth), arrived[None]
 
 
 def solution(mesh):

time: 97.1 us -> 92 us (0.947)
  blocking collectives: 0 us -> 34.8 us
  waiting for transfers between devices: 24.6 us -> 4.29 us
  starting transfers between devices: 24.2 us -> 8.94 us
  other arithmetic: 3.56 us -> 0 us
    all_to_all x0 -> x1, blocking collectives: none -> 34.8 us  [per_device(): lax.all_to_all(outgoing, axes, split_axis=0, concat_axis=0, tiled=True)]
    all_to_all x2 -> x0, waiting for transfers between devices: 14.2 us -> none  [exchange(): lax.all_to_all(outgoing, axes, split_axis=0, concat_axis=0, tiled=True)]
    all_to_all x2 -> x0, starting transfers between devices: 12.8 us -> none  [exchange(): lax.all_to_all(outgoing, axes, split_axis=0, concat_axis=0, tiled=True)]
    ppermute x10 -> x6, waiting for transfers between devices: 10.4 us -> 4.29 us  [the longest x3 4.1 us: swap(): second = lax.ppermute(second, axis, others)]
    broadcast_in_dim x1 -> x0, other arithmetic: 2.52 us -> none  [per_device(): return (grains_after, solid, received[None])]
    ppermute x10 -> x6, starting transfers between devices: 11.4 us -> 8.94 us  [the longest x3 4.82 us: swap(): return (lax.ppermute(first, axis, pairs), second)]
    pallas_call x8 -> x4, Pallas kernels: 30.8 us -> 29.6 us  [the longest x2 24.6 us: deposit(): pl.pallas_call(functools.partial(deposit_kernel, base, chunk, edges), out...]
    concatenate x1 -> x0, other arithmetic: 1.04 us -> none  [per_device(): jnp.concatenate([solid_outer[:columns], solid_inner[columns:], solid_inne...]
  transfers between devices with their start and end apart: 12 -> 6, of which waited for: 5 -> 2; matrix products, arithmetic and copies ran while one was open for 1% -> 0% of each run, Pallas kernels for 20% -> 13%
where the time goes in v5:
time: 92 us; the launch traced here: 92.6 us
  Pallas kernels  42.8 us (47%)
  blocking collectives  34.8 us (38%)
  starting transfers between devices  8.94 us (10%)
  waiting for transfers between devices  4.29 us (5%)
  local copies, waits for them, and re-layouts  0.98 us (1%)
    all_to_all x1, blocking collectives, per_device(): lax.all_to_all(outgoing, axes, split_axis=0, concat_axis=0, tiled=True)  34.8 us
    pallas_call x2, Pallas kernels, deposit(): pl.pallas_call(functools.partial(deposit_kernel, base, chunk, edges), out...  24.6 us
    pallas_call x1, Pallas kernels, leave(): pl.pallas_call(functools.partial(leave_kernel, rows_x, rows_y), out_shape...  9.56 us
    ppermute x3, starting transfers between devices, swap(): return (lax.ppermute(first, axis, pairs), second)  4.82 us
    ppermute x3, starting transfers between devices, swap(): second = lax.ppermute(second, axis, others)  4.12 us
    ppermute x3, waiting for transfers between devices, swap(): second = lax.ppermute(second, axis, others)  4.1 us
    pallas_call x1, Pallas kernels, stream_pass(): pl.pallas_call(functools.partial(stream_kernel, rows_q), out_shape=(jax.S...  3.77 us
    pallas_call x1, Pallas kernels, keep(): pl.pallas_call(functools.partial(keep_kernel, rows_x, rows_y, depth), out...  2.92 us
  transfers between devices with their start and end apart: 6, of which 2 were waited for; matrix products, arithmetic and copies ran while one was open for 0% of the time, Pallas kernels for 13%

profile of v5, /device:TPU:1, one launch (start us, length us, event | category | flops | bytes accessed | tf_op | source)
XLA Modules:
  0.0 92.6 jit_solution(2864740441112665211)
XLA Ops:
  0.6 0.0 copy-start
  0.6 9.6 %leave.1 = (f32[13,2048]{1,0:T(8,128)S(1)}, f32[13,2048]{1,0:T(8,128)S(1)}, bf16[2,256,256]{2,1,0:T(8,128)(2,1)S(1)}, bf16[2,256,304]{2,1,0:T(8,128)(2,1)S(1)}, ...) custom-call(f32[13,24576]{1,0:T(8,128)} %grains_ref.1, ...), custom_call_target="tpu_custom_call" | custom-call | bytes 24000000 | tf_op jit(solution)/shard_map/leave/pallas_call | solution.py:157
  10.2 1.5 %collective-permute-start = (f32[13,2048]{1,0:T(8,128)S(1)}, f32[13,2048]{1,0:T(8,128)S(1)}, u32[]{:S(2)}, u32[]{:S(2)}) collective-permute-start(f32[13,2048]{1,0:T(8,128)S(1)} %get-tuple-element.27), channel_id=1, source_target_pairs={{0,4},{4,0},{8,12},{12,8},{16,20},{20,16},{24,28},{28,24},{1,5},{5... | collective-permute-start | bytes 319496 | tf_op jit(solution)/shard_map/ppermute | solution.py:579
  11.7 2.4 %collective-permute-start.1 = (f32[13,2048]{1,0:T(8,128)S(1)}, f32[13,2048]{1,0:T(8,128)S(1)}, u32[]{:S(2)}, u32[]{:S(2)}) collective-permute-start(f32[13,2048]{1,0:T(8,128)S(1)} %get-tuple-element.28), channel_id=1, source_target_pairs={{0,28},{4,8},{8,4},{12,16},{16,12},{20,24},{24,20},{28,0},{1,29},{... | collective-permute-start | bytes 319496 | tf_op jit(solution)/shard_map/ppermute | solution.py:578
  14.1 0.0 copy-done
  14.1 2.9 %keep.1 = (f32[13,28672]{1,0:T(8,128)}, f32[8,28672]{1,0:T(8,128)S(1)}) custom-call(f32[13,24576]{1,0:T(8,128)S(1)} %copy-done, s32[2,2048]{1,0:T(2,128)S(1)} %get-tuple-element.23.marks_ref, s32[1,28672]{1,0:T(1,128)S(1)} %get-tuple-element.24.cells_ref), custom_call_target="tpu_custom_call" | custom-call | bytes 12000000 | tf_op jit(solution)/shard_map/keep/pallas_call | solution.py:333
  17.0 0.0 collective-permute-done.first_ref
  17.1 0.0 collective-permute-done.1.second_ref
  17.1 0.7 join.1
  17.8 15.8 %deposit.2 = (f32[768,256]{1,0:T(8,128)S(1)}, f32[384,256]{1,0:T(8,128)S(1)}, f32[384,256]{1,0:T(8,128)S(1)}) custom-call(f32[8,28672]{1,0:T(8,128)S(1)} %get-tuple-element.30.quant_ref, bf16[2,256,256]{2,1,0:T(8,128)(2,1)S(1)} %get-tuple-element.31.depth_ref), custom_call_target="tpu_custom_call" | custom-call | bytes 51840000 | tf_op jit(solution)/shard_map/deposit/pallas_call | solution.py:460
  33.6 2.3 %collective-permute-start.2 = (f32[384,256]{1,0:T(8,128)S(1)}, f32[384,256]{1,0:T(8,128)S(1)}, u32[]{:S(2)}, u32[]{:S(2)}) collective-permute-start(f32[384,256]{1,0:T(8,128)S(1)} %get-tuple-element.33), channel_id=1, source_target_pairs={{0,1},{1,0},{2,3},{3,2},{4,5},{5,4},{6,7},{7,6},{8,9},{9,8},{10,11... | collective-permute-start | bytes 1179656 | tf_op jit(solution)/shard_map/ppermute | solution.py:579
  35.9 1.0 %collective-permute-start.3 = (f32[384,256]{1,0:T(8,128)S(1)}, f32[384,256]{1,0:T(8,128)S(1)}, u32[]{:S(2)}, u32[]{:S(2)}) collective-permute-start(f32[384,256]{1,0:T(8,128)S(1)} %get-tuple-element.34), channel_id=1, source_target_pairs={{1,2},{2,1},{5,6},{6,5},{9,10},{10,9},{13,14},{14,13},{17,18},{18,... | collective-permute-start | bytes 1179656 | tf_op jit(solution)/shard_map/ppermute | solution.py:578
  36.9 8.8 %deposit.3.inner_ref = f32[256,256]{1,0:T(8,128)S(1)} custom-call(f32[8,28672]{1,0:T(8,128)S(1)} %get-tuple-element.30.quant_ref, bf16[2,256,256]{2,1,0:T(8,128)(2,1)S(1)} %get-tuple-element.31.depth_ref), custom_call_target="tpu_custom_call" | custom-call | bytes 17280000 | tf_op jit(solution)/shard_map/deposit/pallas_call | solution.py:460
  45.7 0.0 collective-permute-done.2.first_in
  45.7 0.0 collective-permute-done.3.second_in
  45.8 1.2 %span_pass.1 = (f32[1024,256]{1,0:T(8,128)S(1)}, f32[96,256]{1,0:T(8,128)S(1)}, f32[96,256]{1,0:T(8,128)S(1)}) custom-call(f32[768,256]{1,0:T(8,128)S(1)} %get-tuple-element.32.edge_ref, f32[256,256]{1,0:T(8,128)S(1)} %deposit.3.inner_ref, f32[384,256]{1,0:T(8,128)S(1)} %collective-permute-done.2.first_in, f32[384,256]{1,0:T(8,128)S(1)} %collective-permute-done.3.second_in, ...), custom_call_target="tpu_custom_call" | custom-call | bytes 4500000 | tf_op jit(solution)/shard_map/span_pass/pallas_call | solution.py:519
  47.0 1.0 %collective-permute-start.4 = (f32[96,256]{1,0:T(8,128)S(1)}, f32[96,256]{1,0:T(8,128)S(1)}, u32[]{:S(2)}, u32[]{:S(2)}) collective-permute-start(f32[96,256]{1,0:T(8,128)S(1)} %get-tuple-element.37), channel_id=1, source_target_pairs={{0,4},{4,0},{8,12},{12,8},{16,20},{20,16},{24,28},{28,24},{1,5},{5... | collective-permute-start | bytes 294920 | tf_op jit(solution)/shard_map/ppermute | solution.py:579
  48.0 0.8 collective-permute-start.5
  48.8 0.2 collective-permute-done.4.first_in
  48.9 4.1 %collective-permute-done.5.second_in = f32[96,256]{1,0:T(8,128)S(1)} collective-permute-done((f32[96,256]{1,0:T(8,128)S(1)}, f32[96,256]{1,0:T(8,128)S(1)}, u32[]{:S(2)}, u32[]{:S(2)}) %collective-permute-start.5) | collective-permute-done | bytes 98336 | tf_op jit(solution)/shard_map/ppermute | solution.py:578
  53.0 0.0 copy-done.1
  53.0 3.8 %stream_pass.1 = (f32[1024,256]{1,0:T(8,128)}, f32[32,8,4,256]{3,2,1,0:T(4,128)S(1)}) custom-call(f32[1024,256]{1,0:T(8,128)S(1)} %get-tuple-element.36.own_ref, f32[96,256]{1,0:T(8,128)S(1)} %collective-permute-done.4.first_in, f32[96,256]{1,0:T(8,128)S(1)} %collective-permute-done.5.second_in, bf16[2,256,304]{2,1,0:T(8,128)(2,1)S(1)} %get-tuple-element.39.operator_ref, ...), custom_call_target="tpu_custom_call" | custom-call | bytes 10500000 | tf_op jit(solution)/shard_map/stream_pass/pallas_call | solution.py:557
  56.8 34.8 %all_to_all.5 = f32[32,8,4,256]{3,2,1,0:T(4,128)S(1)} all-to-all(f32[32,8,4,256]{3,2,1,0:T(4,128)S(1)} %get-tuple-element.42), channel_id=1, replica_groups=mesh['stream'=8,'span'=4] {'stream','span'}, dimensions={0} | all-to-all | bytes 2097152 | tf_op jit(solution)/shard_map/all_to_all | solution.py:608
  91.6 1.0 %copy.15 = f32[1,32,8,4,256]{4,3,2,1,0:T(4,128)} copy(f32[1,32,8,4,256]{4,3,2,1,0:T(4,128)S(1)} %bitcast.9) | data formatting | bytes 2097152
  (1 shorter events, 0.0 us)
Async XLA Ops:
  0.6 13.5 %copy-start = (f32[13,24576]{1,0:T(8,128)S(1)}, f32[13,24576]{1,0:T(8,128)}, u32[]{:S(2)}) copy-start(f32[13,24576]{1,0:T(8,128)} %grains_ref.1) | copy-start | bytes 3833860
  10.2 6.8 %collective-permute-start = (f32[13,2048]{1,0:T(8,128)S(1)}, f32[13,2048]{1,0:T(8,128)S(1)}, u32[]{:S(2)}, u32[]{:S(2)}) collective-permute-start(f32[13,2048]{1,0:T(8,128)S(1)} %get-tuple-element.27), channel_id=1, source_target_pairs={{0,4},{4,0},{8,12},{12,8},{16,20},{20,16},{24,28},{28,24},{1,5},{5... | collective-permute-start | bytes 319496 | tf_op jit(solution)/shard_map/ppermute | solution.py:579
  11.7 5.3 %collective-permute-start.1 = (f32[13,2048]{1,0:T(8,128)S(1)}, f32[13,2048]{1,0:T(8,128)S(1)}, u32[]{:S(2)}, u32[]{:S(2)}) collective-permute-start(f32[13,2048]{1,0:T(8,128)S(1)} %get-tuple-element.28), channel_id=1, source_target_pairs={{0,28},{4,8},{8,4},{12,16},{16,12},{20,24},{24,20},{28,0},{1,29},{... | collective-permute-start | bytes 319496 | tf_op jit(solution)/shard_map/ppermute | solution.py:578
  33.6 12.1 %collective-permute-start.2 = (f32[384,256]{1,0:T(8,128)S(1)}, f32[384,256]{1,0:T(8,128)S(1)}, u32[]{:S(2)}, u32[]{:S(2)}) collective-permute-start(f32[384,256]{1,0:T(8,128)S(1)} %get-tuple-element.33), channel_id=1, source_target_pairs={{0,1},{1,0},{2,3},{3,2},{4,5},{5,4},{6,7},{7,6},{8,9},{9,8},{10,11... | collective-permute-start | bytes 1179656 | tf_op jit(solution)/shard_map/ppermute | solution.py:579
  35.9 17.2 %copy-start.1 = (f32[3,32,8,256]{3,2,1,0:T(8,128)S(1)}, f32[3,32,8,256]{3,2,1,0:T(8,128)}, u32[]{:S(2)}) copy-start(f32[3,32,8,256]{3,2,1,0:T(8,128)} %param.11) | copy-start | bytes 2359300
  35.9 9.9 %collective-permute-start.3 = (f32[384,256]{1,0:T(8,128)S(1)}, f32[384,256]{1,0:T(8,128)S(1)}, u32[]{:S(2)}, u32[]{:S(2)}) collective-permute-start(f32[384,256]{1,0:T(8,128)S(1)} %get-tuple-element.34), channel_id=1, source_target_pairs={{1,2},{2,1},{5,6},{6,5},{9,10},{10,9},{13,14},{14,13},{17,18},{18,... | collective-permute-start | bytes 1179656 | tf_op jit(solution)/shard_map/ppermute | solution.py:578
  47.0 1.9 %collective-permute-start.4 = (f32[96,256]{1,0:T(8,128)S(1)}, f32[96,256]{1,0:T(8,128)S(1)}, u32[]{:S(2)}, u32[]{:S(2)}) collective-permute-start(f32[96,256]{1,0:T(8,128)S(1)} %get-tuple-element.37), channel_id=1, source_target_pairs={{0,4},{4,0},{8,12},{12,8},{16,20},{20,16},{24,28},{28,24},{1,5},{5... | collective-permute-start | bytes 294920 | tf_op jit(solution)/shard_map/ppermute | solution.py:579
  48.0 5.0 %collective-permute-start.5 = (f32[96,256]{1,0:T(8,128)S(1)}, f32[96,256]{1,0:T(8,128)S(1)}, u32[]{:S(2)}, u32[]{:S(2)}) collective-permute-start(f32[96,256]{1,0:T(8,128)S(1)} %get-tuple-element.38), channel_id=1, source_target_pairs={{0,28},{4,8},{8,4},{12,16},{16,12},{20,24},{24,20},{28,0},{1,29},{... | collective-permute-start | bytes 294920 | tf_op jit(solution)/shard_map/ppermute | solution.py:578

commit v6 on v5

--- a/solution.py
+++ b/solution.py
@@ -110,19 +110,28 @@
     run = picked.shape[0]
     lane = lax.broadcasted_iota(jnp.int32, (8, LANES), 1)
     odd = is_odd("stream")
-    for which, out_ref in ((odd, first_ref), (1 - odd, second_ref)):
+    for which in (0, 1):
         live_count = counts_s[0, which]
+
+        def put(lanes, rows_to, value):
+            @pl.when(odd == which)
+            def _():
+                first_ref[rows_to, lanes] = value
+
+            @pl.when(odd != which)
+            def _():
+                second_ref[rows_to, lanes] = value
 
         def gather(i, carry):
             base = i * run
             for k in range(run):
                 row = lax.bitwise_and(slots_s[which, base + k], rows - 1)
                 picked[k:k + 1, :] = table[pl.ds(row, 1), :]
+            heads, rests = [], []
             for piece in range(run // LANES):
                 lanes = pl.ds(pl.multiple_of(base + piece * LANES, LANES), LANES)
                 turned = jnp.transpose(picked[piece * LANES:(piece + 1) * LANES, :])
-                slot = jnp.where(which == 0, slots_v[0:1, lanes], slots_v[1:2, lanes])
-                slot = jnp.broadcast_to(slot, (8, LANES))
+                slot = jnp.broadcast_to(slots_v[which:which + 1, lanes], (8, LANES))
                 part_of = lax.shift_right_logical(slot, rows.bit_length() - 1)
                 live = lane + (base + piece * LANES) < live_count
                 first = jnp.zeros((8, LANES), jnp.float32)
@@ -131,8 +140,11 @@
                     hit = jnp.logical_and(live, part_of == part)
                     first = jnp.where(hit, turned[part * RECORD:part * RECORD + 8], first)
                     second = jnp.where(hit, turned[part * RECORD + 8:part * RECORD + 16], second)
-                out_ref[0:8, lanes] = first
-                out_ref[8:records, lanes] = second[0:records - 8]
+                heads.append(first)
+                rests.append(second[0:records - 8])
+            lanes = pl.ds(pl.multiple_of(base, LANES), run)
+            put(lanes, slice(0, 8), jnp.concatenate(heads, axis=1))
+            put(lanes, slice(8, records), jnp.concatenate(rests, axis=1))
             return carry
 
         used = lax.div(live_count + (run - 1), run)
@@ -140,7 +152,7 @@
 
         def blank(i, carry):
             lanes = pl.ds(pl.multiple_of(i * run, LANES), run)
-            out_ref[:, lanes] = jnp.zeros((records, run), jnp.float32)
+            put(lanes, slice(0, records), jnp.zeros((records, run), jnp.float32))
             return carry
 
         lax.fori_loop(used, width // run, blank, 0)
@@ -151,7 +163,7 @@
     width = slots.shape[1]
     columns = rows_x * rows_y
     rows = max(LANES, 1 << (-(-slot_count // 8) - 1).bit_length())
-    run = 4 * LANES if width % (4 * LANES) == 0 else LANES
+    run = 2 * LANES if width % (2 * LANES) == 0 else LANES
     out = jax.ShapeDtypeStruct((records, width), jnp.float32)
     bf16 = jnp.bfloat16
     return pl.pallas_call(
@@ -402,8 +414,10 @@
     depth = depth_ref.shape[1]
     steps = quant_ref.shape[1] // chunk
     row16 = lax.broadcasted_iota(jnp.int32, (16, LANES), 0).astype(jnp.float32)
+    lanes_at = lax.broadcasted_iota(jnp.int32, (LANES, LANES), 1).astype(jnp.float32)
     zero = jnp.zeros((16, LANES), jnp.bfloat16)
-    one = jnp.ones((16, LANES), jnp.bfloat16)
+    zeros = jnp.zeros((LANES, LANES), jnp.bfloat16)
+    ones = jnp.ones((LANES, LANES), jnp.bfloat16)
     total[...] = jnp.zeros_like(total)
 
     def build(left, right, step):
@@ -412,28 +426,32 @@
             lanes = pl.ds(pl.multiple_of(step * chunk + j * LANES, LANES), LANES)
             parts = [wide(quant_ref[r:r + 1, lanes]) for r in QUANT_ROW]
             column = wide(quant_ref[COLUMN_ROW:COLUMN_ROW + 1, lanes])
-            level = wide(quant_ref[LEVEL_ROW:LEVEL_ROW + 1, lanes])
             for k in range(columns // 16):
                 hit = (row16 + (base + 16.0 * k)).astype(jnp.bfloat16) == column
                 for c in range(channels):
                     left[c * columns + 16 * k:c * columns + 16 * k + 16, here] = jnp.where(hit, parts[c], zero)
-            for k in range(depth // 16):
-                hit = (row16 + 16.0 * k).astype(jnp.bfloat16) == level
-                right[16 * k:16 * k + 16, here] = jnp.where(hit, one, zero)
+        tiles = [quant_ref[:, pl.ds(pl.multiple_of(step * chunk + j * LANES, LANES), LANES)] for j in range(chunk // LANES)]
+        turned = jnp.transpose(jnp.concatenate(tiles, axis=0))
+        for j in range(chunk // LANES):
+            place = j * 8 + LEVEL_ROW
+            level = jnp.broadcast_to(turned[:, place:place + 1], (LANES, LANES)).astype(jnp.bfloat16)
+            for k in range(depth // LANES):
+                hit = (lanes_at + k * LANES).astype(jnp.bfloat16) == level
+                right[j * LANES:(j + 1) * LANES, k * LANES:(k + 1) * LANES] = jnp.where(hit, ones, zeros)
 
     build(left_a, right_a, 0)
 
     def two(i, carry):
         now = 2 * i
         build(left_b, right_b, now + 1)
-        total[...] += dot(left_a[...], right_a[...], NT)
+        total[...] += dot(left_a[...], right_a[...])
         build(left_a, right_a, jnp.minimum(now + 2, steps - 1))
-        total[...] += dot(left_b[...], right_b[...], NT)
+        total[...] += dot(left_b[...], right_b[...])
         return carry
 
     lax.fori_loop(0, steps // 2, two, 0)
     if steps % 2:
-        total[...] += dot(left_a[...], right_a[...], NT)
+        total[...] += dot(left_a[...], right_a[...])
 
     high, low = halves(total[...])
     field_ref[...] = dot(high, depth_ref[0]) + (dot(high, depth_ref[1]) + dot(low, depth_ref[0]))
@@ -456,7 +474,7 @@
     edge = jax.ShapeDtypeStruct((channels * columns // 2, depth), jnp.float32)
     outs = (field, edge, edge) if edges else (field,)
     left = pltpu.VMEM((channels * columns, chunk), jnp.bfloat16)
-    right = pltpu.VMEM((depth, chunk), jnp.bfloat16)
+    right = pltpu.VMEM((chunk, depth), jnp.bfloat16)
     return pl.pallas_call(
         functools.partial(deposit_kernel, base, chunk, edges),
         out_shape=outs,
@@ -469,18 +487,39 @@
     )(quant, depth_op)
 
 
-def mix(operator_ref, pieces):
-    total = None
-    start = 0
-    for piece in pieces:
-        take = slice(start, start + piece.shape[0])
-        high, low = halves(piece)
-        value = dot(operator_ref[0, :, take], high) + (
-            dot(operator_ref[1, :, take], high) + dot(operator_ref[0, :, take], low)
-        )
-        total = value if total is None else total + value
-        start += piece.shape[0]
-    return total
+def mix(operator_ref, start, piece):
+    take = slice(start, start + piece.shape[0])
+    high, low = halves(piece)
+    return dot(operator_ref[0, :, take], high) + (
+        dot(operator_ref[1, :, take], high) + dot(operator_ref[0, :, take], low)
+    )
+
+
+def own_kernel(operator_ref, *refs):
+    channels = len(QUANT_ROW)
+    part_ref = refs[-1]
+    columns = part_ref.shape[0] // channels
+    for c in range(channels):
+        start, value = 0, None
+        for ref in refs[:-1]:
+            size = ref.shape[0] // channels
+            piece = mix(operator_ref, start, ref[c * size:(c + 1) * size, :])
+            value = piece if value is None else value + piece
+            start += size
+        part_ref[c * columns:(c + 1) * columns, :] = value
+
+
+def own_part(operator, *fields):
+    rows = sum(field.shape[0] for field in fields)
+    return pl.pallas_call(
+        own_kernel,
+        out_shape=jax.ShapeDtypeStruct((rows, fields[0].shape[1]), jnp.float32),
+        in_specs=[VMEM] * (1 + len(fields)),
+        out_specs=VMEM,
+        compiler_params=params(12),
+        cost_estimate=cost(1),
+        name="own_part",
+    )(operator, *fields)
 
 
 def sides(axis, first, second):
@@ -488,21 +527,19 @@
     return jnp.concatenate([jnp.where(odd, first, second), jnp.where(odd, second, first)], axis=0)
 
 
-def span_kernel(rows_x, rows_y, edge_ref, inner_ref, first_in, second_in, operator_ref, field_ref, first_ref, second_ref):
+def span_kernel(rows_x, rows_y, part_ref, first_in, second_in, operator_ref, field_ref, first_ref, second_ref):
     channels = len(QUANT_ROW)
     columns = rows_x * rows_y
-    outer = edge_ref.shape[0] // channels
-    inner = inner_ref.shape[0] // channels
     halo = first_in.shape[0] // channels
     odd = is_odd("stream")
     first_x = (1 - odd) * (rows_x - REACH)
     second_x = odd * (rows_x - REACH)
     for c in range(channels):
-        own = [edge_ref[c * outer:(c + 1) * outer, :], inner_ref[c * inner:(c + 1) * inner, :]]
+        own = slice(c * columns, (c + 1) * columns)
         side = slice(c * halo, (c + 1) * halo)
-        own = jnp.concatenate(own, axis=0)
-        value = mix(operator_ref, [own, sides("span", first_in[side, :], second_in[side, :])])
-        field_ref[c * columns:(c + 1) * columns, :] = value
+        field_ref[own, :] = part_ref[own, :] + mix(
+            operator_ref, columns, sides("span", first_in[side, :], second_in[side, :])
+        )
     for c in range(channels):
         for k in range(REACH):
             for y in range(rows_y):
@@ -512,31 +549,33 @@
                 second_ref[to:to + 1, :] = field_ref[pl.ds(row + second_x, 1), :]
 
 
-def span_pass(rows_x, rows_y, edge, inner, first, second, operator):
+def span_pass(rows_x, rows_y, part, first, second, operator):
     channels = len(QUANT_ROW)
-    depth = edge.shape[1]
+    depth = part.shape[1]
     halo = jax.ShapeDtypeStruct((channels * REACH * rows_y, depth), jnp.float32)
     return pl.pallas_call(
         functools.partial(span_kernel, rows_x, rows_y),
         out_shape=(jax.ShapeDtypeStruct((channels * rows_x * rows_y, depth), jnp.float32), halo, halo),
-        in_specs=[VMEM] * 5,
+        in_specs=[VMEM] * 4,
         out_specs=(VMEM,) * 3,
         compiler_params=params(12),
-        cost_estimate=cost(1.5),
+        cost_estimate=cost(1),
         name="span_pass",
-    )(edge, inner, first, second, operator)
-
-
-def stream_kernel(rows_q, own_ref, first_in, second_in, operator_ref, choose_ref, fluid_ref, solid_ref, out_ref):
+    )(part, first, second, operator)
+
+
+def stream_kernel(rows_q, part_ref, first_in, second_in, operator_ref, choose_ref, fluid_ref, solid_ref, out_ref):
     channels = len(QUANT_ROW)
-    columns = own_ref.shape[0] // channels
+    columns = part_ref.shape[0] // channels
     halo = first_in.shape[0] // channels
     choose = choose_ref[...]
     base = None
     for c in range(channels):
         own = slice(c * columns, (c + 1) * columns)
         side = slice(c * halo, (c + 1) * halo)
-        solid = mix(operator_ref, [own_ref[own, :], sides("stream", first_in[side, :], second_in[side, :])])
+        solid = part_ref[own, :] + mix(
+            operator_ref, columns, sides("stream", first_in[side, :], second_in[side, :])
+        )
         solid_ref[own, :] = solid
         if c == 0:
             base = solid
@@ -551,13 +590,13 @@
         out_ref[:, :, place, :] = sent.reshape(sent.shape[0] // rows_q, rows_q, -1)
 
 
-def stream_pass(peers, rows_q, own, first, second, operator, choose, fluid):
+def stream_pass(peers, rows_q, part, first, second, operator, choose, fluid):
     channels = len(QUANT_ROW)
-    depth = own.shape[1]
+    depth = part.shape[1]
     return pl.pallas_call(
         functools.partial(stream_kernel, rows_q),
         out_shape=(
-            jax.ShapeDtypeStruct(own.shape, jnp.float32),
+            jax.ShapeDtypeStruct(part.shape, jnp.float32),
             jax.ShapeDtypeStruct((peers, rows_q, channels, depth), jnp.float32),
         ),
         in_specs=[VMEM] * 6,
@@ -565,7 +604,7 @@
         compiler_params=params(16),
         cost_estimate=cost(3.5),
         name="stream_pass",
-    )(own, first, second, operator, choose, fluid)
+    )(part, first, second, operator, choose, fluid)
 
 
 def swap(first, second, axis, periodic):
@@ -600,10 +639,12 @@
     edge, first, second = deposit(0, faces, chunk, True, quant, depth_op)
     first, second = swap(first, second, "span", False)
     (inner,) = deposit(faces, columns - faces, chunk, False, quant, depth_op)
-    field, *halos = span_pass(rows_x, rows_y, edge, inner, first, second, span_op)
+    part = own_part(span_op, edge, inner)
+    field, *halos = span_pass(rows_x, rows_y, part, first, second, span_op)
     halos = swap(*halos, "stream", True)
+    part = own_part(stream_op, field)
     solid, outgoing = stream_pass(
-        peers, rows_q, field, *halos, stream_op, choose, fluid.reshape(3 * columns, depth)
+        peers, rows_q, part, *halos, stream_op, choose, fluid.reshape(3 * columns, depth)
     )
     arrived = lax.all_to_all(outgoing, axes, split_axis=0, concat_axis=0, tiled=True)
     return grains_after, solid.reshape(4, rows_x, rows_y, depth), arrived[None]

time: 92 us -> 91 us (0.989)
  starting transfers between devices: 8.94 us -> 4.57 us
  waiting for transfers between devices: 4.29 us -> 6.84 us
    ppermute x3, starting transfers between devices: 4.12 us -> 0.86 us  [swap(): second = lax.ppermute(second, axis, others)]
    ppermute x3, waiting for transfers between devices: 4.1 us -> 6.49 us  [swap(): second = lax.ppermute(second, axis, others)]
    pallas_call x2, Pallas kernels: 24.6 us -> 26.7 us  [deposit(): pl.pallas_call(functools.partial(deposit_kernel, base, chunk, edges), out...]
    pallas_call x1, Pallas kernels: 3.77 us -> 2.18 us  [stream_pass(): pl.pallas_call(functools.partial(stream_kernel, rows_q), out_shape=(jax.S...]
    pallas_call x0 -> x2, Pallas kernels: none -> 1.57 us  [own_part(): pl.pallas_call(own_kernel, out_shape=jax.ShapeDtypeStruct((rows, fields[0...]
    ppermute x3, starting transfers between devices: 4.82 us -> 3.71 us  [swap(): return (lax.ppermute(first, axis, pairs), second)]
    pallas_call x1, Pallas kernels: 9.56 us -> 8.55 us  [leave(): pl.pallas_call(functools.partial(leave_kernel, rows_x, rows_y), out_shape...]
  transfers between devices with their start and end apart: 6 -> 6, of which waited for: 2 -> 3; matrix products, arithmetic and copies ran while one was open for 0% -> 0% of each run, Pallas kernels for 13% -> 15%
where the time goes in v6:
time: 91 us; the launch traced here: 91.1 us
  Pallas kernels  43.4 us (48%)
  blocking collectives  34.5 us (38%)
  waiting for transfers between devices  6.84 us (8%)
  starting transfers between devices  4.57 us (5%)
  local copies, waits for them, and re-layouts  0.98 us (1%)
    all_to_all x1, blocking collectives, per_device(): lax.all_to_all(outgoing, axes, split_axis=0, concat_axis=0, tiled=True)  34.5 us
    pallas_call x2, Pallas kernels, deposit(): pl.pallas_call(functools.partial(deposit_kernel, base, chunk, edges), out...  26.7 us
    pallas_call x1, Pallas kernels, leave(): pl.pallas_call(functools.partial(leave_kernel, rows_x, rows_y), out_shape...  8.55 us
    ppermute x3, waiting for transfers between devices, swap(): second = lax.ppermute(second, axis, others)  6.49 us
    ppermute x3, starting transfers between devices, swap(): return (lax.ppermute(first, axis, pairs), second)  3.71 us
    pallas_call x1, Pallas kernels, keep(): pl.pallas_call(functools.partial(keep_kernel, rows_x, rows_y, depth), out...  2.92 us
    pallas_call x1, Pallas kernels, stream_pass(): pl.pallas_call(functools.partial(stream_kernel, rows_q), out_shape=(jax.S...  2.18 us
  transfers between devices with their start and end apart: 6, of which 3 were waited for; matrix products, arithmetic and copies ran while one was open for 0% of the time, Pallas kernels for 15%

profile of v6, /device:TPU:1, one launch (start us, length us, event | category | flops | bytes accessed | tf_op | source)
XLA Modules:
  0.0 91.1 jit_solution(582588088276494526)
XLA Ops:
  0.6 8.6 %leave.1 = (f32[13,2048]{1,0:T(8,128)S(1)}, f32[13,2048]{1,0:T(8,128)S(1)}, bf16[2,256,256]{2,1,0:T(8,128)(2,1)S(1)}, bf16[2,256,304]{2,1,0:T(8,128)(2,1)S(1)}, ...) custom-call(f32[13,24576]{1,0:T(8,128)} %grains_ref.1, ...), custom_call_target="tpu_custom_call" | custom-call | bytes 24000000 | tf_op jit(solution)/shard_map/leave/pallas_call | solution.py:169
  9.2 0.4 collective-permute-start
  9.6 0.0 collective-permute-start.1
  9.6 2.9 %keep.1 = (f32[13,28672]{1,0:T(8,128)}, f32[8,28672]{1,0:T(8,128)S(1)}) custom-call(f32[13,24576]{1,0:T(8,128)S(1)} %copy-done, s32[2,2048]{1,0:T(2,128)S(1)} %get-tuple-element.23.marks_ref, s32[1,28672]{1,0:T(1,128)S(1)} %get-tuple-element.24.cells_ref), custom_call_target="tpu_custom_call" | custom-call | bytes 12000000 | tf_op jit(solution)/shard_map/keep/pallas_call | solution.py:345
  12.5 0.0 collective-permute-done.first_ref
  12.5 2.6 %collective-permute-done.1.second_ref = f32[13,2048]{1,0:T(8,128)S(1)} collective-permute-done((f32[13,2048]{1,0:T(8,128)S(1)}, f32[13,2048]{1,0:T(8,128)S(1)}, u32[]{:S(2)}, u32[]{:S(2)}) %collective-permute-start.1) | collective-permute-done | bytes 106528 | tf_op jit(solution)/shard_map/ppermute | solution.py:617
  15.1 0.7 join.1
  15.8 17.8 %deposit.2 = (f32[768,256]{1,0:T(8,128)S(1)}, f32[384,256]{1,0:T(8,128)S(1)}, f32[384,256]{1,0:T(8,128)S(1)}) custom-call(f32[8,28672]{1,0:T(8,128)S(1)} %get-tuple-element.32.quant_ref, bf16[2,256,256]{2,1,0:T(8,128)(2,1)S(1)} %get-tuple-element.33.depth_ref), custom_call_target="tpu_custom_call" | custom-call | bytes 51840000 | tf_op jit(solution)/shard_map/deposit/pallas_call | solution.py:478
  33.6 0.4 collective-permute-start.2
  34.0 0.9 collective-permute-start.3
  34.9 8.9 %deposit.3.refs_1_ = f32[256,256]{1,0:T(8,128)S(1)} custom-call(f32[8,28672]{1,0:T(8,128)S(1)} %get-tuple-element.32.quant_ref, bf16[2,256,256]{2,1,0:T(8,128)(2,1)S(1)} %get-tuple-element.33.depth_ref), custom_call_target="tpu_custom_call" | custom-call | bytes 17280000 | tf_op jit(solution)/shard_map/deposit/pallas_call | solution.py:478
  43.8 1.0 %own_part.2.part_ref = f32[1024,256]{1,0:T(8,128)S(1)} custom-call(bf16[2,256,448]{2,1,0:T(8,128)(2,1)S(1)} %get-tuple-element.31.operator_ref, f32[768,256]{1,0:T(8,128)S(1)} %get-tuple-element.34.refs_0_, f32[256,256]{1,0:T(8,128)S(1)} %deposit.3.refs_1_), custom_call_target="tpu_custom_call" | custom-call | bytes 3000000 | tf_op jit(solution)/shard_map/own_part/pallas_call | solution.py:514
  44.8 0.0 collective-permute-done.2.first_in
  44.8 0.0 collective-permute-done.3.second_in
  44.8 0.8 span_pass.1
  45.6 0.0 copy-start.1
  45.7 2.9 %collective-permute-start.4 = (f32[96,256]{1,0:T(8,128)S(1)}, f32[96,256]{1,0:T(8,128)S(1)}, u32[]{:S(2)}, u32[]{:S(2)}) collective-permute-start(f32[96,256]{1,0:T(8,128)S(1)} %get-tuple-element.38), channel_id=1, source_target_pairs={{0,4},{4,0},{8,12},{12,8},{16,20},{20,16},{24,28},{28,24},{1,5},{5... | collective-permute-start | bytes 294920 | tf_op jit(solution)/shard_map/ppermute | solution.py:618
  48.6 0.0 collective-permute-start.5
  48.6 0.6 own_part.3.part_ref
  49.2 0.3 collective-permute-done.4.first_in
  49.5 3.9 %collective-permute-done.5.second_in = f32[96,256]{1,0:T(8,128)S(1)} collective-permute-done((f32[96,256]{1,0:T(8,128)S(1)}, f32[96,256]{1,0:T(8,128)S(1)}, u32[]{:S(2)}, u32[]{:S(2)}) %collective-permute-start.5) | collective-permute-done | bytes 98336 | tf_op jit(solution)/shard_map/ppermute | solution.py:617
  53.4 2.2 %stream_pass.1 = (f32[1024,256]{1,0:T(8,128)}, f32[32,8,4,256]{3,2,1,0:T(4,128)S(1)}) custom-call(f32[1024,256]{1,0:T(8,128)S(1)} %own_part.3.part_ref, f32[96,256]{1,0:T(8,128)S(1)} %collective-permute-done.4.first_in, f32[96,256]{1,0:T(8,128)S(1)} %collective-permute-done.5.second_in, bf16[2,256,304]{2,1,0:T(8,128)(2,1)S(1)} %get-tuple-element.30.operator_ref, ...), custom_call_target="tpu_custom_call" | custom-call | bytes 10500000 | tf_op jit(solution)/shard_map/stream_pass/pallas_call | solution.py:596
  55.6 34.5 %all_to_all.5 = f32[32,8,4,256]{3,2,1,0:T(4,128)S(1)} all-to-all(f32[32,8,4,256]{3,2,1,0:T(4,128)S(1)} %get-tuple-element.42), channel_id=1, replica_groups=mesh['stream'=8,'span'=4] {'stream','span'}, dimensions={0} | all-to-all | bytes 2097152 | tf_op jit(solution)/shard_map/all_to_all | solution.py:649
  90.1 1.0 %copy.15 = f32[1,32,8,4,256]{4,3,2,1,0:T(4,128)} copy(f32[1,32,8,4,256]{4,3,2,1,0:T(4,128)S(1)} %bitcast.9) | data formatting | bytes 2097152
  (3 shorter events, 0.0 us)
Async XLA Ops:
  0.6 9.0 %copy-start = (f32[13,24576]{1,0:T(8,128)S(1)}, f32[13,24576]{1,0:T(8,128)}, u32[]{:S(2)}) copy-start(f32[13,24576]{1,0:T(8,128)} %grains_ref.1) | copy-start | bytes 3833860
  9.2 3.3 %collective-permute-start = (f32[13,2048]{1,0:T(8,128)S(1)}, f32[13,2048]{1,0:T(8,128)S(1)}, u32[]{:S(2)}, u32[]{:S(2)}) collective-permute-start(f32[13,2048]{1,0:T(8,128)S(1)} %get-tuple-element.27), channel_id=1, source_target_pairs={{0,4},{4,0},{8,12},{12,8},{16,20},{20,16},{24,28},{28,24},{1,5},{5... | collective-permute-start | bytes 319496 | tf_op jit(solution)/shard_map/ppermute | solution.py:618
  9.6 5.5 %collective-permute-start.1 = (f32[13,2048]{1,0:T(8,128)S(1)}, f32[13,2048]{1,0:T(8,128)S(1)}, u32[]{:S(2)}, u32[]{:S(2)}) collective-permute-start(f32[13,2048]{1,0:T(8,128)S(1)} %get-tuple-element.28), channel_id=1, source_target_pairs={{0,28},{4,8},{8,4},{12,16},{16,12},{20,24},{24,20},{28,0},{1,29},{... | collective-permute-start | bytes 319496 | tf_op jit(solution)/shard_map/ppermute | solution.py:617
  33.6 11.2 %collective-permute-start.2 = (f32[384,256]{1,0:T(8,128)S(1)}, f32[384,256]{1,0:T(8,128)S(1)}, u32[]{:S(2)}, u32[]{:S(2)}) collective-permute-start(f32[384,256]{1,0:T(8,128)S(1)} %get-tuple-element.35), channel_id=1, source_target_pairs={{0,1},{1,0},{2,3},{3,2},{4,5},{5,4},{6,7},{7,6},{8,9},{9,8},{10,11... | collective-permute-start | bytes 1179656 | tf_op jit(solution)/shard_map/ppermute | solution.py:618
  34.0 10.8 %collective-permute-start.3 = (f32[384,256]{1,0:T(8,128)S(1)}, f32[384,256]{1,0:T(8,128)S(1)}, u32[]{:S(2)}, u32[]{:S(2)}) collective-permute-start(f32[384,256]{1,0:T(8,128)S(1)} %get-tuple-element.36), channel_id=1, source_target_pairs={{1,2},{2,1},{5,6},{6,5},{9,10},{10,9},{13,14},{14,13},{17,18},{18,... | collective-permute-start | bytes 1179656 | tf_op jit(solution)/shard_map/ppermute | solution.py:617
  45.6 7.8 %copy-start.1 = (f32[3,32,8,256]{3,2,1,0:T(8,128)S(1)}, f32[3,32,8,256]{3,2,1,0:T(8,128)}, u32[]{:S(2)}) copy-start(f32[3,32,8,256]{3,2,1,0:T(8,128)} %param.11) | copy-start | bytes 2359300
  45.7 3.9 %collective-permute-start.4 = (f32[96,256]{1,0:T(8,128)S(1)}, f32[96,256]{1,0:T(8,128)S(1)}, u32[]{:S(2)}, u32[]{:S(2)}) collective-permute-start(f32[96,256]{1,0:T(8,128)S(1)} %get-tuple-element.38), channel_id=1, source_target_pairs={{0,4},{4,0},{8,12},{12,8},{16,20},{20,16},{24,28},{28,24},{1,5},{5... | collective-permute-start | bytes 294920 | tf_op jit(solution)/shard_map/ppermute | solution.py:618
  48.6 4.8 %collective-permute-start.5 = (f32[96,256]{1,0:T(8,128)S(1)}, f32[96,256]{1,0:T(8,128)S(1)}, u32[]{:S(2)}, u32[]{:S(2)}) collective-permute-start(f32[96,256]{1,0:T(8,128)S(1)} %get-tuple-element.39), channel_id=1, source_target_pairs={{0,28},{4,8},{8,4},{12,16},{16,12},{20,24},{24,20},{28,0},{1,29},{... | collective-permute-start | bytes 294920 | tf_op jit(solution)/shard_map/ppermute | solution.py:617

commit v7 on v6

--- a/solution.py
+++ b/solution.py
@@ -11,6 +11,7 @@
 REACH = 3
 LANES = 128
 RECORD = 16
+BATCH = 32
 
 spread_cells = 1.5
 drag_rate = 0.25
@@ -124,9 +125,11 @@
 
         def gather(i, carry):
             base = i * run
-            for k in range(run):
-                row = lax.bitwise_and(slots_s[which, base + k], rows - 1)
-                picked[k:k + 1, :] = table[pl.ds(row, 1), :]
+            for k in range(0, run, BATCH):
+                found = [lax.bitwise_and(slots_s[which, base + k + n], rows - 1) for n in range(BATCH)]
+                found = [table[pl.ds(row, 1), :] for row in found]
+                for n in range(BATCH):
+                    picked[k + n:k + n + 1, :] = found[n]
             heads, rests = [], []
             for piece in range(run // LANES):
                 lanes = pl.ds(pl.multiple_of(base + piece * LANES, LANES), LANES)
@@ -295,44 +298,52 @@
         lax.fori_loop(0, width // LANES, put, 0, unroll=8)
     gone[...] = dot(high_rows[...], low_rows[...], NT)
 
-    row8 = lax.broadcasted_iota(jnp.int32, (8, LANES), 0)
-
     def place(cell):
         x, rest = split(cell, rows_y * depth)
         y, level = split(rest, depth)
         return (row_of(y, rows_y) * rows_x + x).astype(jnp.float32), level.astype(jnp.float32)
 
+    block = math.gcd(math.gcd(slot_count, total - slot_count), 16 * LANES)
+
+    def table(head, volume, start):
+        row8 = lax.broadcasted_iota(jnp.int32, (8, block), 0)
+        col, lev = place(cells_ref[:, pl.ds(start, block)])
+        value = jnp.where(row8 == QUANT_ROW[0], volume, volume * head)
+        value = jnp.where(row8 == COLUMN_ROW, col, value)
+        return jnp.where(row8 == LEVEL_ROW, lev, value)
+
     def keep(i, carry):
-        lanes = lane_tile(i)
-        stay = 1.0 - gone[pl.ds(i, 1), :]
+        start = pl.multiple_of(i * block, block)
+        lanes = pl.ds(start, block)
+        first = i * (block // LANES)
+        stay = [1.0 - gone[pl.ds(first + n, 1), :] for n in range(block // LANES)]
+        stay = jnp.concatenate(stay, axis=1)
         head = grains_ref[0:8, lanes] * stay
         rest = grains_ref[8:records, lanes] * stay
+        radius = rest[1:2]
+        value = table(head, 4.18879 * (radius * radius * radius), start)
         kept[0:8, lanes] = head
         kept[8:records, lanes] = rest
-        radius = rest[1:2]
-        volume = 4.18879 * (radius * radius * radius)
-        col, lev = place(cells_ref[:, lanes])
-        value = jnp.where(row8 == QUANT_ROW[0], volume, volume * head)
-        value = jnp.where(row8 == COLUMN_ROW, col, value)
-        quant_ref[:, lanes] = jnp.where(row8 == LEVEL_ROW, lev, value)
+        quant_ref[:, lanes] = value
         return carry
 
     writes = []
+    blocks = slot_count // block
     for n in range(pieces):
-        first = tiles * n // pieces
-        last = tiles * (n + 1) // pieces
-        lax.fori_loop(first, last, keep, 0, unroll=16)
-        here = pl.ds(first * LANES, (last - first) * LANES)
+        first = blocks * n // pieces
+        last = blocks * (n + 1) // pieces
+        lax.fori_loop(first, last, keep, 0)
+        here = pl.ds(first * block, (last - first) * block)
         writes.append(pltpu.make_async_copy(kept.at[:, here], after_hbm.at[:, here], sems.at[n]))
         writes[n].start()
 
     def arrivals(i, carry):
-        lanes = lane_tile(i)
-        col, lev = place(cells_ref[:, lanes])
-        quant_ref[:, lanes] = jnp.where(row8 == COLUMN_ROW, col, lev)
+        start = pl.multiple_of(i * block, block)
+        none = jnp.zeros((8, block), jnp.float32)
+        quant_ref[:, pl.ds(start, block)] = table(none, none[0:1], start)
         return carry
 
-    lax.fori_loop(tiles, total // LANES, arrivals, 0, unroll=8)
+    lax.fori_loop(blocks, total // block, arrivals, 0)
     for write in writes:
         write.wait()
 
@@ -363,7 +374,8 @@
 def join_kernel(after_in, quant_in, first_ref, second_ref, after_ref, quant_ref, sems):
     records, width = first_ref.shape
     start = after_ref.shape[1] - 2 * width
-    row8 = lax.broadcasted_iota(jnp.int32, (8, LANES), 0)
+    block = math.gcd(math.gcd(width, start), 16 * LANES)
+    row8 = lax.broadcasted_iota(jnp.int32, (8, block), 0)
     odd = is_odd("stream")
     copies = []
     for n, arrived in enumerate((first_ref, second_ref)):
@@ -374,9 +386,9 @@
     for n, arrived in enumerate((first_ref, second_ref)):
 
         def step(i, carry):
-            lanes = lane_tile(i)
+            lanes = pl.ds(pl.multiple_of(i * block, block), block)
             place = start + (1 - odd if n == 0 else odd) * width
-            to = pl.ds(pl.multiple_of(place + i * LANES, LANES), LANES)
+            to = pl.ds(pl.multiple_of(place + i * block, block), block)
             head = arrived[0:8, lanes]
             radius = arrived[9:10, lanes]
             volume = 4.18879 * (radius * radius * radius)
@@ -384,7 +396,7 @@
             quant_ref[:, to] = jnp.where(row8 >= COLUMN_ROW, quant_in[:, to], value)
             return carry
 
-        lax.fori_loop(0, width // LANES, step, 0, unroll=8)
+        lax.fori_loop(0, width // block, step, 0)
     for copy in copies:
         copy.wait()
 
@@ -408,50 +420,44 @@
 
 def deposit_kernel(base, chunk, edges, quant_ref, depth_ref, *refs):
     field_ref = refs[0]
-    left_a, left_b, right_a, right_b, total = refs[-5:]
+    left_a, left_b, right_a, right_b, now_a, now_b, total = refs[-7:]
     channels = len(QUANT_ROW)
     columns = field_ref.shape[0] // channels
     depth = depth_ref.shape[1]
     steps = quant_ref.shape[1] // chunk
     row16 = lax.broadcasted_iota(jnp.int32, (16, LANES), 0).astype(jnp.float32)
-    lanes_at = lax.broadcasted_iota(jnp.int32, (LANES, LANES), 1).astype(jnp.float32)
     zero = jnp.zeros((16, LANES), jnp.bfloat16)
-    zeros = jnp.zeros((LANES, LANES), jnp.bfloat16)
-    ones = jnp.ones((LANES, LANES), jnp.bfloat16)
+    one = jnp.ones((16, LANES), jnp.bfloat16)
     total[...] = jnp.zeros_like(total)
 
-    def build(left, right, step):
+    def build(left, right, now, step):
+        now[...] = quant_ref[:, pl.ds(pl.multiple_of(step * chunk, chunk), chunk)]
         for j in range(chunk // LANES):
             here = slice(j * LANES, (j + 1) * LANES)
-            lanes = pl.ds(pl.multiple_of(step * chunk + j * LANES, LANES), LANES)
-            parts = [wide(quant_ref[r:r + 1, lanes]) for r in QUANT_ROW]
-            column = wide(quant_ref[COLUMN_ROW:COLUMN_ROW + 1, lanes])
+            parts = [wide(now[r:r + 1, here]) for r in QUANT_ROW]
+            column = wide(now[COLUMN_ROW:COLUMN_ROW + 1, here])
+            level = wide(now[LEVEL_ROW:LEVEL_ROW + 1, here])
             for k in range(columns // 16):
                 hit = (row16 + (base + 16.0 * k)).astype(jnp.bfloat16) == column
                 for c in range(channels):
                     left[c * columns + 16 * k:c * columns + 16 * k + 16, here] = jnp.where(hit, parts[c], zero)
-        tiles = [quant_ref[:, pl.ds(pl.multiple_of(step * chunk + j * LANES, LANES), LANES)] for j in range(chunk // LANES)]
-        turned = jnp.transpose(jnp.concatenate(tiles, axis=0))
-        for j in range(chunk // LANES):
-            place = j * 8 + LEVEL_ROW
-            level = jnp.broadcast_to(turned[:, place:place + 1], (LANES, LANES)).astype(jnp.bfloat16)
-            for k in range(depth // LANES):
-                hit = (lanes_at + k * LANES).astype(jnp.bfloat16) == level
-                right[j * LANES:(j + 1) * LANES, k * LANES:(k + 1) * LANES] = jnp.where(hit, ones, zeros)
-
-    build(left_a, right_a, 0)
+            for k in range(depth // 16):
+                hit = (row16 + 16.0 * k).astype(jnp.bfloat16) == level
+                right[16 * k:16 * k + 16, here] = jnp.where(hit, one, zero)
+
+    build(left_a, right_a, now_a, 0)
 
     def two(i, carry):
         now = 2 * i
-        build(left_b, right_b, now + 1)
-        total[...] += dot(left_a[...], right_a[...])
-        build(left_a, right_a, jnp.minimum(now + 2, steps - 1))
-        total[...] += dot(left_b[...], right_b[...])
+        build(left_b, right_b, now_b, now + 1)
+        total[...] += dot(left_a[...], right_a[...], NT)
+        build(left_a, right_a, now_a, jnp.minimum(now + 2, steps - 1))
+        total[...] += dot(left_b[...], right_b[...], NT)
         return carry
 
     lax.fori_loop(0, steps // 2, two, 0)
     if steps % 2:
-        total[...] += dot(left_a[...], right_a[...])
+        total[...] += dot(left_a[...], right_a[...], NT)
 
     high, low = halves(total[...])
     field_ref[...] = dot(high, depth_ref[0]) + (dot(high, depth_ref[1]) + dot(low, depth_ref[0]))
@@ -474,13 +480,14 @@
     edge = jax.ShapeDtypeStruct((channels * columns // 2, depth), jnp.float32)
     outs = (field, edge, edge) if edges else (field,)
     left = pltpu.VMEM((channels * columns, chunk), jnp.bfloat16)
-    right = pltpu.VMEM((chunk, depth), jnp.bfloat16)
+    right = pltpu.VMEM((depth, chunk), jnp.bfloat16)
+    now = pltpu.VMEM((8, chunk), jnp.float32)
     return pl.pallas_call(
         functools.partial(deposit_kernel, base, chunk, edges),
         out_shape=outs,
         in_specs=[VMEM, VMEM],
         out_specs=(VMEM,) * len(outs),
-        scratch_shapes=[left, left, right, right, pltpu.VMEM(field.shape, jnp.float32)],
+        scratch_shapes=[left, left, right, right, now, now, pltpu.VMEM(field.shape, jnp.float32)],
         compiler_params=params(20),
         cost_estimate=cost(columns * 0.09),
         name="deposit",
@@ -564,30 +571,36 @@
     )(part, first, second, operator)
 
 
-def stream_kernel(rows_q, part_ref, first_in, second_in, operator_ref, choose_ref, fluid_ref, solid_ref, out_ref):
+def stream_kernel(
+    rows_q, part_ref, first_in, second_in, operator_ref, choose_ref, fluid_ref, solid_hbm, out_ref, solid_ref, sems
+):
     channels = len(QUANT_ROW)
     columns = part_ref.shape[0] // channels
     halo = first_in.shape[0] // channels
     choose = choose_ref[...]
-    base = None
+    copies = []
     for c in range(channels):
         own = slice(c * columns, (c + 1) * columns)
         side = slice(c * halo, (c + 1) * halo)
-        solid = part_ref[own, :] + mix(
+        solid_ref[own, :] = part_ref[own, :] + mix(
             operator_ref, columns, sides("stream", first_in[side, :], second_in[side, :])
         )
-        solid_ref[own, :] = solid
+        copies.append(pltpu.make_async_copy(solid_ref.at[own, :], solid_hbm.at[own, :], sems.at[c]))
+        copies[c].start()
+    base = solid_ref[0:columns, :]
+    for c in range(channels):
         if c == 0:
-            base = solid
             value = 1.0 / (1.0 + base)
         else:
             flow = fluid_ref[(c - 1) * columns:c * columns, :]
-            value = flow + drag_rate * (solid - base * flow)
+            value = flow + drag_rate * (solid_ref[c * columns:(c + 1) * columns, :] - base * flow)
         first, rest = halves(value)
         second, third = halves(value - first.astype(jnp.float32))
         sent = dot(choose, first) + (dot(choose, second) + dot(choose, third))
         place = (c - 1) % channels
         out_ref[:, :, place, :] = sent.reshape(sent.shape[0] // rows_q, rows_q, -1)
+    for copy in copies:
+        copy.wait()
 
 
 def stream_pass(peers, rows_q, part, first, second, operator, choose, fluid):
@@ -600,9 +613,10 @@
             jax.ShapeDtypeStruct((peers, rows_q, channels, depth), jnp.float32),
         ),
         in_specs=[VMEM] * 6,
-        out_specs=(VMEM, VMEM),
+        out_specs=(HBM, VMEM),
+        scratch_shapes=[pltpu.VMEM(part.shape, jnp.float32), pltpu.SemaphoreType.DMA((channels,))],
         compiler_params=params(16),
-        cost_estimate=cost(3.5),
+        cost_estimate=cost(2),
         name="stream_pass",
     )(part, first, second, operator, choose, fluid)
 

time: 91 us -> 87.9 us (0.966)
  starting transfers between devices: 4.57 us -> 12.3 us
  Pallas kernels: 43.4 us -> 37.2 us
  waiting for transfers between devices: 6.84 us -> 2.28 us
    ppermute x3, starting transfers between devices: 0.86 us -> 5.14 us  [swap(): second = lax.ppermute(second, axis, others)]
    ppermute x3, waiting for transfers between devices: 6.49 us -> 2.27 us  [swap(): second = lax.ppermute(second, axis, others)]
    ppermute x3, starting transfers between devices: 3.71 us -> 7.2 us  [swap(): return (lax.ppermute(first, axis, pairs), second)]
    pallas_call x1, Pallas kernels: 8.55 us -> 5.18 us  [leave(): pl.pallas_call(functools.partial(leave_kernel, rows_x, rows_y), out_shape...]
    pallas_call x2, Pallas kernels: 26.7 us -> 24.8 us  [deposit(): pl.pallas_call(functools.partial(deposit_kernel, base, chunk, edges), out...]
  transfers between devices with their start and end apart: 6 -> 6, of which waited for: 3 -> 2; matrix products, arithmetic and copies ran while one was open for 0% -> 0% of each run, Pallas kernels for 15% -> 15%
where the time goes in v7:
time: 87.9 us; the launch traced here: 87.5 us
  Pallas kernels  37.2 us (42%)
  blocking collectives  33.9 us (39%)
  starting transfers between devices  12.3 us (14%)
  waiting for transfers between devices  2.28 us (3%)
  local copies, waits for them, and re-layouts  0.98 us (1%)
    all_to_all x1, blocking collectives, per_device(): lax.all_to_all(outgoing, axes, split_axis=0, concat_axis=0, tiled=True)  33.9 us
    pallas_call x2, Pallas kernels, deposit(): pl.pallas_call(functools.partial(deposit_kernel, base, chunk, edges), out...  24.8 us
    ppermute x3, starting transfers between devices, swap(): return (lax.ppermute(first, axis, pairs), second)  7.2 us
    pallas_call x1, Pallas kernels, leave(): pl.pallas_call(functools.partial(leave_kernel, rows_x, rows_y), out_shape...  5.18 us
    ppermute x3, starting transfers between devices, swap(): second = lax.ppermute(second, axis, others)  5.14 us
    pallas_call x1, Pallas kernels, keep(): pl.pallas_call(functools.partial(keep_kernel, rows_x, rows_y, depth), out...  2.6 us
    ppermute x3, waiting for transfers between devices, swap(): second = lax.ppermute(second, axis, others)  2.27 us
  transfers between devices with their start and end apart: 6, of which 2 were waited for; matrix products, arithmetic and copies ran while one was open for 0% of the time, Pallas kernels for 15%

profile of v7, /device:TPU:1, one launch (start us, length us, event | category | flops | bytes accessed | tf_op | source)
XLA Modules:
  0.0 87.5 jit_solution(7900586728321946938)
XLA Ops:
  0.6 5.2 %leave.1 = (f32[13,2048]{1,0:T(8,128)S(1)}, f32[13,2048]{1,0:T(8,128)S(1)}, bf16[2,256,256]{2,1,0:T(8,128)(2,1)S(1)}, bf16[2,256,304]{2,1,0:T(8,128)(2,1)S(1)}, ...) custom-call(f32[13,24576]{1,0:T(8,128)} %grains_ref.1, ...), custom_call_target="tpu_custom_call" | custom-call | bytes 24000000 | tf_op jit(solution)/shard_map/leave/pallas_call | solution.py:172
  5.8 3.8 %collective-permute-start = (f32[13,2048]{1,0:T(8,128)S(1)}, f32[13,2048]{1,0:T(8,128)S(1)}, u32[]{:S(2)}, u32[]{:S(2)}) collective-permute-start(f32[13,2048]{1,0:T(8,128)S(1)} %get-tuple-element.27), channel_id=1, source_target_pairs={{0,4},{4,0},{8,12},{12,8},{16,20},{20,16},{24,28},{28,24},{1,5},{5... | collective-permute-start | bytes 319496 | tf_op jit(solution)/shard_map/ppermute | solution.py:632
  9.6 2.0 %collective-permute-start.1 = (f32[13,2048]{1,0:T(8,128)S(1)}, f32[13,2048]{1,0:T(8,128)S(1)}, u32[]{:S(2)}, u32[]{:S(2)}) collective-permute-start(f32[13,2048]{1,0:T(8,128)S(1)} %get-tuple-element.28), channel_id=1, source_target_pairs={{0,28},{4,8},{8,4},{12,16},{16,12},{20,24},{24,20},{28,0},{1,29},{... | collective-permute-start | bytes 319496 | tf_op jit(solution)/shard_map/ppermute | solution.py:631
  11.6 2.6 %keep.1 = (f32[13,28672]{1,0:T(8,128)}, f32[8,28672]{1,0:T(8,128)S(1)}) custom-call(f32[13,24576]{1,0:T(8,128)S(1)} %copy-done, s32[2,2048]{1,0:T(2,128)S(1)} %get-tuple-element.23.marks_ref, s32[1,28672]{1,0:T(1,128)S(1)} %get-tuple-element.24.cells_ref), custom_call_target="tpu_custom_call" | custom-call | bytes 12000000 | tf_op jit(solution)/shard_map/keep/pallas_call | solution.py:356
  14.2 0.0 collective-permute-done.first_ref
  14.2 0.3 collective-permute-done.1.second_ref
  14.5 0.7 join.1
  15.3 16.0 %deposit.2 = (f32[768,256]{1,0:T(8,128)S(1)}, f32[384,256]{1,0:T(8,128)S(1)}, f32[384,256]{1,0:T(8,128)S(1)}) custom-call(f32[8,28672]{1,0:T(8,128)S(1)} %get-tuple-element.32.quant_ref, bf16[2,256,256]{2,1,0:T(8,128)(2,1)S(1)} %get-tuple-element.33.depth_ref), custom_call_target="tpu_custom_call" | custom-call | bytes 51840000 | tf_op jit(solution)/shard_map/deposit/pallas_call | solution.py:485
  31.3 3.3 %collective-permute-start.2 = (f32[384,256]{1,0:T(8,128)S(1)}, f32[384,256]{1,0:T(8,128)S(1)}, u32[]{:S(2)}, u32[]{:S(2)}) collective-permute-start(f32[384,256]{1,0:T(8,128)S(1)} %get-tuple-element.35), channel_id=1, source_target_pairs={{0,1},{1,0},{2,3},{3,2},{4,5},{5,4},{6,7},{7,6},{8,9},{9,8},{10,11... | collective-permute-start | bytes 1179656 | tf_op jit(solution)/shard_map/ppermute | solution.py:632
  34.6 0.7 collective-permute-start.3
  35.3 8.8 %deposit.3.refs_1_ = f32[256,256]{1,0:T(8,128)S(1)} custom-call(f32[8,28672]{1,0:T(8,128)S(1)} %get-tuple-element.32.quant_ref, bf16[2,256,256]{2,1,0:T(8,128)(2,1)S(1)} %get-tuple-element.33.depth_ref), custom_call_target="tpu_custom_call" | custom-call | bytes 17280000 | tf_op jit(solution)/shard_map/deposit/pallas_call | solution.py:485
  44.1 1.0 %own_part.2.part_ref = f32[1024,256]{1,0:T(8,128)S(1)} custom-call(bf16[2,256,448]{2,1,0:T(8,128)(2,1)S(1)} %get-tuple-element.31.operator_ref, f32[768,256]{1,0:T(8,128)S(1)} %get-tuple-element.34.refs_0_, f32[256,256]{1,0:T(8,128)S(1)} %deposit.3.refs_1_), custom_call_target="tpu_custom_call" | custom-call | bytes 3000000 | tf_op jit(solution)/shard_map/own_part/pallas_call | solution.py:521
  45.1 0.0 collective-permute-done.2.first_in
  45.1 0.0 collective-permute-done.3.second_in
  45.1 0.8 span_pass.1
  46.0 0.0 copy-start.1
  46.0 0.1 collective-permute-start.4
  46.1 2.5 %collective-permute-start.5 = (f32[96,256]{1,0:T(8,128)S(1)}, f32[96,256]{1,0:T(8,128)S(1)}, u32[]{:S(2)}, u32[]{:S(2)}) collective-permute-start(f32[96,256]{1,0:T(8,128)S(1)} %get-tuple-element.39), channel_id=1, source_target_pairs={{0,28},{4,8},{8,4},{12,16},{16,12},{20,24},{24,20},{28,0},{1,29},{... | collective-permute-start | bytes 294920 | tf_op jit(solution)/shard_map/ppermute | solution.py:631
  48.5 0.6 own_part.3.part_ref
  49.1 0.0 collective-permute-done.4.first_in
  49.2 1.9 %collective-permute-done.5.second_in = f32[96,256]{1,0:T(8,128)S(1)} collective-permute-done((f32[96,256]{1,0:T(8,128)S(1)}, f32[96,256]{1,0:T(8,128)S(1)}, u32[]{:S(2)}, u32[]{:S(2)}) %collective-permute-start.5) | collective-permute-done | bytes 98336 | tf_op jit(solution)/shard_map/ppermute | solution.py:631
  51.1 1.5 %stream_pass.1 = (f32[1024,256]{1,0:T(8,128)}, f32[32,8,4,256]{3,2,1,0:T(4,128)S(1)}) custom-call(f32[1024,256]{1,0:T(8,128)S(1)} %own_part.3.part_ref, f32[96,256]{1,0:T(8,128)S(1)} %collective-permute-done.4.first_in, f32[96,256]{1,0:T(8,128)S(1)} %collective-permute-done.5.second_in, bf16[2,256,304]{2,1,0:T(8,128)(2,1)S(1)} %get-tuple-element.30.operator_ref, ...), custom_call_target="tpu_custom_call" | custom-call | bytes 6000000 | tf_op jit(solution)/shard_map/stream_pass/pallas_call | solution.py:609
  52.6 33.9 %all_to_all.5 = f32[32,8,4,256]{3,2,1,0:T(4,128)S(1)} all-to-all(f32[32,8,4,256]{3,2,1,0:T(4,128)S(1)} %get-tuple-element.42), channel_id=1, replica_groups=mesh['stream'=8,'span'=4] {'stream','span'}, dimensions={0} | all-to-all | bytes 2097152 | tf_op jit(solution)/shard_map/all_to_all | solution.py:663
  86.5 1.0 %copy.15 = f32[1,32,8,4,256]{4,3,2,1,0:T(4,128)} copy(f32[1,32,8,4,256]{4,3,2,1,0:T(4,128)S(1)} %bitcast.9) | data formatting | bytes 2097152
  (3 shorter events, 0.0 us)
Async XLA Ops:
  0.6 11.0 %copy-start = (f32[13,24576]{1,0:T(8,128)S(1)}, f32[13,24576]{1,0:T(8,128)}, u32[]{:S(2)}) copy-start(f32[13,24576]{1,0:T(8,128)} %grains_ref.1) | copy-start | bytes 3833860
  5.8 8.4 %collective-permute-start = (f32[13,2048]{1,0:T(8,128)S(1)}, f32[13,2048]{1,0:T(8,128)S(1)}, u32[]{:S(2)}, u32[]{:S(2)}) collective-permute-start(f32[13,2048]{1,0:T(8,128)S(1)} %get-tuple-element.27), channel_id=1, source_target_pairs={{0,4},{4,0},{8,12},{12,8},{16,20},{20,16},{24,28},{28,24},{1,5},{5... | collective-permute-start | bytes 319496 | tf_op jit(solution)/shard_map/ppermute | solution.py:632
  9.6 4.9 %collective-permute-start.1 = (f32[13,2048]{1,0:T(8,128)S(1)}, f32[13,2048]{1,0:T(8,128)S(1)}, u32[]{:S(2)}, u32[]{:S(2)}) collective-permute-start(f32[13,2048]{1,0:T(8,128)S(1)} %get-tuple-element.28), channel_id=1, source_target_pairs={{0,28},{4,8},{8,4},{12,16},{16,12},{20,24},{24,20},{28,0},{1,29},{... | collective-permute-start | bytes 319496 | tf_op jit(solution)/shard_map/ppermute | solution.py:631
  31.3 13.8 %collective-permute-start.2 = (f32[384,256]{1,0:T(8,128)S(1)}, f32[384,256]{1,0:T(8,128)S(1)}, u32[]{:S(2)}, u32[]{:S(2)}) collective-permute-start(f32[384,256]{1,0:T(8,128)S(1)} %get-tuple-element.35), channel_id=1, source_target_pairs={{0,1},{1,0},{2,3},{3,2},{4,5},{5,4},{6,7},{7,6},{8,9},{9,8},{10,11... | collective-permute-start | bytes 1179656 | tf_op jit(solution)/shard_map/ppermute | solution.py:632
  34.6 10.5 %collective-permute-start.3 = (f32[384,256]{1,0:T(8,128)S(1)}, f32[384,256]{1,0:T(8,128)S(1)}, u32[]{:S(2)}, u32[]{:S(2)}) collective-permute-start(f32[384,256]{1,0:T(8,128)S(1)} %get-tuple-element.36), channel_id=1, source_target_pairs={{1,2},{2,1},{5,6},{6,5},{9,10},{10,9},{13,14},{14,13},{17,18},{18,... | collective-permute-start | bytes 1179656 | tf_op jit(solution)/shard_map/ppermute | solution.py:631
  46.0 5.1 %copy-start.1 = (f32[3,32,8,256]{3,2,1,0:T(8,128)S(1)}, f32[3,32,8,256]{3,2,1,0:T(8,128)}, u32[]{:S(2)}) copy-start(f32[3,32,8,256]{3,2,1,0:T(8,128)} %param.11) | copy-start | bytes 2359300
  46.0 3.2 %collective-permute-start.4 = (f32[96,256]{1,0:T(8,128)S(1)}, f32[96,256]{1,0:T(8,128)S(1)}, u32[]{:S(2)}, u32[]{:S(2)}) collective-permute-start(f32[96,256]{1,0:T(8,128)S(1)} %get-tuple-element.38), channel_id=1, source_target_pairs={{0,4},{4,0},{8,12},{12,8},{16,20},{20,16},{24,28},{28,24},{1,5},{5... | collective-permute-start | bytes 294920 | tf_op jit(solution)/shard_map/ppermute | solution.py:632
  46.1 5.0 %collective-permute-start.5 = (f32[96,256]{1,0:T(8,128)S(1)}, f32[96,256]{1,0:T(8,128)S(1)}, u32[]{:S(2)}, u32[]{:S(2)}) collective-permute-start(f32[96,256]{1,0:T(8,128)S(1)} %get-tuple-element.39), channel_id=1, source_target_pairs={{0,28},{4,8},{8,4},{12,16},{16,12},{20,24},{24,20},{28,0},{1,29},{... | collective-permute-start | bytes 294920 | tf_op jit(solution)/shard_map/ppermute | solution.py:631

commit v8 on v7

--- a/solution.py
+++ b/solution.py
@@ -76,14 +76,14 @@
 def leave_kernel(
     rows_x, rows_y, grains_hbm, slots_hbm, counts_hbm, cells_hbm, picks_hbm, alive_hbm,
     first_ref, second_ref, depth_ref, stream_ref, span_ref, choose_ref, marks_ref, cells_ref,
-    grains_ref, stage, table, picked, slots_v, slots_s, counts_s, picks_v, alive_v, sems,
+    grains_ref, stage, table, picked, slots_v, rows_v, rows_s, counts_s, picks_v, alive_v, sems,
 ):
     records, slot_count = grains_ref.shape
     width = first_ref.shape[1]
     rows = table.shape[0]
     parts = -(-slot_count // rows)
-    sources = (grains_hbm, slots_hbm, slots_hbm, counts_hbm, picks_hbm, alive_hbm, cells_hbm)
-    targets = (grains_ref, slots_v, slots_s, counts_s, picks_v, alive_v, cells_ref)
+    sources = (grains_hbm, slots_hbm, counts_hbm, picks_hbm, alive_hbm, cells_hbm)
+    targets = (grains_ref, slots_v, counts_s, picks_v, alive_v, cells_ref)
     copies = [
         pltpu.make_async_copy(source, target, sems.at[i])
         for i, (source, target) in enumerate(zip(sources, targets))
@@ -91,6 +91,10 @@
     for copy in copies:
         copy.start()
     build_operators(rows_x, rows_y, depth_ref, stream_ref, span_ref)
+    copies[1].wait()
+    rows_v[...] = lax.bitwise_and(slots_v[...], table.shape[0] - 1)
+    copies.append(pltpu.make_async_copy(rows_v, rows_s, sems.at[len(copies)]))
+    copies[-1].start()
     copies[0].wait()
 
     for part in range(parts):
@@ -101,7 +105,7 @@
     for block in range(rows // LANES):
         here = slice(block * LANES, (block + 1) * LANES)
         table[here, :] = jnp.transpose(stage[:, here])
-    for copy in copies[1:]:
+    for copy in copies[2:]:
         copy.wait()
     build_choice(picks_v, alive_v, choose_ref)
     for which in (0, 1):
@@ -126,7 +130,7 @@
         def gather(i, carry):
             base = i * run
             for k in range(0, run, BATCH):
-                found = [lax.bitwise_and(slots_s[which, base + k + n], rows - 1) for n in range(BATCH)]
+                found = [rows_s[which, base + k + n] for n in range(BATCH)]
                 found = [table[pl.ds(row, 1), :] for row in found]
                 for n in range(BATCH):
                     picked[k + n:k + n + 1, :] = found[n]
@@ -189,6 +193,7 @@
             pltpu.VMEM((rows, LANES), jnp.float32),
             pltpu.VMEM((run, LANES), jnp.float32),
             pltpu.VMEM(slots.shape, jnp.int32),
+            pltpu.VMEM(slots.shape, jnp.int32),
             pltpu.SMEM(slots.shape, jnp.int32),
             pltpu.SMEM(counts.shape, jnp.int32),
             pltpu.VMEM(picks.shape, jnp.int32),
@@ -371,7 +376,7 @@
     )(grains, marks, cells)
 
 
-def join_kernel(after_in, quant_in, first_ref, second_ref, after_ref, quant_ref, sems):
+def join_kernel(after_in, quant_in, first_ref, second_ref, earlier_ref, after_ref, quant_ref, sems):
     records, width = first_ref.shape
     start = after_ref.shape[1] - 2 * width
     block = math.gcd(math.gcd(width, start), 16 * LANES)
@@ -401,34 +406,37 @@
         copy.wait()
 
 
-def join(after, quant, first, second):
+def join(after, quant, first, second, earlier):
     return pl.pallas_call(
         join_kernel,
         out_shape=(
             jax.ShapeDtypeStruct(after.shape, after.dtype),
             jax.ShapeDtypeStruct(quant.shape, quant.dtype),
         ),
-        in_specs=[HBM, VMEM, VMEM, VMEM],
+        in_specs=[HBM, VMEM, VMEM, VMEM, pl.BlockSpec(memory_space=pl.ANY)],
         out_specs=(HBM, VMEM),
         scratch_shapes=[pltpu.SemaphoreType.DMA((2,))],
         input_output_aliases={0: 0, 1: 1},
         compiler_params=params(16),
         cost_estimate=cost(1),
         name="join",
-    )(*in_hbm(after), quant, first, second)
-
-
-def deposit_kernel(base, chunk, edges, quant_ref, depth_ref, *refs):
+    )(*in_hbm(after), quant, first, second, earlier)
+
+
+def deposit_kernel(base, chunk, span, begins, ends, edges, quant_ref, *refs):
+    refs = list(refs)
+    partial_ref = None if begins else refs.pop(0)
+    depth_ref = refs.pop(0) if ends else None
     field_ref = refs[0]
+    begin, end = span
     left_a, left_b, right_a, right_b, now_a, now_b, total = refs[-7:]
     channels = len(QUANT_ROW)
     columns = field_ref.shape[0] // channels
-    depth = depth_ref.shape[1]
-    steps = quant_ref.shape[1] // chunk
+    depth = field_ref.shape[1]
     row16 = lax.broadcasted_iota(jnp.int32, (16, LANES), 0).astype(jnp.float32)
     zero = jnp.zeros((16, LANES), jnp.bfloat16)
     one = jnp.ones((16, LANES), jnp.bfloat16)
-    total[...] = jnp.zeros_like(total)
+    total[...] = jnp.zeros_like(total) if begins else partial_ref[...]
 
     def build(left, right, now, step):
         now[...] = quant_ref[:, pl.ds(pl.multiple_of(step * chunk, chunk), chunk)]
@@ -445,20 +453,23 @@
                 hit = (row16 + 16.0 * k).astype(jnp.bfloat16) == level
                 right[16 * k:16 * k + 16, here] = jnp.where(hit, one, zero)
 
-    build(left_a, right_a, now_a, 0)
+    build(left_a, right_a, now_a, begin)
 
     def two(i, carry):
-        now = 2 * i
+        now = begin + 2 * i
         build(left_b, right_b, now_b, now + 1)
         total[...] += dot(left_a[...], right_a[...], NT)
-        build(left_a, right_a, now_a, jnp.minimum(now + 2, steps - 1))
+        build(left_a, right_a, now_a, jnp.minimum(now + 2, end - 1))
         total[...] += dot(left_b[...], right_b[...], NT)
         return carry
 
-    lax.fori_loop(0, steps // 2, two, 0)
-    if steps % 2:
+    lax.fori_loop(0, (end - begin) // 2, two, 0)
+    if (end - begin) % 2:
         total[...] += dot(left_a[...], right_a[...], NT)
 
+    if not ends:
+        field_ref[...] = total[...]
+        return
     high, low = halves(total[...])
     field_ref[...] = dot(high, depth_ref[0]) + (dot(high, depth_ref[1]) + dot(low, depth_ref[0]))
     if edges:
@@ -473,25 +484,26 @@
             second_ref[to, :] = field_ref[pl.ds(pl.multiple_of(back, 8), edge), :]
 
 
-def deposit(base, columns, chunk, edges, quant, depth_op):
-    depth = depth_op.shape[1]
+def deposit(base, columns, depth, chunk, span, edges, quant, partial=None, depth_op=None):
     channels = len(QUANT_ROW)
+    begins, ends = partial is None, depth_op is not None
     field = jax.ShapeDtypeStruct((channels * columns, depth), jnp.float32)
     edge = jax.ShapeDtypeStruct((channels * columns // 2, depth), jnp.float32)
+    operands = [quant] + ([] if begins else [partial]) + ([depth_op] if ends else [])
     outs = (field, edge, edge) if edges else (field,)
     left = pltpu.VMEM((channels * columns, chunk), jnp.bfloat16)
     right = pltpu.VMEM((depth, chunk), jnp.bfloat16)
     now = pltpu.VMEM((8, chunk), jnp.float32)
     return pl.pallas_call(
-        functools.partial(deposit_kernel, base, chunk, edges),
+        functools.partial(deposit_kernel, base, chunk, span, begins, ends, edges),
         out_shape=outs,
-        in_specs=[VMEM, VMEM],
+        in_specs=[VMEM] * len(operands),
         out_specs=(VMEM,) * len(outs),
         scratch_shapes=[left, left, right, right, now, now, pltpu.VMEM(field.shape, jnp.float32)],
-        compiler_params=params(20),
-        cost_estimate=cost(columns * 0.09),
+        compiler_params=params(28),
+        cost_estimate=cost(columns * 0.006 * (span[1] - span[0])),
         name="deposit",
-    )(quant, depth_op)
+    )(*operands)
 
 
 def mix(operator_ref, start, piece):
@@ -621,15 +633,22 @@
     )(part, first, second, operator, choose, fluid)
 
 
-def swap(first, second, axis, periodic):
+def swap_first(value, axis):
     count = lax.axis_size(axis)
     assert count % 2 == 0
-    pairs = [(source, source ^ 1) for source in range(count)]
-    others = [(source, (source + 1 if source % 2 else source - 1) % count) for source in range(count)]
+    return lax.ppermute(value, axis, [(source, source ^ 1) for source in range(count)])
+
+
+def swap_second(value, axis, periodic):
+    count = lax.axis_size(axis)
+    pairs = [(source, (source + 1 if source % 2 else source - 1) % count) for source in range(count)]
     if not periodic:
-        others = [pair for pair in others if abs(pair[0] - pair[1]) == 1]
-    second = lax.ppermute(second, axis, others)
-    return lax.ppermute(first, axis, pairs), second
+        pairs = [pair for pair in pairs if abs(pair[0] - pair[1]) == 1]
+    return lax.ppermute(value, axis, pairs)
+
+
+def swap(first, second, axis, periodic):
+    return swap_first(first, axis), swap_second(second, axis, periodic)
 
 
 def per_device(grains, send_slots, send_counts, cell_index, fluid, block_slots, block_counts):
@@ -644,15 +663,20 @@
         grains, send_slots[0], send_counts, cell_index.reshape(1, -1), block_slots[0].T, block_counts,
         rows_x, rows_y, depth,
     )
-    arrived = swap(first, second, "stream", True)
+    first = swap_first(first, "stream")
     after, quant = keep(grains, marks, cells, rows_x, rows_y, depth)
-    grains_after, quant = join(after, quant, *arrived)
-
-    chunk = math.gcd(total, 2048)
+    second, quant = lax.optimization_barrier((second, quant))
+    second = swap_second(second, "stream", True)
+
+    chunk = math.gcd(math.gcd(grains.shape[1], 2 * width), 4096)
+    steps = total // chunk
+    kept = grains.shape[1] // chunk
     faces = 2 * REACH * rows_x
-    edge, first, second = deposit(0, faces, chunk, True, quant, depth_op)
+    (partial,) = deposit(0, faces, depth, chunk, (0, kept), False, quant)
+    grains_after, quant = join(after, quant, first, second, partial)
+    edge, first, second = deposit(0, faces, depth, chunk, (kept, steps), True, quant, partial, depth_op)
     first, second = swap(first, second, "span", False)
-    (inner,) = deposit(faces, columns - faces, chunk, False, quant, depth_op)
+    (inner,) = deposit(faces, columns - faces, depth, chunk, (0, steps), False, quant, None, depth_op)
     part = own_part(span_op, edge, inner)
     field, *halos = span_pass(rows_x, rows_y, part, first, second, span_op)
     halos = swap(*halos, "stream", True)

time: 87.9 us -> 86 us (0.978)
  starting transfers between devices: 12.3 us -> 7.98 us
  waiting for transfers between devices: 2.28 us -> 4.61 us
  Pallas kernels: 37.2 us -> 38.6 us
    ppermute x6, starting transfers between devices: 12.3 us -> 7.98 us  [the longest x3 5.69 us: swap_first(): lax.ppermute(value, axis, [(source, source ^ 1) for source in range(count)])]
    ppermute x6, waiting for transfers between devices: 2.28 us -> 4.61 us  [the longest x3 4.26 us: swap_second(): return lax.ppermute(value, axis, pairs)]
    pallas_call x1, Pallas kernels: 5.18 us -> 6.1 us  [leave(): pl.pallas_call(functools.partial(leave_kernel, rows_x, rows_y), out_shape...]
    pallas_call x2 -> x3, Pallas kernels: 24.8 us -> 25.3 us  [deposit(): pl.pallas_call(functools.partial(deposit_kernel, base, chunk, span, begin...]
  transfers between devices with their start and end apart: 6 -> 6, of which waited for: 2 -> 2; matrix products, arithmetic and copies ran while one was open for 0% -> 0% of each run, Pallas kernels for 15% -> 31%
where the time goes in v8:
time: 86 us; the launch traced here: 86.2 us
  Pallas kernels  38.6 us (45%)
  blocking collectives  33.3 us (39%)
  starting transfers between devices  7.98 us (9%)
  waiting for transfers between devices  4.61 us (5%)
  local copies, waits for them, and re-layouts  0.98 us (1%)
    all_to_all x1, blocking collectives, per_device(): lax.all_to_all(outgoing, axes, split_axis=0, concat_axis=0, tiled=True)  33.3 us
    pallas_call x3, Pallas kernels, deposit(): pl.pallas_call(functools.partial(deposit_kernel, base, chunk, span, begin...  25.3 us
    pallas_call x1, Pallas kernels, leave(): pl.pallas_call(functools.partial(leave_kernel, rows_x, rows_y), out_shape...  6.1 us
    ppermute x3, starting transfers between devices, swap_first(): lax.ppermute(value, axis, [(source, source ^ 1) for source in range(count)])  5.69 us
    ppermute x3, waiting for transfers between devices, swap_second(): return lax.ppermute(value, axis, pairs)  4.26 us
    pallas_call x1, Pallas kernels, keep(): pl.pallas_call(functools.partial(keep_kernel, rows_x, rows_y, depth), out...  2.6 us
    ppermute x3, starting transfers between devices, swap_second(): return lax.ppermute(value, axis, pairs)  2.29 us
  transfers between devices with their start and end apart: 6, of which 2 were waited for; matrix products, arithmetic and copies ran while one was open for 0% of the time, Pallas kernels for 31%

profile of v8, /device:TPU:1, one launch (start us, length us, event | category | flops | bytes accessed | tf_op | source)
XLA Modules:
  0.0 86.2 jit_solution(9886735610654007018)
XLA Ops:
  0.6 6.1 %leave.1 = (f32[13,2048]{1,0:T(8,128)S(1)}, f32[13,2048]{1,0:T(8,128)S(1)}, bf16[2,256,256]{2,1,0:T(8,128)(2,1)S(1)}, bf16[2,256,304]{2,1,0:T(8,128)(2,1)S(1)}, ...) custom-call(f32[13,24576]{1,0:T(8,128)} %grains_ref.1, ...), custom_call_target="tpu_custom_call" | custom-call | bytes 24000000 | tf_op jit(solution)/shard_map/leave/pallas_call | solution.py:176
  6.8 2.8 %collective-permute-start = (f32[13,2048]{1,0:T(8,128)S(1)}, f32[13,2048]{1,0:T(8,128)S(1)}, u32[]{:S(2)}, u32[]{:S(2)}) collective-permute-start(f32[13,2048]{1,0:T(8,128)S(1)} %get-tuple-element.31), channel_id=1, source_target_pairs={{0,4},{4,0},{8,12},{12,8},{16,20},{20,16},{24,28},{28,24},{1,5},{5... | collective-permute-start | bytes 319496 | tf_op jit(solution)/shard_map/ppermute | solution.py:639
  9.5 2.6 %keep.1 = (f32[13,28672]{1,0:T(8,128)}, f32[8,28672]{1,0:T(8,128)S(1)}) custom-call(f32[13,24576]{1,0:T(8,128)S(1)} %copy-done, s32[2,2048]{1,0:T(2,128)S(1)} %get-tuple-element.25.marks_ref, s32[1,28672]{1,0:T(1,128)S(1)} %get-tuple-element.26.cells_ref), custom_call_target="tpu_custom_call" | custom-call | bytes 12000000 | tf_op jit(solution)/shard_map/keep/pallas_call | solution.py:361
  12.2 1.4 %collective-permute-start.1 = (f32[13,2048]{1,0:T(8,128)S(1)}, f32[13,2048]{1,0:T(8,128)S(1)}, u32[]{:S(2)}, u32[]{:S(2)}) collective-permute-start(f32[13,2048]{1,0:T(8,128)S(1)} %get-tuple-element.32), channel_id=1, source_target_pairs={{0,28},{4,8},{8,4},{12,16},{16,12},{20,24},{24,20},{28,0},{1,29},{... | collective-permute-start | bytes 319496 | tf_op jit(solution)/shard_map/ppermute | solution.py:647
  13.6 13.8 %deposit.3.earlier_ref.refs_0_ = f32[768,256]{1,0:T(8,128)S(1)} custom-call(f32[8,28672]{1,0:T(8,128)S(1)} %get-tuple-element.30.quant_ref.quant_in), custom_call_target="tpu_custom_call" | custom-call | bytes 20736000 | tf_op jit(solution)/shard_map/deposit/pallas_call | solution.py:497
  27.4 0.0 collective-permute-done.first_ref
  27.4 0.0 collective-permute-done.1.second_ref
  27.4 0.7 join.1
  28.1 3.0 %deposit.4 = (f32[768,256]{1,0:T(8,128)S(1)}, f32[384,256]{1,0:T(8,128)S(1)}, f32[384,256]{1,0:T(8,128)S(1)}) custom-call(f32[8,28672]{1,0:T(8,128)S(1)} %get-tuple-element.36.quant_ref, f32[768,256]{1,0:T(8,128)S(1)} %deposit.3.earlier_ref.refs_0_, bf16[2,256,256]{2,1,0:T(8,128)(2,1)S(1)} %get-tuple-element.37.refs_1_.refs_0_), custom_call_target="tpu_custom_call" | custom-call | bytes 3456000 | tf_op jit(solution)/shard_map/deposit/pallas_call | solution.py:497
  31.2 1.6 %collective-permute-start.2 = (f32[384,256]{1,0:T(8,128)S(1)}, f32[384,256]{1,0:T(8,128)S(1)}, u32[]{:S(2)}, u32[]{:S(2)}) collective-permute-start(f32[384,256]{1,0:T(8,128)S(1)} %get-tuple-element.39), channel_id=1, source_target_pairs={{0,1},{1,0},{2,3},{3,2},{4,5},{5,4},{6,7},{7,6},{8,9},{9,8},{10,11... | collective-permute-start | bytes 1179656 | tf_op jit(solution)/shard_map/ppermute | solution.py:639
  32.8 0.9 collective-permute-start.3
  33.6 8.5 %deposit.5.refs_1_ = f32[256,256]{1,0:T(8,128)S(1)} custom-call(f32[8,28672]{1,0:T(8,128)S(1)} %get-tuple-element.36.quant_ref, bf16[2,256,256]{2,1,0:T(8,128)(2,1)S(1)} %get-tuple-element.37.refs_1_.refs_0_), custom_call_target="tpu_custom_call" | custom-call | bytes 8064000 | tf_op jit(solution)/shard_map/deposit/pallas_call | solution.py:497
  42.1 1.0 %own_part.2.part_ref = f32[1024,256]{1,0:T(8,128)S(1)} custom-call(bf16[2,256,448]{2,1,0:T(8,128)(2,1)S(1)} %get-tuple-element.35.operator_ref, f32[768,256]{1,0:T(8,128)S(1)} %get-tuple-element.38.refs_0_, f32[256,256]{1,0:T(8,128)S(1)} %deposit.5.refs_1_), custom_call_target="tpu_custom_call" | custom-call | bytes 3000000 | tf_op jit(solution)/shard_map/own_part/pallas_call | solution.py:533
  43.1 0.0 collective-permute-done.2.first_in
  43.1 0.0 collective-permute-done.3.second_in
  43.1 0.8 span_pass.1
  43.9 0.0 copy-start.1
  44.0 1.3 %collective-permute-start.4 = (f32[96,256]{1,0:T(8,128)S(1)}, f32[96,256]{1,0:T(8,128)S(1)}, u32[]{:S(2)}, u32[]{:S(2)}) collective-permute-start(f32[96,256]{1,0:T(8,128)S(1)} %get-tuple-element.42), channel_id=1, source_target_pairs={{0,4},{4,0},{8,12},{12,8},{16,20},{20,16},{24,28},{28,24},{1,5},{5... | collective-permute-start | bytes 294920 | tf_op jit(solution)/shard_map/ppermute | solution.py:639
  45.3 0.6 own_part.3.part_ref
  45.9 0.3 collective-permute-done.4.first_in
  46.2 4.3 %collective-permute-done.5.second_in = f32[96,256]{1,0:T(8,128)S(1)} collective-permute-done((f32[96,256]{1,0:T(8,128)S(1)}, f32[96,256]{1,0:T(8,128)S(1)}, u32[]{:S(2)}, u32[]{:S(2)}) %collective-permute-start.5) | collective-permute-done | bytes 98336 | tf_op jit(solution)/shard_map/ppermute | solution.py:647
  50.5 1.5 %stream_pass.1 = (f32[1024,256]{1,0:T(8,128)}, f32[32,8,4,256]{3,2,1,0:T(4,128)S(1)}) custom-call(f32[1024,256]{1,0:T(8,128)S(1)} %own_part.3.part_ref, f32[96,256]{1,0:T(8,128)S(1)} %collective-permute-done.4.first_in, f32[96,256]{1,0:T(8,128)S(1)} %collective-permute-done.5.second_in, bf16[2,256,304]{2,1,0:T(8,128)(2,1)S(1)} %get-tuple-element.34.operator_ref, ...), custom_call_target="tpu_custom_call" | custom-call | bytes 6000000 | tf_op jit(solution)/shard_map/stream_pass/pallas_call | solution.py:621
  51.9 33.3 %all_to_all.5 = f32[32,8,4,256]{3,2,1,0:T(4,128)S(1)} all-to-all(f32[32,8,4,256]{3,2,1,0:T(4,128)S(1)} %get-tuple-element.46), channel_id=1, replica_groups=mesh['stream'=8,'span'=4] {'stream','span'}, dimensions={0} | all-to-all | bytes 2097152 | tf_op jit(solution)/shard_map/all_to_all | solution.py:687
  85.2 1.0 %copy.15 = f32[1,32,8,4,256]{4,3,2,1,0:T(4,128)} copy(f32[1,32,8,4,256]{4,3,2,1,0:T(4,128)S(1)} %bitcast.9) | data formatting | bytes 2097152
  (4 shorter events, 0.0 us)
Async XLA Ops:
  0.6 8.9 %copy-start = (f32[13,24576]{1,0:T(8,128)S(1)}, f32[13,24576]{1,0:T(8,128)}, u32[]{:S(2)}) copy-start(f32[13,24576]{1,0:T(8,128)} %grains_ref.1) | copy-start | bytes 3833860
  6.8 20.6 %collective-permute-start = (f32[13,2048]{1,0:T(8,128)S(1)}, f32[13,2048]{1,0:T(8,128)S(1)}, u32[]{:S(2)}, u32[]{:S(2)}) collective-permute-start(f32[13,2048]{1,0:T(8,128)S(1)} %get-tuple-element.31), channel_id=1, source_target_pairs={{0,4},{4,0},{8,12},{12,8},{16,20},{20,16},{24,28},{28,24},{1,5},{5... | collective-permute-start | bytes 319496 | tf_op jit(solution)/shard_map/ppermute | solution.py:639
  12.2 15.2 %collective-permute-start.1 = (f32[13,2048]{1,0:T(8,128)S(1)}, f32[13,2048]{1,0:T(8,128)S(1)}, u32[]{:S(2)}, u32[]{:S(2)}) collective-permute-start(f32[13,2048]{1,0:T(8,128)S(1)} %get-tuple-element.32), channel_id=1, source_target_pairs={{0,28},{4,8},{8,4},{12,16},{16,12},{20,24},{24,20},{28,0},{1,29},{... | collective-permute-start | bytes 319496 | tf_op jit(solution)/shard_map/ppermute | solution.py:647
  31.2 11.9 %collective-permute-start.2 = (f32[384,256]{1,0:T(8,128)S(1)}, f32[384,256]{1,0:T(8,128)S(1)}, u32[]{:S(2)}, u32[]{:S(2)}) collective-permute-start(f32[384,256]{1,0:T(8,128)S(1)} %get-tuple-element.39), channel_id=1, source_target_pairs={{0,1},{1,0},{2,3},{3,2},{4,5},{5,4},{6,7},{7,6},{8,9},{9,8},{10,11... | collective-permute-start | bytes 1179656 | tf_op jit(solution)/shard_map/ppermute | solution.py:639
  32.8 10.3 %collective-permute-start.3 = (f32[384,256]{1,0:T(8,128)S(1)}, f32[384,256]{1,0:T(8,128)S(1)}, u32[]{:S(2)}, u32[]{:S(2)}) collective-permute-start(f32[384,256]{1,0:T(8,128)S(1)} %get-tuple-element.40), channel_id=1, source_target_pairs={{1,2},{2,1},{5,6},{6,5},{9,10},{10,9},{13,14},{14,13},{17,18},{18,... | collective-permute-start | bytes 1179656 | tf_op jit(solution)/shard_map/ppermute | solution.py:647
  43.9 6.5 %copy-start.1 = (f32[3,32,8,256]{3,2,1,0:T(8,128)S(1)}, f32[3,32,8,256]{3,2,1,0:T(8,128)}, u32[]{:S(2)}) copy-start(f32[3,32,8,256]{3,2,1,0:T(8,128)} %param.11) | copy-start | bytes 2359300
  44.0 2.3 %collective-permute-start.4 = (f32[96,256]{1,0:T(8,128)S(1)}, f32[96,256]{1,0:T(8,128)S(1)}, u32[]{:S(2)}, u32[]{:S(2)}) collective-permute-start(f32[96,256]{1,0:T(8,128)S(1)} %get-tuple-element.42), channel_id=1, source_target_pairs={{0,4},{4,0},{8,12},{12,8},{16,20},{20,16},{24,28},{28,24},{1,5},{5... | collective-permute-start | bytes 294920 | tf_op jit(solution)/shard_map/ppermute | solution.py:639
  45.3 5.2 %collective-permute-start.5 = (f32[96,256]{1,0:T(8,128)S(1)}, f32[96,256]{1,0:T(8,128)S(1)}, u32[]{:S(2)}, u32[]{:S(2)}) collective-permute-start(f32[96,256]{1,0:T(8,128)S(1)} %get-tuple-element.43), channel_id=1, source_target_pairs={{0,28},{4,8},{8,4},{12,16},{16,12},{20,24},{24,20},{28,0},{1,29},{... | collective-permute-start | bytes 294920 | tf_op jit(solution)/shard_map/ppermute | solution.py:647

commit v9 on v8

--- a/solution.py
+++ b/solution.py
@@ -546,7 +546,7 @@
     return jnp.concatenate([jnp.where(odd, first, second), jnp.where(odd, second, first)], axis=0)
 
 
-def span_kernel(rows_x, rows_y, part_ref, first_in, second_in, operator_ref, field_ref, first_ref, second_ref):
+def span_kernel(rows_x, rows_y, part_ref, second_in, first_in, operator_ref, field_ref, first_ref, second_ref):
     channels = len(QUANT_ROW)
     columns = rows_x * rows_y
     halo = first_in.shape[0] // channels
@@ -580,11 +580,11 @@
         compiler_params=params(12),
         cost_estimate=cost(1),
         name="span_pass",
-    )(part, first, second, operator)
+    )(part, second, first, operator)
 
 
 def stream_kernel(
-    rows_q, part_ref, first_in, second_in, operator_ref, choose_ref, fluid_ref, solid_hbm, out_ref, solid_ref, sems
+    rows_q, part_ref, second_in, first_in, operator_ref, choose_ref, fluid_ref, solid_hbm, out_ref, solid_ref, sems
 ):
     channels = len(QUANT_ROW)
     columns = part_ref.shape[0] // channels
@@ -630,7 +630,7 @@
         compiler_params=params(16),
         cost_estimate=cost(2),
         name="stream_pass",
-    )(part, first, second, operator, choose, fluid)
+    )(part, second, first, operator, choose, fluid)
 
 
 def swap_first(value, axis):

time: 86 us -> 85.4 us (level)
  waiting for transfers between devices: 4.61 us -> 0.76 us
  starting transfers between devices: 7.98 us -> 10.8 us
  Pallas kernels: 38.6 us -> 40.8 us
  blocking collectives: 33.3 us -> 31.7 us
    ppermute x3, waiting for transfers between devices: 4.26 us -> 0.75 us  [swap_second(): return lax.ppermute(value, axis, pairs)]
    pallas_call x1, Pallas kernels: 6.1 us -> 8.36 us  [leave(): pl.pallas_call(functools.partial(leave_kernel, rows_x, rows_y), out_shape...]
    all_to_all x1, blocking collectives: 33.3 us -> 31.7 us  [per_device(): lax.all_to_all(outgoing, axes, split_axis=0, concat_axis=0, tiled=True)]
    ppermute x3, starting transfers between devices: 5.69 us -> 7.21 us  [swap_first(): lax.ppermute(value, axis, [(source, source ^ 1) for source in range(count)])]
    ppermute x3, starting transfers between devices: 2.29 us -> 3.58 us  [swap_second(): return lax.ppermute(value, axis, pairs)]
  transfers between devices with their start and end apart: 6 -> 6, of which waited for: 2 -> 1; matrix products, arithmetic and copies ran while one was open for 0% -> 0% of each run, Pallas kernels for 31% -> 31%
where the time goes in v9:
time: 85.4 us; the launch traced here: 85.8 us
  Pallas kernels  40.8 us (48%)
  blocking collectives  31.7 us (37%)
  starting transfers between devices  10.8 us (13%)
  local copies, waits for them, and re-layouts  0.98 us (1%)
    all_to_all x1, blocking collectives, per_device(): lax.all_to_all(outgoing, axes, split_axis=0, concat_axis=0, tiled=True)  31.7 us
    pallas_call x3, Pallas kernels, deposit(): pl.pallas_call(functools.partial(deposit_kernel, base, chunk, span, begin...  25.3 us
    pallas_call x1, Pallas kernels, leave(): pl.pallas_call(functools.partial(leave_kernel, rows_x, rows_y), out_shape...  8.36 us
    ppermute x3, starting transfers between devices, swap_first(): lax.ppermute(value, axis, [(source, source ^ 1) for source in range(count)])  7.21 us
    ppermute x3, starting transfers between devices, swap_second(): return lax.ppermute(value, axis, pairs)  3.58 us
    pallas_call x1, Pallas kernels, keep(): pl.pallas_call(functools.partial(keep_kernel, rows_x, rows_y, depth), out...  2.6 us
  transfers between devices with their start and end apart: 6, of which 1 were waited for; matrix products, arithmetic and copies ran while one was open for 0% of the time, Pallas kernels for 31%

profile of v9, /device:TPU:1, one launch (start us, length us, event | category | flops | bytes accessed | tf_op | source)
XLA Modules:
  0.0 85.8 jit_solution(1823023445279807524)
XLA Ops:
  0.6 8.4 %leave.1 = (f32[13,2048]{1,0:T(8,128)S(1)}, f32[13,2048]{1,0:T(8,128)S(1)}, bf16[2,256,256]{2,1,0:T(8,128)(2,1)S(1)}, bf16[2,256,304]{2,1,0:T(8,128)(2,1)S(1)}, ...) custom-call(f32[13,24576]{1,0:T(8,128)} %grains_ref.1, ...), custom_call_target="tpu_custom_call" | custom-call | bytes 24000000 | tf_op jit(solution)/shard_map/leave/pallas_call | solution.py:176
  9.0 0.1 collective-permute-start
  9.1 2.6 %keep.1 = (f32[13,28672]{1,0:T(8,128)}, f32[8,28672]{1,0:T(8,128)S(1)}) custom-call(f32[13,24576]{1,0:T(8,128)S(1)} %copy-done, s32[2,2048]{1,0:T(2,128)S(1)} %get-tuple-element.25.marks_ref, s32[1,28672]{1,0:T(1,128)S(1)} %get-tuple-element.26.cells_ref), custom_call_target="tpu_custom_call" | custom-call | bytes 12000000 | tf_op jit(solution)/shard_map/keep/pallas_call | solution.py:361
  11.7 2.1 %collective-permute-start.1 = (f32[13,2048]{1,0:T(8,128)S(1)}, f32[13,2048]{1,0:T(8,128)S(1)}, u32[]{:S(2)}, u32[]{:S(2)}) collective-permute-start(f32[13,2048]{1,0:T(8,128)S(1)} %get-tuple-element.32), channel_id=1, source_target_pairs={{0,28},{4,8},{8,4},{12,16},{16,12},{20,24},{24,20},{28,0},{1,29},{... | collective-permute-start | bytes 319496 | tf_op jit(solution)/shard_map/ppermute | solution.py:647
  13.8 13.8 %deposit.3.earlier_ref.refs_0_ = f32[768,256]{1,0:T(8,128)S(1)} custom-call(f32[8,28672]{1,0:T(8,128)S(1)} %get-tuple-element.30.quant_ref.quant_in), custom_call_target="tpu_custom_call" | custom-call | bytes 20736000 | tf_op jit(solution)/shard_map/deposit/pallas_call | solution.py:497
  27.6 0.0 collective-permute-done.first_ref
  27.6 0.0 collective-permute-done.1.second_ref
  27.6 0.7 join.1
  28.3 3.0 %deposit.4 = (f32[768,256]{1,0:T(8,128)S(1)}, f32[384,256]{1,0:T(8,128)S(1)}, f32[384,256]{1,0:T(8,128)S(1)}) custom-call(f32[8,28672]{1,0:T(8,128)S(1)} %get-tuple-element.36.quant_ref, f32[768,256]{1,0:T(8,128)S(1)} %deposit.3.earlier_ref.refs_0_, bf16[2,256,256]{2,1,0:T(8,128)(2,1)S(1)} %get-tuple-element.37.refs_1_.refs_0_), custom_call_target="tpu_custom_call" | custom-call | bytes 3456000 | tf_op jit(solution)/shard_map/deposit/pallas_call | solution.py:497
  31.4 0.9 %collective-permute-start.2 = (f32[384,256]{1,0:T(8,128)S(1)}, f32[384,256]{1,0:T(8,128)S(1)}, u32[]{:S(2)}, u32[]{:S(2)}) collective-permute-start(f32[384,256]{1,0:T(8,128)S(1)} %get-tuple-element.39), channel_id=1, source_target_pairs={{1,2},{2,1},{5,6},{6,5},{9,10},{10,9},{13,14},{14,13},{17,18},{18,... | collective-permute-start | bytes 1179656 | tf_op jit(solution)/shard_map/ppermute | solution.py:647
  32.2 5.0 %collective-permute-start.3 = (f32[384,256]{1,0:T(8,128)S(1)}, f32[384,256]{1,0:T(8,128)S(1)}, u32[]{:S(2)}, u32[]{:S(2)}) collective-permute-start(f32[384,256]{1,0:T(8,128)S(1)} %get-tuple-element.40), channel_id=1, source_target_pairs={{0,1},{1,0},{2,3},{3,2},{4,5},{5,4},{6,7},{7,6},{8,9},{9,8},{10,11... | collective-permute-start | bytes 1179656 | tf_op jit(solution)/shard_map/ppermute | solution.py:639
  37.2 8.5 %deposit.5.refs_1_ = f32[256,256]{1,0:T(8,128)S(1)} custom-call(f32[8,28672]{1,0:T(8,128)S(1)} %get-tuple-element.36.quant_ref, bf16[2,256,256]{2,1,0:T(8,128)(2,1)S(1)} %get-tuple-element.37.refs_1_.refs_0_), custom_call_target="tpu_custom_call" | custom-call | bytes 8064000 | tf_op jit(solution)/shard_map/deposit/pallas_call | solution.py:497
  45.7 1.0 %own_part.2.part_ref = f32[1024,256]{1,0:T(8,128)S(1)} custom-call(bf16[2,256,448]{2,1,0:T(8,128)(2,1)S(1)} %get-tuple-element.35.operator_ref, f32[768,256]{1,0:T(8,128)S(1)} %get-tuple-element.38.refs_0_, f32[256,256]{1,0:T(8,128)S(1)} %deposit.5.refs_1_), custom_call_target="tpu_custom_call" | custom-call | bytes 3000000 | tf_op jit(solution)/shard_map/own_part/pallas_call | solution.py:533
  46.6 0.0 collective-permute-done.2.second_in
  46.7 0.8 span_pass.1
  47.5 0.0 copy-start.1
  47.5 0.6 collective-permute-start.4
  48.2 2.2 %collective-permute-start.5 = (f32[96,256]{1,0:T(8,128)S(1)}, f32[96,256]{1,0:T(8,128)S(1)}, u32[]{:S(2)}, u32[]{:S(2)}) collective-permute-start(f32[96,256]{1,0:T(8,128)S(1)} %get-tuple-element.43), channel_id=1, source_target_pairs={{0,4},{4,0},{8,12},{12,8},{16,20},{20,16},{24,28},{28,24},{1,5},{5... | collective-permute-start | bytes 294920 | tf_op jit(solution)/shard_map/ppermute | solution.py:639
  50.4 0.6 own_part.3.part_ref
  50.9 0.7 collective-permute-done.4.second_in
  51.7 0.0 collective-permute-done.5.first_in
  51.7 1.5 %stream_pass.1 = (f32[1024,256]{1,0:T(8,128)}, f32[32,8,4,256]{3,2,1,0:T(4,128)S(1)}) custom-call(f32[1024,256]{1,0:T(8,128)S(1)} %own_part.3.part_ref, f32[96,256]{1,0:T(8,128)S(1)} %collective-permute-done.4.second_in, f32[96,256]{1,0:T(8,128)S(1)} %collective-permute-done.5.first_in, bf16[2,256,304]{2,1,0:T(8,128)(2,1)S(1)} %get-tuple-element.34.operator_ref, ...), custom_call_target="tpu_custom_call" | custom-call | bytes 6000000 | tf_op jit(solution)/shard_map/stream_pass/pallas_call | solution.py:621
  53.2 31.7 %all_to_all.5 = f32[32,8,4,256]{3,2,1,0:T(4,128)S(1)} all-to-all(f32[32,8,4,256]{3,2,1,0:T(4,128)S(1)} %get-tuple-element.46), channel_id=1, replica_groups=mesh['stream'=8,'span'=4] {'stream','span'}, dimensions={0} | all-to-all | bytes 2097152 | tf_op jit(solution)/shard_map/all_to_all | solution.py:687
  84.9 1.0 %copy.15 = f32[1,32,8,4,256]{4,3,2,1,0:T(4,128)} copy(f32[1,32,8,4,256]{4,3,2,1,0:T(4,128)S(1)} %bitcast.9) | data formatting | bytes 2097152
  (4 shorter events, 0.0 us)
Async XLA Ops:
  0.6 8.5 %copy-start = (f32[13,24576]{1,0:T(8,128)S(1)}, f32[13,24576]{1,0:T(8,128)}, u32[]{:S(2)}) copy-start(f32[13,24576]{1,0:T(8,128)} %grains_ref.1) | copy-start | bytes 3833860
  9.0 18.5 %collective-permute-start = (f32[13,2048]{1,0:T(8,128)S(1)}, f32[13,2048]{1,0:T(8,128)S(1)}, u32[]{:S(2)}, u32[]{:S(2)}) collective-permute-start(f32[13,2048]{1,0:T(8,128)S(1)} %get-tuple-element.31), channel_id=1, source_target_pairs={{0,4},{4,0},{8,12},{12,8},{16,20},{20,16},{24,28},{28,24},{1,5},{5... | collective-permute-start | bytes 319496 | tf_op jit(solution)/shard_map/ppermute | solution.py:639
  11.7 15.9 %collective-permute-start.1 = (f32[13,2048]{1,0:T(8,128)S(1)}, f32[13,2048]{1,0:T(8,128)S(1)}, u32[]{:S(2)}, u32[]{:S(2)}) collective-permute-start(f32[13,2048]{1,0:T(8,128)S(1)} %get-tuple-element.32), channel_id=1, source_target_pairs={{0,28},{4,8},{8,4},{12,16},{16,12},{20,24},{24,20},{28,0},{1,29},{... | collective-permute-start | bytes 319496 | tf_op jit(solution)/shard_map/ppermute | solution.py:647
  31.4 15.3 %collective-permute-start.2 = (f32[384,256]{1,0:T(8,128)S(1)}, f32[384,256]{1,0:T(8,128)S(1)}, u32[]{:S(2)}, u32[]{:S(2)}) collective-permute-start(f32[384,256]{1,0:T(8,128)S(1)} %get-tuple-element.39), channel_id=1, source_target_pairs={{1,2},{2,1},{5,6},{6,5},{9,10},{10,9},{13,14},{14,13},{17,18},{18,... | collective-permute-start | bytes 1179656 | tf_op jit(solution)/shard_map/ppermute | solution.py:647
  32.2 14.4 %collective-permute-start.3 = (f32[384,256]{1,0:T(8,128)S(1)}, f32[384,256]{1,0:T(8,128)S(1)}, u32[]{:S(2)}, u32[]{:S(2)}) collective-permute-start(f32[384,256]{1,0:T(8,128)S(1)} %get-tuple-element.40), channel_id=1, source_target_pairs={{0,1},{1,0},{2,3},{3,2},{4,5},{5,4},{6,7},{7,6},{8,9},{9,8},{10,11... | collective-permute-start | bytes 1179656 | tf_op jit(solution)/shard_map/ppermute | solution.py:639
  47.5 4.2 %copy-start.1 = (f32[3,32,8,256]{3,2,1,0:T(8,128)S(1)}, f32[3,32,8,256]{3,2,1,0:T(8,128)}, u32[]{:S(2)}) copy-start(f32[3,32,8,256]{3,2,1,0:T(8,128)} %param.11) | copy-start | bytes 2359300
  47.5 4.2 %collective-permute-start.4 = (f32[96,256]{1,0:T(8,128)S(1)}, f32[96,256]{1,0:T(8,128)S(1)}, u32[]{:S(2)}, u32[]{:S(2)}) collective-permute-start(f32[96,256]{1,0:T(8,128)S(1)} %get-tuple-element.42), channel_id=1, source_target_pairs={{0,28},{4,8},{8,4},{12,16},{16,12},{20,24},{24,20},{28,0},{1,29},{... | collective-permute-start | bytes 294920 | tf_op jit(solution)/shard_map/ppermute | solution.py:647
  48.2 3.5 %collective-permute-start.5 = (f32[96,256]{1,0:T(8,128)S(1)}, f32[96,256]{1,0:T(8,128)S(1)}, u32[]{:S(2)}, u32[]{:S(2)}) collective-permute-start(f32[96,256]{1,0:T(8,128)S(1)} %get-tuple-element.43), channel_id=1, source_target_pairs={{0,4},{4,0},{8,12},{12,8},{16,20},{20,16},{24,28},{28,24},{1,5},{5... | collective-permute-start | bytes 294920 | tf_op jit(solution)/shard_map/ppermute | solution.py:639
